TPU v7x, 256 devices: a whole 4x4x8 slice. The times are simulated.
256 devices in a mesh: row: 8 (over x, z_hi), col: 32 (over y, z_lo, core).
Axes of the slice: x: 4, y: 4, z: 8 (z_hi: 2, z_lo: 4; z = z_hi * 4 + z_lo), core: 2. Of those that a mesh axis runs over, the one named last changes fastest.
Arguments:
- query_single: bfloat16 [1024, 384], P(('row', 'col')), may hold values from -6 to 6
- query_frames: float32 [12, 1024], P(None, 'row'), may hold values from -30 to 30, as said below
- query_chain: int32 [1024], P('row'), may hold values from 0 to 3, never falling along the last dimension, each value on 1 to 512 neighbouring positions
- key_single: bfloat16 [8192, 384], P('col', 'row'), may hold values from -32 to 32
- key_frames: float32 [12, 8192], P(None, 'col'), may hold values from -30 to 30, as said below
- key_chain: int32 [8192], P('col'), may hold values from 0 to 7, never falling along the last dimension, each value on 1 to 2048 neighbouring positions
- key_mask: int32 [8192], P('col'), may hold values 0 or 1
- pair: bfloat16 [1024, 8192, 128], P('row', 'col'), may hold values from -1000 to 1000
- w_query: bfloat16 [384, 336], replicated, may hold values from -0.3125 to 0.3125
- w_key: bfloat16 [384, 816], replicated, may hold values from -0.3125 to 0.3125
- pair_weight: bfloat16 [128, 12], replicated, may hold values from -1 to 1
- point_raw: float32 [12], replicated, may hold values from -1.5 to 1
- chain_bias: float32 [12], replicated, may hold values from -2 to 2
- out_weight: bfloat16 [2112, 384], replicated, may hold values from -0.125 to 0.125
- out_bias: float32 [384], replicated, may hold values from -2 to 2
Outputs:
- update: bfloat16 [1024, 384], P(('row', 'col'))
Inputs may be any that keep to these rules, and one draw needn't show every extreme that they name: `query_frames`: rows 0 to 8 of each column are a rotation matrix in row-major order, rows 9 to 11 a translation. `key_frames`: rows 0 to 8 of each column are a rotation matrix in row-major order, rows 9 to 11 a translation.
All inputs are finite; a program needn't handle non-finite values. No bound on the sum of `key_mask` on one device may be relied on, other than what follows from the above.
Results may differ from a plain program's by a relative error of at most 0.0095.
Values may be sent and summed in bfloat16 or wider, within the bound.
No kernel may reach another device: no remote copies, remote signals or barrier semaphores. Data moves between devices by JAX's collectives and lax.ppermute only.
A program may use at most 64 MiB of HBM per device.

v0:
```python
import math

import jax
import jax.numpy as jnp
from jax import lax
from jax.sharding import PartitionSpec as P

H = 12
C = 16
PQ = 4
PV = 8
CZ = 128


HIGH = lax.Precision.HIGHEST


def to_global(local, frames):
    count = local.shape[0]
    points = local.reshape(count, -1, 3)
    rotation = frames[:9].T.reshape(count, 3, 3)
    moved = jnp.einsum("nxy,nay->nax", rotation, points, precision=HIGH)
    return (moved + frames[9:].T[:, None, :]).reshape(count, -1)


def logits_of(
    queries,
    query_points,
    query_chain,
    keys,
    key_points,
    key_chain,
    pair_tile,
    pair_weight,
    point_raw,
    chain_bias,
):
    rows = queries.shape[0]
    cols = keys.shape[0]
    dots = jnp.einsum(
        "mhc,nhc->hmn",
        queries.reshape(rows, H, C),
        keys.reshape(cols, H, C),
        preferred_element_type=jnp.float32,
    )
    qpts = query_points.reshape(rows, H, 3 * PQ)
    kpts = key_points.reshape(cols, H, 3 * PQ)
    cross = jnp.einsum("mhe,nhe->hmn", qpts, kpts, precision=HIGH)
    dist = (
        jnp.sum(qpts * qpts, 2).T[:, :, None] + jnp.sum(kpts * kpts, 2).T[:, None, :] - 2.0 * cross
    )
    bias = jnp.einsum("mnc,ch->hmn", pair_tile, pair_weight, preferred_element_type=jnp.float32)
    same = (query_chain[:, None] == key_chain[None, :]).astype(jnp.float32)
    gamma = jax.nn.softplus(point_raw)
    total = (
        dots * (1.0 / math.sqrt(C))
        + bias
        + chain_bias[:, None, None] * same[None]
        - 0.5 * math.sqrt(2.0 / (9.0 * PQ)) * gamma[:, None, None] * dist
    )
    return math.sqrt(1.0 / 3.0) * total


def weigh(logits, peak, keep, values, value_points, pair_tile):
    rows = logits.shape[1]
    cols = logits.shape[2]
    expd = jnp.where(keep[None, None, :], jnp.exp(logits - peak.T[:, :, None]), 0.0)
    total = jnp.sum(expd, 2).T
    weights = expd.astype(jnp.bfloat16)
    mixed = jnp.einsum(
        "hmn,nhc->mhc", weights, values.reshape(cols, H, C), preferred_element_type=jnp.float32
    ).reshape(rows, -1)
    points = jnp.einsum(
        "hmn,nhe->mhe",
        weights,
        value_points.reshape(cols, H, 3 * PV),
        preferred_element_type=jnp.float32,
    ).reshape(rows, -1)
    paired = jnp.einsum(
        "hmn,mnc->mhc", weights, pair_tile, preferred_element_type=jnp.float32
    ).reshape(rows, -1)
    return (total, mixed, points, paired)


def finish(total, mixed, points, paired, frames, out_weight, out_bias):
    rows = total.shape[0]
    scale = 1.0 / total
    mixed = (mixed.reshape(rows, H, C) * scale[:, :, None]).reshape(rows, -1)
    spots = points.reshape(rows, H, 3 * PV) * scale[:, :, None]
    spots = spots.reshape(rows, H * PV, 3) - frames[9:].T[:, None, :]
    rotation = frames[:9].T.reshape(rows, 3, 3)
    local = jnp.einsum("nyx,nay->nax", rotation, spots, precision=HIGH)
    lengths = jnp.sqrt(jnp.sum(local * local, 2) + 1.0)
    paired = (paired.reshape(rows, H, CZ) * scale[:, :, None]).reshape(rows, -1)
    features = jnp.concatenate([mixed, local.reshape(rows, -1), lengths, paired], 1).astype(
        jnp.bfloat16
    )
    return (jnp.dot(features, out_weight, preferred_element_type=jnp.float32) + out_bias).astype(
        jnp.bfloat16
    )


def body(
    query_single,
    query_frames,
    query_chain,
    key_single,
    key_frames,
    key_chain,
    key_mask,
    pair,
    w_query,
    w_key,
    pair_weight,
    point_raw,
    chain_bias,
    out_weight,
    out_bias,
):
    key_proj = jnp.dot(
        lax.all_gather(key_single, "row", axis=1, tiled=True),
        w_key,
        preferred_element_type=jnp.float32,
    )
    keys = key_proj[:, : H * C].astype(jnp.bfloat16)
    values = key_proj[:, H * C : 2 * H * C].astype(jnp.bfloat16)
    key_points = to_global(key_proj[:, 2 * H * C : 2 * H * C + 3 * H * PQ], key_frames)
    value_points = to_global(key_proj[:, 2 * H * C + 3 * H * PQ :], key_frames).astype(jnp.bfloat16)
    block_single = lax.all_gather(query_single, "col", axis=0, tiled=True)
    query_proj = jnp.dot(block_single, w_query, preferred_element_type=jnp.float32)
    queries = query_proj[:, : H * C].astype(jnp.bfloat16)
    query_points = to_global(query_proj[:, H * C :], query_frames)
    keep = key_mask == 1
    logits = logits_of(
        queries,
        query_points,
        query_chain,
        keys,
        key_points,
        key_chain,
        pair,
        pair_weight,
        point_raw,
        chain_bias,
    )
    local_peak = jnp.max(jnp.where(keep[None, None, :], logits, -1e30), 2).T
    share = queries.shape[0] // lax.axis_size("col")
    first_row = lax.axis_index("col") * share
    own_frames = lax.dynamic_slice_in_dim(query_frames, first_row, share, 1)
    peak = lax.pmax(local_peak, "col")
    total, mixed, points, paired = weigh(logits, peak, keep, values, value_points, pair)
    total, mixed, points, paired = (
        lax.psum_scatter(total, "col", scatter_dimension=0, tiled=True),
        lax.psum_scatter(mixed, "col", scatter_dimension=0, tiled=True),
        lax.psum_scatter(points, "col", scatter_dimension=0, tiled=True),
        lax.psum_scatter(paired, "col", scatter_dimension=0, tiled=True),
    )
    return finish(total, mixed, points, paired, own_frames, out_weight, out_bias)


def solution(mesh):
    return jax.shard_map(
        body,
        mesh=mesh,
        in_specs=(
            P(("row", "col"), None),
            P(None, "row"),
            P("row"),
            P("col", "row"),
            P(None, "col"),
            P("col"),
            P("col"),
            P("row", "col", None),
            P(),
            P(),
            P(),
            P(),
            P(),
            P(),
            P(),
        ),
        out_specs=P(("row", "col"), None),
        check_vma=False,
    )
```

profile of v0, /device:TPU:2, one launch (start us, length us, event | category | flops | bytes accessed | tf_op | source)
XLA Modules:
  0.0 488.3 jit_solution(2895496774177744130)
XLA Ops:
  6.5 0.8 slice_bitcast_fusion.3
  7.4 0.7 slice_bitcast_fusion.1
  8.1 0.7 slice_bitcast_fusion.2
  8.8 0.7 slice_bitcast_fusion
  9.5 45.2 %all-gather = bf16[32,4,384]{2,1,0:T(4,128)(2,1)S(1)} all-gather(bf16[1,4,384]{2,1,0:T(4,128)(2,1)} %bitcast.96), channel_id=1, replica_groups=mesh['row'=8,'col'=32] {'col'}, dimensions={0}, use_global_device_ids=true | all-gather | bytes 101376 | tf_op jit(solution)/shard_map/all_gather | solution.py:129
  54.7 1.2 fusion.21
  55.9 0.6 slice.64
  56.6 42.4 %all_gather.6 = bf16[256,384]{0,1:T(8,128)(2,1)S(1)} all-gather(bf16[256,48]{0,1:T(8,128)(2,1)} %param.18), channel_id=1, replica_groups=mesh['row'=8,'col'=32] {'row'}, dimensions={1}, use_global_device_ids=true | all-gather | bytes 221184 | tf_op jit(solution)/shard_map/all_gather | solution.py:121
  99.0 0.4 fusion.20
  99.5 0.1 copy.59
  99.6 0.8 copy.63
  100.4 0.2 copy.57
  100.6 0.2 copy.58
  100.7 1.1 multiply_reduce_fusion.1
  101.8 0.7 copy.60
  102.5 0.1 copy.65
  102.7 1.0 copy.62
  103.7 0.7 fusion.19
  104.4 0.1 reshape.104
  104.4 0.1 reshape.107
  104.6 0.3 copy.69
  104.8 3.7 fusion.5
  108.5 1.2 copy.72
  109.7 0.1 convert_element_type.27
  109.9 0.2 copy.61
  110.2 3.6 multiply_reduce_fusion
  113.8 1.0 copy.64
  114.8 0.8 reduce_sum.52
  115.6 0.2 copy.66
  115.8 0.1 reshape_reshape.7
  115.9 0.1 compare_convert_fusion
  116.0 1.4 fusion.22
  117.5 5.7 %fusion.16 = f32[12,128,256]{2,0,1:T(8,128)S(1)} fusion(bf16[128,256,128]{2,1,0:T(8,128)(2,1)} %param.22, bf16[128,12]{0,1:T(8,128)(2,1)S(1)} %copy-done.6), kind=kOutput, calls=%fused_computation.34 | convolution fusion | flops 100663296 | bytes 9964544 | tf_op jit(solution)/shard_map/mnc,ch->hmn/dot_general | solution.py:52
  123.2 2.0 select_reduce_fusion
  125.2 68.7 %pmax.7 = f32[12,128]{1,0:T(8,128)S(1)} all-reduce(f32[12,128]{1,0:T(8,128)S(1)} %get-tuple-element.20), channel_id=1, replica_groups=mesh['row'=8,'col'=32] {'col'}, use_global_device_ids=true, to_apply=%region_5.6 | all-reduce | flops 1536 | bytes 12288 | tf_op jit(solution)/shard_map/pmax | solution.py:150
  193.9 0.5 fusion.3
  194.5 4.8 fusion.7
  199.3 0.3 fusion.24
  199.6 1.0 fusion.23
  200.6 0.8 copy.73
  201.4 1.3 copy.80
  202.7 0.1 dynamic-slice_bitcast_fusion.1
  202.8 0.1 copy.74
  202.9 0.1 dynamic-slice_bitcast_fusion
  203.0 0.1 copy.84
  203.1 0.1 copy.67
  203.2 0.6 dynamic-slice
  204.4 133.5 %all-reduce.1 = f32[128,12]{1,0:T(8,128)S(1)} all-reduce(f32[128,12]{1,0:T(8,128)S(1)} %copy.67), channel_id=3, replica_groups=mesh['row'=8,'col'=32] {'col'}, use_global_device_ids=true, to_apply=%region_8.9.clone | all-reduce | flops 1536 | bytes 12288
  337.9 0.1 copy.68
  338.0 0.1 mul.109
  338.1 0.1 mul.110
  338.2 0.1 broadcast_bitcast_fusion
  338.3 137.5 %all-reduce.7.cloned.1.call-done = (f32[128,192]{0,1:T(8,128)}, f32[128,288]{1,0:T(8,128)}, f32[128,1536]{0,1:T(8,128)}) async-done(((f32[128,192]{0,1:T(8,128)}, f32[128,288]{1,0:T(8,128)}, f32[128,1536]{0,1:T(8,128)}), (f32[128,192]{0,1:T(8,128)}, f32[128,288]{1,0:T(8,128)}, f32[128,1536]{0,1:T(8,128)})) %all-reduce.7.cloned.1.call-update) | async-done | bytes 1032208
  475.8 1.0 fusion.12
  476.8 0.1 copy.82
  476.9 0.7 constant_dynamic-slice_fusion.1
  477.6 1.4 constant_dynamic-slice_fusion
  479.0 0.3 copy.81
  479.3 0.2 reshape.109
  479.5 0.5 multiply_reduce_fusion.2
  480.1 0.2 copy.78
  480.2 0.2 reshape.111
  480.4 0.1 concatenate.4
  480.6 0.9 fusion.6
  (46 shorter events, 0.4 us)
Async XLA Ops:
  6.5 474.0 %copy-start = (bf16[2112,384]{1,0:T(8,128)(2,1)S(1)}, bf16[2112,384]{1,0:T(8,128)(2,1)}, u32[]{:S(2)}) copy-start(bf16[2112,384]{1,0:T(8,128)(2,1)} %param.28) | copy-start | bytes 4866052
  6.5 92.4 %copy-start.1 = (bf16[384,816]{0,1:T(8,128)(2,1)S(1)}, bf16[384,816]{0,1:T(8,128)(2,1)}, u32[]{:S(2)}) copy-start(bf16[384,816]{0,1:T(8,128)(2,1)} %param.24) | copy-start | bytes 1880068
  6.5 469.3 %all-reduce.7.cloned.1.call-start = ((), (), s32[]{:S(2)}) async-start(), calls=%async_computation | async-start | bytes 2162688
  56.5 42.8 %copy-start.10 = (s32[256]{0:T(256)S(1)}, s32[256]{0:T(256)}, u32[]{:S(2)}) copy-start(s32[256]{0:T(256)} %param.21) | copy-start | bytes 3076
  56.6 42.9 %copy-start.11 = (f32[12]{0:T(128)S(1)}, f32[12]{0:T(128)}, u32[]{:S(2)}) copy-start(f32[12]{0:T(128)} %param.26) | copy-start | bytes 148
  104.8 5.3 %copy-start.2 = (f32[256,3,3]{2,1,0:T(4,128)S(1)}, f32[256,3,3]{2,1,0:T(4,128)}, u32[]{:S(2)}) copy-start(f32[256,3,3]{2,1,0:T(4,128)} %copy.62) | copy-start | bytes 27652
  110.1 5.8 %copy-start.8 = (s32[256]{0:T(256)S(1)}, s32[256]{0:T(256)}, u32[]{:S(2)}) copy-start(s32[256]{0:T(256)} %param.20) | copy-start | bytes 3076
  110.1 5.7 %copy-start.9 = (s32[128]{0:T(128)S(1)}, s32[128]{0:T(128)}, u32[]{:S(2)}) copy-start(s32[128]{0:T(128)} %param.17) | copy-start | bytes 1540
  115.6 1.9 copy-start.6
  117.5 5.7 %copy-start.3 = (bf16[256,192]{0,1:T(8,128)(2,1)S(1)}, bf16[256,192]{0,1:T(8,128)(2,1)}, u32[]{:S(2)}) copy-start(bf16[256,192]{0,1:T(8,128)(2,1)} %get-tuple-element.10) | copy-start | bytes 294916
  117.5 5.7 %copy-start.5 = (bf16[128,192]{0,1:T(8,128)(2,1)S(1)}, bf16[128,192]{0,1:T(8,128)(2,1)}, u32[]{:S(2)}) copy-start(bf16[128,192]{0,1:T(8,128)(2,1)} %slice.64) | copy-start | bytes 147460
  117.5 5.7 %copy-start.12 = (f32[12]{0:T(128)S(1)}, f32[12]{0:T(128)}, u32[]{:S(2)}) copy-start(f32[12]{0:T(128)} %param.27) | copy-start | bytes 148
  200.6 2.1 copy-start.4
  201.4 1.8 copy-start.13
  476.9 3.7 copy-start.7
Sparse Core Ops, SparseCore 0:
  202.8 272.9 all-reduce.6
where the time goes:
time: 490 us; the launch traced here: 488 us
  blocking collectives  290 us (59%)
  waiting for transfers between devices  138 us (28%)
  matrix products  26.7 us (5%)
  local copies, waits for them, and re-layouts  17.4 us (4%)
  between operations  14.5 us (3%)
    unnamed x2, waiting for transfers between devices  138 us
    unnamed x1, blocking collectives  133 us
    pmax x1, blocking collectives, body(): peak = lax.pmax(local_peak, 'col')  68.7 us
    all_gather x1, blocking collectives, body(): block_single = lax.all_gather(query_single, 'col', axis=0, tiled=True)  45.2 us
    all_gather x1, blocking collectives, body(): lax.all_gather(key_single, 'row', axis=1, tiled=True)  42.4 us
  transfers between devices with their start and end apart: 1, of which 1 were waited for; matrix products, arithmetic and copies ran while one was open for 0% of the time, Pallas kernels for 0%

commit v1 on v0

v1 whole, which is shorter than its diff:
```python
import math

import jax
import jax.numpy as jnp
import numpy as np
from jax import lax
from jax.experimental import pallas as pl
from jax.experimental.pallas import tpu as pltpu
from jax.sharding import PartitionSpec as P

H = 12
C = 16
PQ = 4
PV = 8
CZ = 128
HP = 16
KD = 768
GL = 512
QB = 16
FAR = -1e30
F32 = jnp.float32
BF16 = jnp.bfloat16
NT = (((1,), (1,)), ((), ()))
NN = (((1,), (0,)), ((), ()))


def lane_heads():
    head = np.full((GL,), -1)
    for row in range(3):
        head[128 * row : 128 * row + 96] = np.arange(96) // PV
        head[128 * row + 96 : 128 * row + 128] = (np.arange(32) + 32 * row) // C
    head[384:480] = (np.arange(96) + 96) // C
    plain = head.copy()
    head[480:492] = np.arange(H)
    head[492:504] = np.arange(H)
    return plain, head


def depth_mask():
    column = np.arange(KD)
    head = np.full((KD,), -1)
    head[:192] = column[:192] // C
    head[192:624] = ((column[192:624] - 192) % 48) // PQ
    head[624:720] = (column[624:720] - 624) % HP
    mask = (head[None, :] == np.arange(HP)[:, None]).astype(np.float32)
    mask[:, 744] = 1.0
    mask[H:] = 0.0
    return mask


def split(x):
    hi = x.astype(BF16).astype(F32)
    return hi, x - hi


def split3(x):
    hi, rest = split(x)
    mid, rest = split(rest)
    return hi, mid, rest.astype(BF16).astype(F32)


def column_of(row, rows, per):
    shape = (rows, H)
    index = lax.broadcasted_iota(jnp.int32, shape, 0)
    lane = lax.broadcasted_iota(jnp.int32, shape, 1)
    hit = (index >= lane * per) & (index < lane * per + per)
    return jnp.sum(jnp.where(hit, row, 0.0), 1, keepdims=True)


def rotate(points, frames):
    return [
        frames[3 * x : 3 * x + 1] * points[0]
        + frames[3 * x + 1 : 3 * x + 2] * points[1]
        + frames[3 * x + 2 : 3 * x + 3] * points[2]
        + frames[9 + x : 10 + x]
        for x in range(3)
    ]


def take(ref, start, count, stride):
    return jnp.concatenate(
        [ref.at[tile][pl.ds(start, count, stride=stride), :] for tile in range(ref.shape[0])], 1
    )


def put(ref, start, value):
    for tile in range(ref.shape[0]):
        ref[tile, start : start + value.shape[0], :] = value[:, 128 * tile : 128 * tile + 128]


def prepare(
    ks_ref, wk_ref, kf_ref, kc_ref, km_ref, qs_ref, wq_ref, qf_ref, qc_ref, pw_ref, raw_ref, cb_ref,
    dm_ref, kp_s, kpt_s, qp_s, qpt_s, nk_s, nq_s, pw_s, kt_s, vt_s, qft_s, qf_s, m_s, w_s,
):
    raw = raw_ref[...]
    soft = jnp.maximum(raw, 0.0) + jnp.log1p(jnp.exp(-jnp.abs(raw)))
    gamma = (0.5 * math.sqrt(2.0 / (9.0 * PQ))) * soft
    gamma16 = column_of(gamma, HP, 1)
    gamma48 = column_of(gamma, H * PQ, PQ)

    kp_s[:, :816] = jnp.dot(ks_ref[...].T, wk_ref[...], preferred_element_type=F32)
    put(kpt_s, 0, kp_s[...].T)
    frames = kf_ref[...]
    kt_s[0:192] = take(kpt_s, 0, 192, 1).astype(BF16)
    points = rotate([take(kpt_s, 384 + x, 48, 3) for x in range(3)], frames)
    for x in range(3):
        hi, lo = split(points[x])
        kt_s[192 + 48 * x : 240 + 48 * x] = hi.astype(BF16)
        kt_s[336 + 48 * x : 384 + 48 * x] = lo.astype(BF16)
        kt_s[480 + 48 * x : 528 + 48 * x] = hi.astype(BF16)
    put(kpt_s, 832, points[0] * points[0] + points[1] * points[1] + points[2] * points[2])
    nk_s[...] = jnp.zeros_like(nk_s)
    nk_s[0:H] = sum(take(kpt_s, 832 + p, H, PQ) for p in range(PQ))
    for t, part in enumerate(split3(-gamma16 * nk_s[...])):
        kt_s[624 + HP * t : 640 + HP * t] = part.astype(BF16)
    kt_s[672:720] = jnp.ones((48, kt_s.shape[1]), BF16)
    shape = (48, kt_s.shape[1])
    index = lax.broadcasted_iota(jnp.int32, shape, 0)
    same = (jnp.bitwise_and(index, 7) == kc_ref[...]) & (index < 24)
    away = jnp.where((index == 24) & (km_ref[...] != 1), FAR, 0.0)
    kt_s[720:768] = (same.astype(F32) + away).astype(BF16)
    points = rotate([take(kpt_s, 528 + x, 96, 3) for x in range(3)], frames)
    for x in range(3):
        vt_s[128 * x : 128 * x + 96] = points[x].astype(BF16)
        vt_s[128 * x + 96 : 128 * x + 128] = take(kpt_s, 192 + 32 * x, 32, 1).astype(BF16)
    vt_s[384:480] = take(kpt_s, 288, 96, 1).astype(BF16)
    vt_s[480:512] = jnp.zeros((32, vt_s.shape[1]), BF16)

    qp_s[:, :336] = jnp.dot(qs_ref[...], wq_ref[...], preferred_element_type=F32)
    put(qpt_s, 0, qp_s[...].T)
    frames = qf_ref[...]
    qft_s[0:192] = take(qpt_s, 0, 192, 1).astype(BF16).astype(F32) * (1.0 / math.sqrt(C))
    points = rotate([take(qpt_s, 192 + x, 48, 3) for x in range(3)], frames)
    for x in range(3):
        hi, lo = split(2.0 * gamma48 * points[x])
        qft_s[192 + 48 * x : 240 + 48 * x] = hi
        qft_s[336 + 48 * x : 384 + 48 * x] = hi
        qft_s[480 + 48 * x : 528 + 48 * x] = lo
    put(qpt_s, 336, points[0] * points[0] + points[1] * points[1] + points[2] * points[2])
    nq_s[...] = jnp.zeros_like(nq_s)
    nq_s[0:H] = sum(take(qpt_s, 336 + p, H, PQ) for p in range(PQ))
    qft_s[624:672] = jnp.ones((48, qft_s.shape[1]), F32)
    for t, part in enumerate(split3(-gamma16 * nq_s[...])):
        qft_s[672 + HP * t : 688 + HP * t] = part
    shape = (48, qft_s.shape[1])
    index = lax.broadcasted_iota(jnp.int32, shape, 0)
    same = (jnp.bitwise_and(index, 7) == qc_ref[...]) & (index < 24)
    qft_s[720:768] = (same | (index == 24)).astype(F32)
    qf_s[...] = qft_s[...].T

    m_s[...] = dm_ref[...]
    lane = lax.broadcasted_iota(jnp.int32, (HP, 128), 1)
    tail = dm_ref[:, 640:768]
    for t, part in enumerate(split3(column_of(cb_ref[...], HP, 1))):
        tail = jnp.where((lane >= 80 + 8 * t) & (lane < 88 + 8 * t), part, tail)
    m_s[:, 640:768] = tail
    pw_s[...] = jnp.zeros_like(pw_s)
    pw_s[:, :H] = pw_ref[...].astype(F32)
    w_s[...] = pw_s[...].T[:HP].astype(BF16)


def attend_kernel(
    ks_ref, wk_ref, kf_ref, kc_ref, km_ref, qs_ref, wq_ref, qf_ref, qc_ref, pw_ref, raw_ref, cb_ref,
    dm_ref, lm_ref, pair_ref, out_ref,
    kp_s, kpt_s, qp_s, qpt_s, nk_s, nq_s, pw_s, kt_s, vt_s, qft_s, qf_s, m_s, w_s, o_s,
):
    step = pl.program_id(0)

    @pl.when(step == 0)
    def _():
        prepare(
            ks_ref, wk_ref, kf_ref, kc_ref, km_ref, qs_ref, wq_ref, qf_ref, qc_ref, pw_ref, raw_ref,
            cb_ref, dm_ref, kp_s, kpt_s, qp_s, qpt_s, nk_s, nq_s, pw_s, kt_s, vt_s, qft_s, qf_s,
            m_s, w_s,
        )

    rows = QB * HP
    first = pl.multiple_of(step * QB, QB)
    mine = qf_s[pl.ds(first, QB), :]
    spread = (mine[:, None, :] * m_s[...][None]).reshape(rows, KD).astype(BF16)
    logits = jnp.dot(spread, kt_s[...], preferred_element_type=F32)
    weight = w_s[...]
    bias = jnp.concatenate(
        [lax.dot_general(weight, pair_ref[i], NT, preferred_element_type=F32) for i in range(QB)], 0
    )
    logits = math.sqrt(1.0 / 3.0) * (logits + bias)
    peak = jnp.maximum(jnp.max(logits, 1, keepdims=True), 0.1 * FAR)
    expd = jnp.exp(logits - peak)
    total = jnp.maximum(jnp.sum(expd, 1, keepdims=True), 1e-30)
    weights = expd.astype(BF16)
    scale = 1.0 / total
    level = peak + jnp.log(total)
    hi, lo = split(level)
    paired = jnp.concatenate(
        [
            jnp.dot(weights[HP * i : HP * i + HP], pair_ref[i], preferred_element_type=F32)
            for i in range(QB)
        ],
        0,
    )
    o_s[...] = paired * scale
    spots = lax.dot_general(weights, vt_s[...], NT, preferred_element_type=F32) * scale
    lane = lax.broadcasted_iota(jnp.int32, (rows, 128), 1)
    for row in range(4):
        part = spots[:, 128 * row : 128 * row + 128]
        if row == 3:
            part = jnp.where(lane < 96, part, jnp.where(lane < 108, hi, lo))
        part = part.reshape(QB, HP, 128) * lm_ref[:, 128 * row : 128 * row + 128][None]
        o_s[pl.ds(H + row, QB, stride=HP), :] = jnp.sum(part, 1)
    out_ref[...] = o_s[...].astype(BF16)


def whole(shape):
    return pl.BlockSpec(shape, lambda i: (0,) * len(shape))


def attend(ks, wk, kf, kc, km, qs, wq, qf, qc, pw, raw, cb, pair):
    queries, keys = pair.shape[:2]
    operands = [
        ks, wk, kf, kc.reshape(1, -1), km.reshape(1, -1), qs, wq, qf, qc.reshape(1, -1), pw,
        raw.reshape(1, -1), cb.reshape(1, -1), jnp.asarray(depth_mask()),
        jnp.asarray((lane_heads()[1][None, :] == np.arange(HP)[:, None]).astype(np.float32)),
    ]
    return pl.pallas_call(
        attend_kernel,
        grid=(queries // QB,),
        out_shape=jax.ShapeDtypeStruct((queries * HP, CZ), BF16),
        in_specs=[whole(x.shape) for x in operands]
        + [pl.BlockSpec((QB, keys, CZ), lambda i: (i, 0, 0))],
        out_specs=pl.BlockSpec((QB * HP, CZ), lambda i: (i, 0)),
        scratch_shapes=[
            pltpu.VMEM((keys, 896), F32),
            pltpu.VMEM((keys // 128, 896, 128), F32),
            pltpu.VMEM((queries, 384), F32),
            pltpu.VMEM((queries // 128, 384, 128), F32),
            pltpu.VMEM((HP, keys), F32),
            pltpu.VMEM((HP, queries), F32),
            pltpu.VMEM((CZ, 128), F32),
            pltpu.VMEM((KD, keys), BF16),
            pltpu.VMEM((GL, keys), BF16),
            pltpu.VMEM((KD, queries), F32),
            pltpu.VMEM((queries, KD), F32),
            pltpu.VMEM((HP, KD), F32),
            pltpu.VMEM((HP, CZ), BF16),
            pltpu.VMEM((QB * HP, CZ), F32),
        ],
        compiler_params=pltpu.CompilerParams(vmem_limit_bytes=32 * 2**20),
    )(*operands, pair)


def finish_kernel(x_ref, qf_ref, em_ref, ow_ref, ob_ref, out_ref, x_s, p_s, g_s, w_s, f_s):
    share = out_ref.shape[0]
    sources = x_ref.shape[0]
    first = lax.axis_index("col") * share
    lane = lax.broadcasted_iota(jnp.int32, (sources, 128), 1)
    stat = (lane >= 96) & (lane < 108)
    for q in range(share):
        block = x_ref[:, HP * q : HP * q + HP, :].reshape(sources * HP, 128)
        x_s[...] = block.astype(F32)
        rows = [x_s[pl.ds(H + r, sources, stride=HP), :] for r in range(4)]
        level = jnp.where(stat, rows[3] + pltpu.roll(rows[3], 128 - H, 1), 0.0)
        part = jnp.exp(level - jnp.max(level, 0, keepdims=True))
        part = jnp.where(stat, part / jnp.sum(part, 0, keepdims=True), 0.0)
        hi, lo = split(part)
        spread = jnp.dot(hi.astype(BF16), em_ref[...], preferred_element_type=F32) + jnp.dot(
            lo.astype(BF16), em_ref[...], preferred_element_type=F32
        )
        for r in range(4):
            g_s[pl.ds(8 * r + q, 1), :] = jnp.sum(
                spread[:, 128 * r : 128 * r + 128] * rows[r], 0, keepdims=True
            )
        w_s[...] = jnp.zeros_like(w_s)
        w_s[0:sources] = part
        turned = w_s[...].T[96:112]
        source = lax.broadcasted_iota(jnp.int32, (128, sources * HP), 0)
        column = lax.broadcasted_iota(jnp.int32, (128, sources * HP), 1)
        repeat = (lax.shift_right_logical(column, 4) == source).astype(BF16)
        own = lax.broadcasted_iota(jnp.int32, (HP, sources * HP), 0) == jnp.bitwise_and(
            lax.broadcasted_iota(jnp.int32, (HP, sources * HP), 1), HP - 1
        )
        paired = jnp.zeros((HP, 128), F32)
        for piece in split(turned):
            wide = jnp.dot(piece.astype(BF16), repeat, preferred_element_type=F32)
            wide = jnp.where(own, wide, 0.0).astype(BF16)
            paired += jnp.dot(wide, block, preferred_element_type=F32)
        p_s[HP * q : HP * q + HP] = paired

    slot = lax.broadcasted_iota(jnp.int32, (share, 128), 1) == first + lax.broadcasted_iota(
        jnp.int32, (share, 128), 0
    )
    frame = [
        jnp.sum(jnp.where(slot, qf_ref[j : j + 1, :], 0.0), 1, keepdims=True) for j in range(12)
    ]
    g = [g_s[8 * r : 8 * r + share, :] for r in range(4)]
    moved = [g[x] - frame[9 + x] for x in range(3)]
    local = [
        frame[x] * moved[0] + frame[3 + x] * moved[1] + frame[6 + x] * moved[2] for x in range(3)
    ]
    lengths = jnp.sqrt(local[0] * local[0] + local[1] * local[1] + local[2] * local[2] + 1.0)
    spot = lax.broadcasted_iota(jnp.int32, (128, 384), 0)
    column = lax.broadcasted_iota(jnp.int32, (128, 384), 1)
    woven = sum(
        jnp.dot(
            local[x].astype(BF16),
            ((column == 3 * spot + x) & (spot < 96)).astype(BF16),
            preferred_element_type=F32,
        )
        for x in range(3)
    )
    f_s[:, 0:384] = woven
    f_s[:, 384:512] = lengths
    for r in range(3):
        f_s[:, 512 + 128 * r : 640 + 128 * r] = pltpu.roll(g[r], 32, 1)
    total = ob_ref[...] + jnp.zeros((share, ob_ref.shape[1]), F32)

    def add(value, low, high):
        return jnp.dot(value.astype(BF16), ow_ref[low:high, :], preferred_element_type=F32)

    total += add(f_s[:, 0:288], 192, 480)
    total += add(f_s[:, 384:480], 480, 576)
    for r in range(3):
        total += add(f_s[:, 512 + 128 * r : 544 + 128 * r], 32 * r, 32 * r + 32)
    total += add(g[3][:, 0:96], 96, 192)
    for h in range(H):
        value = p_s[pl.ds(h, share, stride=HP), :]
        total += add(value, 576 + CZ * h, 576 + CZ * h + CZ)
    out_ref[...] = total.astype(BF16)


def finish(parts, qf, out_weight, out_bias):
    share = parts.shape[1] // HP
    expand = np.zeros((128, GL), np.float32)
    for index, head in enumerate(lane_heads()[0]):
        if head >= 0:
            expand[96 + head, index] = 1.0
    sources = parts.shape[0]
    return pl.pallas_call(
        finish_kernel,
        out_shape=jax.ShapeDtypeStruct((share, out_bias.shape[0]), BF16),
        scratch_shapes=[
            pltpu.VMEM((sources * HP, 128), F32),
            pltpu.VMEM((share * HP, 128), F32),
            pltpu.VMEM((32, 128), F32),
            pltpu.VMEM((128, 128), F32),
            pltpu.VMEM((share, 896), F32),
        ],
        compiler_params=pltpu.CompilerParams(vmem_limit_bytes=24 * 2**20),
    )(parts, qf, jnp.asarray(expand, BF16), out_weight, out_bias.reshape(1, -1))


def body(
    query_single,
    query_frames,
    query_chain,
    key_single,
    key_frames,
    key_chain,
    key_mask,
    pair,
    w_query,
    w_key,
    pair_weight,
    point_raw,
    chain_bias,
    out_weight,
    out_bias,
):
    rows, cols = lax.axis_size("row"), lax.axis_size("col")
    turned = key_single.T
    keys = lax.all_to_all(
        jnp.broadcast_to(turned[None], (rows, *turned.shape)), "row", 0, 0, tiled=True
    ).reshape(-1, turned.shape[1])
    queries = lax.all_to_all(
        jnp.broadcast_to(query_single[None], (cols, *query_single.shape)), "col", 0, 0, tiled=True
    ).reshape(-1, query_single.shape[1])
    sums = attend(
        keys, w_key, key_frames, key_chain, key_mask, queries, w_query, query_frames, query_chain,
        pair_weight, point_raw, chain_bias, pair,
    )
    parts = lax.all_to_all(sums.reshape(cols, -1, CZ), "col", 0, 0, tiled=True)
    return finish(parts, query_frames, out_weight, out_bias)


def solution(mesh):
    return jax.shard_map(
        body,
        mesh=mesh,
        in_specs=(
            P(("row", "col"), None),
            P(None, "row"),
            P("row"),
            P("col", "row"),
            P(None, "col"),
            P("col"),
            P("col"),
            P("row", "col", None),
            P(),
            P(),
            P(),
            P(),
            P(),
            P(),
            P(),
        ),
        out_specs=P(("row", "col"), None),
        check_vma=False,
    )
```

time: 490 us -> 84.9 us (0.17)
  the two profiles are of different devices: /device:TPU:2 before, /device:TPU:1 now
where the time goes in v1:
time: 84.9 us; the launch traced here: 84.1 us
  waiting for transfers between devices  23.2 us (27%)
  blocking collectives  18.3 us (22%)
  local copies, waits for them, and re-layouts  15.4 us (18%)
  starting transfers between devices  14.3 us (17%)
  Pallas kernels  13 us (15%)
    all_to_all x1, blocking collectives, body(): lax.all_to_all(jnp.broadcast_to(query_single[None], (cols, *query_single....  18.3 us
    all_to_all x1, waiting for transfers between devices, body(): parts = lax.all_to_all(sums.reshape(cols, -1, CZ), 'col', 0, 0, tiled=True)  16.8 us
    unnamed x31, local copies, waits for them, and re-layouts  13.1 us
    pallas_call x1, Pallas kernels, attend(): pl.pallas_call(attend_kernel, grid=(queries // QB,), out_shape=jax.ShapeD...  10.9 us
    all_to_all x1, starting transfers between devices, body(): lax.all_to_all(jnp.broadcast_to(turned[None], (rows, *turned.shape)), 'ro...  7.95 us
    all_to_all x1, waiting for transfers between devices, body(): lax.all_to_all(jnp.broadcast_to(turned[None], (rows, *turned.shape)), 'ro...  6.39 us
    all_to_all x1, starting transfers between devices, body(): parts = lax.all_to_all(sums.reshape(cols, -1, CZ), 'col', 0, 0, tiled=True)  6.31 us
    pallas_call x1, Pallas kernels, finish(): pl.pallas_call(finish_kernel, out_shape=jax.ShapeDtypeStruct((share, out_...  2.06 us
  transfers between devices with their start and end apart: 2, of which 2 were waited for; matrix products, arithmetic and copies ran while one was open for 4% of the time, Pallas kernels for 0%

profile of v1, /device:TPU:1, one launch (start us, length us, event | category | flops | bytes accessed | tf_op | source)
XLA Modules:
  0.0 84.1 jit_solution(15652145210665398703)
XLA Ops:
  0.0 0.0 copy-start.2
  0.0 0.0 copy-start.6
  0.0 0.0 copy-start.13
  0.0 0.0 copy-start.1
  0.0 0.8 broadcast_in_dim.5
  0.9 18.3 %all_to_all.15 = bf16[32,4,384]{2,1,0:T(4,128)(2,1)S(1)} all-to-all(bf16[32,4,384]{2,1,0:T(4,128)(2,1)S(1)} %broadcast_in_dim.5), channel_id=1, replica_groups=mesh['row'=8,'col'=32] {'col'}, dimensions={0} | all-to-all | bytes 196608 | tf_op jit(solution)/shard_map/all_to_all | solution.py:373
  19.1 1.4 %broadcast_in_dim.4 = bf16[8,48,256]{2,1,0:T(8,128)(2,1)} broadcast(bf16[48,256]{1,0:T(8,128)(2,1)} %bitcast.14), dimensions={1,2} | broadcast | bytes 221184 | tf_op jit(solution)/shard_map/broadcast_in_dim | solution.py:371
  20.5 7.9 %all-to-all-start = ((bf16[8,48,256]{2,1,0:T(8,128)(2,1)}), bf16[8,48,256]{2,1,0:T(8,128)(2,1)S(1)}, u32[]{:S(2)}, u32[]{:S(2)}) async-start(bf16[8,48,256]{2,1,0:T(8,128)(2,1)} %broadcast_in_dim.4), calls=%async_computation | async-start | bytes 393216 | tf_op jit(solution)/shard_map/all_to_all | solution.py:370
  28.5 1.4 %copy.19.wk_ref = bf16[384,816]{1,0:T(8,128)(2,1)S(1)} copy(bf16[384,816]{0,1:T(8,128)(2,1)} %param.27) | data formatting | bytes 1253376 | tf_op args[9]
  29.9 1.2 %copy.20.wq_ref = bf16[384,336]{1,0:T(8,128)(2,1)S(1)} copy(bf16[384,336]{0,1:T(8,128)(2,1)} %param.26) | data formatting | bytes 516096 | tf_op args[8]
  31.1 0.8 copy.21.pw_ref
  31.9 6.4 %all-to-all-done = bf16[8,48,256]{2,1,0:T(8,128)(2,1)S(1)} async-done(((bf16[8,48,256]{2,1,0:T(8,128)(2,1)}), bf16[8,48,256]{2,1,0:T(8,128)(2,1)S(1)}, u32[]{:S(2)}, u32[]{:S(2)}) %all-to-all-start) | async-done | bytes 196640 | tf_op jit(solution)/shard_map/all_to_all | solution.py:370
  38.3 0.0 copy-start
  38.3 3.4 %copy-done = bf16[128,256,128]{2,1,0:T(8,128)(2,1)S(1)} copy-done((bf16[128,256,128]{2,1,0:T(8,128)(2,1)S(1)}, bf16[128,256,128]{2,1,0:T(8,128)(2,1)}, u32[]{:S(2)}) %copy-start) | copy-done | bytes 8388632
  41.7 0.0 copy-start.3
  41.7 0.8 copy-done.3
  42.5 0.0 copy-start.4
  42.5 0.8 copy-done.4
  43.3 0.0 copy-start.5
  43.3 0.7 copy-done.5
  44.0 0.0 copy-start.7
  44.0 0.7 copy-done.7
  44.7 0.0 copy-start.8
  44.7 0.7 copy-done.8
  45.4 0.0 copy-start.9
  45.4 0.7 copy-done.9
  46.0 0.0 copy-start.10
  46.0 0.7 copy-done.10
  46.7 0.0 copy-start.11
  46.7 0.7 copy-done.11
  47.3 0.0 copy-start.12
  47.3 0.7 copy-done.12
  48.0 10.9 %shard_map.172 = bf16[2048,128]{1,0:T(8,128)(2,1)} custom-call(bf16[384,256]{1,0:T(8,128)(2,1)S(1)} %bitcast.8, bf16[384,816]{1,0:T(8,128)(2,1)S(1)} %copy.19.wk_ref, f32[12,256]{1,0:T(8,128)S(1)} %copy-done.7, s32[1,256]{1,0:T(1,128)S(1)} %bitcast.9, s32[1,256]{1,0:T(1,128)S(1)} %bitcast.10, bf16[128,384]{1,0:T(8,128)(2,1)S(1)} %reshape.32.qs_ref, ...), custom_call_target="tpu_custom_call" | custom-call | tf_op jit(solution)/shard_map/pallas_call | solution.py:224
  58.9 6.3 %all-to-all-start.2 = ((bf16[32,64,128]{2,1,0:T(8,128)(2,1)}), bf16[32,64,128]{2,1,0:T(8,128)(2,1)S(1)}, u32[]{:S(2)}, u32[]{:S(2)}) async-start(bf16[32,64,128]{2,1,0:T(8,128)(2,1)} %bitcast.7), calls=%async_computation.2 | async-start | bytes 1048576 | tf_op jit(solution)/shard_map/all_to_all | solution.py:380
  65.2 0.0 copy-done.13
  65.2 16.8 %all-to-all-done.2.x_ref = bf16[32,64,128]{2,1,0:T(8,128)(2,1)S(1)} async-done(((bf16[32,64,128]{2,1,0:T(8,128)(2,1)}), bf16[32,64,128]{2,1,0:T(8,128)(2,1)S(1)}, u32[]{:S(2)}, u32[]{:S(2)}) %all-to-all-start.2) | async-done | bytes 524320 | tf_op jit(solution)/shard_map/all_to_all | solution.py:380
  82.0 0.0 copy-done.2
  82.0 0.0 copy-done.6
  82.0 0.0 copy-done.1
  82.0 2.1 %shard_map.173 = bf16[4,384]{1,0:T(4,128)(2,1)} custom-call(bf16[32,64,128]{2,1,0:T(8,128)(2,1)S(1)} %all-to-all-done.2.x_ref, f32[12,128]{1,0:T(8,128)S(1)} %copy-done.6, bf16[128,512]{1,0:T(8,128)(2,1)S(1)} %copy-done.2, bf16[2112,384]{1,0:T(8,128)(2,1)S(1)} %copy-done.1, f32[1,384]{1,0:T(1,128)S(1)} %reshape.37.ob_ref), custom_call_target="tpu_custom_call" | custom-call | tf_op jit(solution)/shard_map/pallas_call | solution.py:337
  (2 shorter events, 0.0 us)
Async XLA Ops:
  0.0 82.0 %copy-start.2 = (bf16[128,512]{1,0:T(8,128)(2,1)S(1)}, bf16[128,512]{1,0:T(8,128)(2,1)}, u32[]{:S(2)}) copy-start(bf16[128,512]{1,0:T(8,128)(2,1)} %constant.8.clone.em_ref) | copy-start | bytes 393220
  0.0 82.0 %copy-start.6 = (f32[12,128]{1,0:T(8,128)S(1)}, f32[12,128]{1,0:T(8,128)}, u32[]{:S(2)}) copy-start(f32[12,128]{1,0:T(8,128)} %qf_ref.3) | copy-start | bytes 18436
  0.0 65.2 %copy-start.13 = (f32[384]{0:T(512)S(1)}, f32[384]{0:T(512)}, u32[]{:S(2)}) copy-start(f32[384]{0:T(512)} %param.32) | copy-start | bytes 4612
  0.0 82.0 %copy-start.1 = (bf16[2112,384]{1,0:T(8,128)(2,1)S(1)}, bf16[2112,384]{1,0:T(8,128)(2,1)}, u32[]{:S(2)}) copy-start(bf16[2112,384]{1,0:T(8,128)(2,1)} %ow_ref.1) | copy-start | bytes 4866052
  20.5 17.8 %all-to-all-start = ((bf16[8,48,256]{2,1,0:T(8,128)(2,1)}), bf16[8,48,256]{2,1,0:T(8,128)(2,1)S(1)}, u32[]{:S(2)}, u32[]{:S(2)}) async-start(bf16[8,48,256]{2,1,0:T(8,128)(2,1)} %broadcast_in_dim.4), calls=%async_computation | async-start | bytes 393216 | tf_op jit(solution)/shard_map/all_to_all | solution.py:370
  38.3 3.4 %copy-start = (bf16[128,256,128]{2,1,0:T(8,128)(2,1)S(1)}, bf16[128,256,128]{2,1,0:T(8,128)(2,1)}, u32[]{:S(2)}) copy-start(bf16[128,256,128]{2,1,0:T(8,128)(2,1)} %pair_ref.1) | copy-start | bytes 25165828
  41.7 0.8 copy-start.3
  42.5 0.8 copy-start.4
  43.3 0.7 copy-start.5
  44.0 0.7 copy-start.7
  44.7 0.7 copy-start.8
  45.4 0.7 copy-start.9
  46.0 0.7 copy-start.10
  46.7 0.7 copy-start.11
  47.3 0.7 copy-start.12
  58.9 23.1 %all-to-all-start.2 = ((bf16[32,64,128]{2,1,0:T(8,128)(2,1)}), bf16[32,64,128]{2,1,0:T(8,128)(2,1)S(1)}, u32[]{:S(2)}, u32[]{:S(2)}) async-start(bf16[32,64,128]{2,1,0:T(8,128)(2,1)} %bitcast.7), calls=%async_computation.2 | async-start | bytes 1048576 | tf_op jit(solution)/shard_map/all_to_all | solution.py:380

commit v2 on v1

--- a/solution.py
+++ b/solution.py
@@ -1,3 +1,4 @@
+import functools
 import math
 
 import jax
@@ -88,46 +89,92 @@
         ref[tile, start : start + value.shape[0], :] = value[:, 128 * tile : 128 * tile + 128]
 
 
-def prepare(
-    ks_ref, wk_ref, kf_ref, kc_ref, km_ref, qs_ref, wq_ref, qf_ref, qc_ref, pw_ref, raw_ref, cb_ref,
-    dm_ref, kp_s, kpt_s, qp_s, qpt_s, nk_s, nq_s, pw_s, kt_s, vt_s, qft_s, qf_s, m_s, w_s,
+def gamma_of(raw):
+    soft = jnp.maximum(raw, 0.0) + jnp.log1p(jnp.exp(-jnp.abs(raw)))
+    return (0.5 * math.sqrt(2.0 / (9.0 * PQ))) * soft
+
+
+def spread_kernel(q_ref, k_ref, q_out, k_out):
+    q_out[...] = jnp.broadcast_to(q_ref[...][None], q_out.shape)
+    k_out[...] = jnp.broadcast_to(k_ref[...][None], k_out.shape)
+
+
+def shadow_kernel(
+    qs_ref, wq_hbm, qf_hbm, qc_hbm, raw_hbm, cb_hbm, dm_hbm, kf_hbm, kc_hbm, km_hbm, pw_hbm, wk_hbm,
+    pair_ref, feat_ref, mask_ref, wk_ref, bias_ref,
+    wq_v, qf_v, qc_v, raw_v, cb_v, dm_v, kf_v, kc_v, km_v, pw_v,
+    qpt_s, nq_s, qft_s, pw_s, pair_v, sem, pair_sem,
 ):
-    raw = raw_ref[...]
-    soft = jnp.maximum(raw, 0.0) + jnp.log1p(jnp.exp(-jnp.abs(raw)))
-    gamma = (0.5 * math.sqrt(2.0 / (9.0 * PQ))) * soft
-    gamma16 = column_of(gamma, HP, 1)
-    gamma48 = column_of(gamma, H * PQ, PQ)
-
-    kp_s[:, :816] = jnp.dot(ks_ref[...].T, wk_ref[...], preferred_element_type=F32)
-    put(kpt_s, 0, kp_s[...].T)
-    frames = kf_ref[...]
-    kt_s[0:192] = take(kpt_s, 0, 192, 1).astype(BF16)
+    moves = [
+        (pw_hbm, pw_v), (wq_hbm, wq_v), (qf_hbm, qf_v), (qc_hbm, qc_v), (raw_hbm, raw_v),
+        (cb_hbm, cb_v), (dm_hbm, dm_v), (kf_hbm, kf_v), (kc_hbm, kc_v), (km_hbm, km_v),
+        (wk_hbm, wk_ref),
+    ]
+    small = [pltpu.make_async_copy(*move, sem.at[i]) for i, move in enumerate(moves)]
+    copies = [
+        pltpu.make_async_copy(
+            pair_ref.at[pl.ds(QB * i, QB)], pair_v.at[pl.ds(QB * i, QB)], pair_sem.at[i]
+        )
+        for i in range(pair_ref.shape[0] // QB)
+    ]
+    for copy in small[:1] + copies[:4] + small[1:] + copies[4:]:
+        copy.start()
+    small[0].wait()
+    pw_s[...] = jnp.zeros_like(pw_s)
+    pw_s[0:H] = pw_v[...].astype(F32)
+    weight = pw_s[...].astype(BF16)
+    for i, copy in enumerate(copies):
+        if i == 4:
+            for other in small[1:]:
+                other.wait()
+            prepare_queries(
+                qs_ref, wq_v, qf_v, qc_v, raw_v, cb_v, dm_v, feat_ref, mask_ref, qpt_s, nq_s, qft_s
+            )
+            mask_ref[0:H, KD + GL : KD + GL + 256] = kf_v[...]
+            mask_ref[H : H + 1, KD + GL : KD + GL + 256] = kc_v[...].astype(F32)
+            mask_ref[H + 1 : H + 2, KD + GL : KD + GL + 256] = km_v[...].astype(F32)
+        copy.wait()
+        for q in range(QB * i, QB * i + QB):
+            bias_ref[HP * q : HP * q + HP] = lax.dot_general(
+                weight, pair_v[q], NT, preferred_element_type=F32
+            )
+
+
+def prepare_keys(info, gamma16, kt_ref, vt_ref, kpt_s, nk_s):
+    frames, chain, kept = info[0:H], info[H : H + 1], info[H + 1 : H + 2]
+    kt_ref[0:192] = take(kpt_s, 0, 192, 1).astype(BF16)
     points = rotate([take(kpt_s, 384 + x, 48, 3) for x in range(3)], frames)
     for x in range(3):
         hi, lo = split(points[x])
-        kt_s[192 + 48 * x : 240 + 48 * x] = hi.astype(BF16)
-        kt_s[336 + 48 * x : 384 + 48 * x] = lo.astype(BF16)
-        kt_s[480 + 48 * x : 528 + 48 * x] = hi.astype(BF16)
-    put(kpt_s, 832, points[0] * points[0] + points[1] * points[1] + points[2] * points[2])
+        kt_ref[192 + 48 * x : 240 + 48 * x] = hi.astype(BF16)
+        kt_ref[336 + 48 * x : 384 + 48 * x] = lo.astype(BF16)
+        kt_ref[480 + 48 * x : 528 + 48 * x] = hi.astype(BF16)
+    put(kpt_s, 816, points[0] * points[0] + points[1] * points[1] + points[2] * points[2])
     nk_s[...] = jnp.zeros_like(nk_s)
-    nk_s[0:H] = sum(take(kpt_s, 832 + p, H, PQ) for p in range(PQ))
+    nk_s[0:H] = sum(take(kpt_s, 816 + p, H, PQ) for p in range(PQ))
     for t, part in enumerate(split3(-gamma16 * nk_s[...])):
-        kt_s[624 + HP * t : 640 + HP * t] = part.astype(BF16)
-    kt_s[672:720] = jnp.ones((48, kt_s.shape[1]), BF16)
-    shape = (48, kt_s.shape[1])
+        kt_ref[624 + HP * t : 640 + HP * t] = part.astype(BF16)
+    kt_ref[672:720] = jnp.ones((48, kt_ref.shape[1]), BF16)
+    shape = (48, kt_ref.shape[1])
     index = lax.broadcasted_iota(jnp.int32, shape, 0)
-    same = (jnp.bitwise_and(index, 7) == kc_ref[...]) & (index < 24)
-    away = jnp.where((index == 24) & (km_ref[...] != 1), FAR, 0.0)
-    kt_s[720:768] = (same.astype(F32) + away).astype(BF16)
+    same = (jnp.bitwise_and(index, 7).astype(F32) == chain) & (index < 24)
+    away = jnp.where((index == 24) & (kept != 1.0), FAR, 0.0)
+    kt_ref[720:768] = (same.astype(F32) + away).astype(BF16)
     points = rotate([take(kpt_s, 528 + x, 96, 3) for x in range(3)], frames)
     for x in range(3):
-        vt_s[128 * x : 128 * x + 96] = points[x].astype(BF16)
-        vt_s[128 * x + 96 : 128 * x + 128] = take(kpt_s, 192 + 32 * x, 32, 1).astype(BF16)
-    vt_s[384:480] = take(kpt_s, 288, 96, 1).astype(BF16)
-    vt_s[480:512] = jnp.zeros((32, vt_s.shape[1]), BF16)
-
-    qp_s[:, :336] = jnp.dot(qs_ref[...], wq_ref[...], preferred_element_type=F32)
-    put(qpt_s, 0, qp_s[...].T)
+        vt_ref[128 * x : 128 * x + 96] = points[x].astype(BF16)
+        vt_ref[128 * x + 96 : 128 * x + 128] = take(kpt_s, 192 + 32 * x, 32, 1).astype(BF16)
+    vt_ref[384:480] = take(kpt_s, 288, 96, 1).astype(BF16)
+    vt_ref[480:512] = jnp.zeros((32, vt_ref.shape[1]), BF16)
+
+
+def prepare_queries(
+    qs_ref, wq_ref, qf_ref, qc_ref, raw_ref, cb_ref, dm_ref, qf_s, m_s, qpt_s, nq_s, qft_s
+):
+    gamma = gamma_of(raw_ref[...])
+    gamma16 = column_of(gamma, HP, 1)
+    gamma48 = column_of(gamma, H * PQ, PQ)
+    put(qpt_s, 0, lax.dot_general(wq_ref[...], qs_ref[...], NT, preferred_element_type=F32))
     frames = qf_ref[...]
     qft_s[0:192] = take(qpt_s, 0, 192, 1).astype(BF16).astype(F32) * (1.0 / math.sqrt(C))
     points = rotate([take(qpt_s, 192 + x, 48, 3) for x in range(3)], frames)
@@ -148,107 +195,172 @@
     qft_s[720:768] = (same | (index == 24)).astype(F32)
     qf_s[...] = qft_s[...].T
 
-    m_s[...] = dm_ref[...]
+    m_s[:, 0 : KD + GL] = dm_ref[...]
+    m_s[:, KD + GL + 256 :] = jnp.broadcast_to(gamma16, (HP, 128))
     lane = lax.broadcasted_iota(jnp.int32, (HP, 128), 1)
     tail = dm_ref[:, 640:768]
     for t, part in enumerate(split3(column_of(cb_ref[...], HP, 1))):
         tail = jnp.where((lane >= 80 + 8 * t) & (lane < 88 + 8 * t), part, tail)
     m_s[:, 640:768] = tail
-    pw_s[...] = jnp.zeros_like(pw_s)
-    pw_s[:, :H] = pw_ref[...].astype(F32)
-    w_s[...] = pw_s[...].T[:HP].astype(BF16)
 
 
 def attend_kernel(
-    ks_ref, wk_ref, kf_ref, kc_ref, km_ref, qs_ref, wq_ref, qf_ref, qc_ref, pw_ref, raw_ref, cb_ref,
-    dm_ref, lm_ref, pair_ref, out_ref,
-    kp_s, kpt_s, qp_s, qpt_s, nk_s, nq_s, pw_s, kt_s, vt_s, qft_s, qf_s, m_s, w_s, o_s,
+    ks_ref, wk_ref, feat_ref, mask_ref, bias_ref, pair_ref,
+    out_ref, kpt_s, nk_s, kt_s, vt_s, v_s, w_s, z_s, o_s, pair_v, pair_sem,
 ):
-    step = pl.program_id(0)
-
-    @pl.when(step == 0)
-    def _():
-        prepare(
-            ks_ref, wk_ref, kf_ref, kc_ref, km_ref, qs_ref, wq_ref, qf_ref, qc_ref, pw_ref, raw_ref,
-            cb_ref, dm_ref, kp_s, kpt_s, qp_s, qpt_s, nk_s, nq_s, pw_s, kt_s, vt_s, qft_s, qf_s,
-            m_s, w_s,
+    queries = pair_ref.shape[0]
+    copies = [
+        pltpu.make_async_copy(
+            pair_ref.at[pl.ds(QB * i, QB)], pair_v.at[pl.ds(QB * i, QB)], pair_sem.at[i]
         )
-
+        for i in range(queries // QB)
+    ]
+    for copy in copies:
+        copy.start()
+    put(kpt_s, 0, jnp.dot(wk_ref[...], ks_ref[...], preferred_element_type=F32))
+    info = mask_ref[:, KD + GL : KD + GL + 256]
+    gamma16 = mask_ref[:, KD + GL + 256 : KD + GL + 257]
+    prepare_keys(info, gamma16, kt_s, vt_s, kpt_s, nk_s)
+    v_s[...] = vt_s[...].T
     rows = QB * HP
-    first = pl.multiple_of(step * QB, QB)
-    mine = qf_s[pl.ds(first, QB), :]
-    spread = (mine[:, None, :] * m_s[...][None]).reshape(rows, KD).astype(BF16)
-    logits = jnp.dot(spread, kt_s[...], preferred_element_type=F32)
-    weight = w_s[...]
-    bias = jnp.concatenate(
-        [lax.dot_general(weight, pair_ref[i], NT, preferred_element_type=F32) for i in range(QB)], 0
-    )
-    logits = math.sqrt(1.0 / 3.0) * (logits + bias)
-    peak = jnp.maximum(jnp.max(logits, 1, keepdims=True), 0.1 * FAR)
-    expd = jnp.exp(logits - peak)
-    total = jnp.maximum(jnp.sum(expd, 1, keepdims=True), 1e-30)
-    weights = expd.astype(BF16)
-    scale = 1.0 / total
-    level = peak + jnp.log(total)
-    hi, lo = split(level)
-    paired = jnp.concatenate(
-        [
-            jnp.dot(weights[HP * i : HP * i + HP], pair_ref[i], preferred_element_type=F32)
-            for i in range(QB)
+    lane = lax.broadcasted_iota(jnp.int32, (rows, 128), 1)
+    gather = (
+        lax.shift_right_logical(lax.broadcasted_iota(jnp.int32, (QB, rows), 1), 4)
+        == lax.broadcasted_iota(jnp.int32, (QB, rows), 0)
+    ).astype(BF16)
+
+    for step in range(queries // QB):
+        first, start = step * QB, step * rows
+        mine = feat_ref[first : first + QB, :]
+        spread = (mine[:, None, :] * mask_ref[:, 0:KD][None]).reshape(rows, KD).astype(BF16)
+        logits = jnp.dot(spread, kt_s[...], preferred_element_type=F32)
+        logits = math.sqrt(1.0 / 3.0) * (logits + bias_ref[start : start + rows, :])
+        peak = jnp.maximum(jnp.max(logits, 1, keepdims=True), 0.1 * FAR)
+        expd = jnp.exp(logits - peak)
+        total = jnp.maximum(jnp.sum(expd, 1, keepdims=True), 1e-30)
+        weights = (expd * (1.0 / total)).astype(BF16)
+        hi, lo = split(peak + jnp.log(total))
+        w_s[start : start + rows, :] = weights
+        spots = jnp.dot(weights, v_s[...], preferred_element_type=F32)
+        tail = jnp.where(lane < 96, spots[:, 384:512], jnp.where(lane < 108, hi, lo))
+        own = [
+            (part.reshape(QB, HP, 128) * mask_ref[:, KD + 128 * row : KD + 128 * row + 128][None])
+            .reshape(rows, 128)
+            .astype(BF16)
+            for row, part in enumerate([spots[:, 128 * r : 128 * r + 128] for r in range(3)] + [tail])
+        ]
+        z_s[first : first + QB, :] = jnp.dot(
+            gather, jnp.concatenate(own, 1), preferred_element_type=F32
+        )
+
+    for step, copy in enumerate(copies):
+        first, start = step * QB, step * rows
+        copy.wait()
+        for i in range(QB):
+            row = start + HP * i
+            o_s[row : row + HP] = jnp.dot(
+                w_s[row : row + HP, :], pair_v[first + i], preferred_element_type=F32
+            )
+        for r in range(4):
+            o_s[pl.ds(start + H + r, QB, stride=HP), :] = z_s[
+                first : first + QB, 128 * r : 128 * r + 128
+            ]
+        out_ref[start : start + rows, :] = o_s[start : start + rows, :].astype(BF16)
+
+
+def inside(x):
+    return pltpu.with_memory_space_constraint(x, pltpu.VMEM)
+
+
+def outside(x):
+    return pltpu.with_memory_space_constraint(x, pltpu.HBM)
+
+
+VMEM = pl.BlockSpec(memory_space=pltpu.VMEM)
+
+
+def spread_out(query_single, key_single, rows, cols):
+    turned = key_single.T
+    return pl.pallas_call(
+        spread_kernel,
+        out_shape=(
+            pltpu.VMEM((cols, *query_single.shape), BF16),
+            pltpu.VMEM((rows, *turned.shape), BF16),
+        ),
+        in_specs=[VMEM, VMEM],
+        out_specs=(VMEM, VMEM),
+        compiler_params=pltpu.CompilerParams(vmem_limit_bytes=4 * 2**20),
+    )(outside(query_single), outside(turned))
+
+
+HBM = pl.BlockSpec(memory_space=pltpu.HBM)
+
+
+def shadow(qs, others, pair):
+    queries, keys = pair.shape[:2]
+    return pl.pallas_call(
+        shadow_kernel,
+        out_shape=(
+            pltpu.VMEM((queries, KD), F32),
+            pltpu.VMEM((HP, KD + GL + keys + 128), F32),
+            pltpu.VMEM(others[10].shape, BF16),
+            pltpu.VMEM((queries * HP, keys), F32),
+        ),
+        in_specs=[VMEM] + [HBM] * 12,
+        out_specs=(VMEM,) * 4,
+        scratch_shapes=[pltpu.VMEM(x.shape, x.dtype) for x in others[:10]]
+        + [
+            pltpu.VMEM((queries // 128, 384, 128), F32),
+            pltpu.VMEM((HP, queries), F32),
+            pltpu.VMEM((KD, queries), F32),
+            pltpu.VMEM((HP, CZ), F32),
+            pltpu.VMEM(pair.shape, BF16),
+            pltpu.SemaphoreType.DMA((11,)),
+            pltpu.SemaphoreType.DMA((queries // QB,)),
         ],
-        0,
-    )
-    o_s[...] = paired * scale
-    spots = lax.dot_general(weights, vt_s[...], NT, preferred_element_type=F32) * scale
-    lane = lax.broadcasted_iota(jnp.int32, (rows, 128), 1)
-    for row in range(4):
-        part = spots[:, 128 * row : 128 * row + 128]
-        if row == 3:
-            part = jnp.where(lane < 96, part, jnp.where(lane < 108, hi, lo))
-        part = part.reshape(QB, HP, 128) * lm_ref[:, 128 * row : 128 * row + 128][None]
-        o_s[pl.ds(H + row, QB, stride=HP), :] = jnp.sum(part, 1)
-    out_ref[...] = o_s[...].astype(BF16)
-
-
-def whole(shape):
-    return pl.BlockSpec(shape, lambda i: (0,) * len(shape))
-
-
-def attend(ks, wk, kf, kc, km, qs, wq, qf, qc, pw, raw, cb, pair):
+        cost_estimate=pl.CostEstimate(
+            flops=2 * queries * keys * CZ * HP, bytes_accessed=pair.size * 2, transcendentals=0
+        ),
+        compiler_params=pltpu.CompilerParams(vmem_limit_bytes=16 * 2**20),
+    )(qs, *[outside(x) for x in (*others, pair)])
+
+
+def attend(ks, wk, feats, mask, bias, pair):
     queries, keys = pair.shape[:2]
-    operands = [
-        ks, wk, kf, kc.reshape(1, -1), km.reshape(1, -1), qs, wq, qf, qc.reshape(1, -1), pw,
-        raw.reshape(1, -1), cb.reshape(1, -1), jnp.asarray(depth_mask()),
-        jnp.asarray((lane_heads()[1][None, :] == np.arange(HP)[:, None]).astype(np.float32)),
-    ]
     return pl.pallas_call(
         attend_kernel,
-        grid=(queries // QB,),
         out_shape=jax.ShapeDtypeStruct((queries * HP, CZ), BF16),
-        in_specs=[whole(x.shape) for x in operands]
-        + [pl.BlockSpec((QB, keys, CZ), lambda i: (i, 0, 0))],
-        out_specs=pl.BlockSpec((QB * HP, CZ), lambda i: (i, 0)),
+        in_specs=[VMEM] * 5 + [HBM],
+        out_specs=VMEM,
         scratch_shapes=[
-            pltpu.VMEM((keys, 896), F32),
             pltpu.VMEM((keys // 128, 896, 128), F32),
-            pltpu.VMEM((queries, 384), F32),
-            pltpu.VMEM((queries // 128, 384, 128), F32),
             pltpu.VMEM((HP, keys), F32),
-            pltpu.VMEM((HP, queries), F32),
-            pltpu.VMEM((CZ, 128), F32),
             pltpu.VMEM((KD, keys), BF16),
             pltpu.VMEM((GL, keys), BF16),
-            pltpu.VMEM((KD, queries), F32),
-            pltpu.VMEM((queries, KD), F32),
-            pltpu.VMEM((HP, KD), F32),
-            pltpu.VMEM((HP, CZ), BF16),
-            pltpu.VMEM((QB * HP, CZ), F32),
+            pltpu.VMEM((keys, GL), BF16),
+            pltpu.VMEM((queries * HP, keys), BF16),
+            pltpu.VMEM((queries, GL), F32),
+            pltpu.VMEM((queries * HP, CZ), F32),
+            pltpu.VMEM(pair.shape, BF16),
+            pltpu.SemaphoreType.DMA((queries // QB,)),
         ],
-        compiler_params=pltpu.CompilerParams(vmem_limit_bytes=32 * 2**20),
-    )(*operands, pair)
-
-
-def finish_kernel(x_ref, qf_ref, em_ref, ow_ref, ob_ref, out_ref, x_s, p_s, g_s, w_s, f_s):
+        cost_estimate=pl.CostEstimate(
+            flops=2 * queries * HP * keys * (KD + GL + CZ),
+            bytes_accessed=queries * keys * CZ * 2,
+            transcendentals=queries * HP * keys,
+        ),
+        compiler_params=pltpu.CompilerParams(vmem_limit_bytes=24 * 2**20),
+    )(ks, *[inside(x) for x in (wk, feats, mask, bias)], outside(pair))
+
+
+def finish_kernel(
+    x_ref, qf_hbm, em_hbm, ob_hbm, ow_hbm, out_ref,
+    qf_ref, em_ref, ob_ref, ow_ref, x_s, p_s, g_s, w_s, f_s, sem,
+):
+    moves = [(em_hbm, em_ref), (qf_hbm, qf_ref), (ob_hbm, ob_ref), (ow_hbm, ow_ref)]
+    copies = [pltpu.make_async_copy(*move, sem.at[i]) for i, move in enumerate(moves)]
+    for copy in copies:
+        copy.start()
     share = out_ref.shape[0]
     sources = x_ref.shape[0]
     first = lax.axis_index("col") * share
@@ -262,6 +374,8 @@
         part = jnp.exp(level - jnp.max(level, 0, keepdims=True))
         part = jnp.where(stat, part / jnp.sum(part, 0, keepdims=True), 0.0)
         hi, lo = split(part)
+        if q == 0:
+            copies[0].wait()
         spread = jnp.dot(hi.astype(BF16), em_ref[...], preferred_element_type=F32) + jnp.dot(
             lo.astype(BF16), em_ref[...], preferred_element_type=F32
         )
@@ -285,6 +399,8 @@
             paired += jnp.dot(wide, block, preferred_element_type=F32)
         p_s[HP * q : HP * q + HP] = paired
 
+    for copy in copies[1:]:
+        copy.wait()
     slot = lax.broadcasted_iota(jnp.int32, (share, 128), 1) == first + lax.broadcasted_iota(
         jnp.int32, (share, 128), 0
     )
@@ -334,18 +450,23 @@
         if head >= 0:
             expand[96 + head, index] = 1.0
     sources = parts.shape[0]
+    others = [qf, jnp.asarray(expand, BF16), out_bias.reshape(1, -1), out_weight]
     return pl.pallas_call(
         finish_kernel,
         out_shape=jax.ShapeDtypeStruct((share, out_bias.shape[0]), BF16),
-        scratch_shapes=[
+        in_specs=[VMEM] + [HBM] * 4,
+        out_specs=VMEM,
+        scratch_shapes=[pltpu.VMEM(x.shape, x.dtype) for x in others]
+        + [
             pltpu.VMEM((sources * HP, 128), F32),
             pltpu.VMEM((share * HP, 128), F32),
             pltpu.VMEM((32, 128), F32),
             pltpu.VMEM((128, 128), F32),
             pltpu.VMEM((share, 896), F32),
+            pltpu.SemaphoreType.DMA((4,)),
         ],
-        compiler_params=pltpu.CompilerParams(vmem_limit_bytes=24 * 2**20),
-    )(parts, qf, jnp.asarray(expand, BF16), out_weight, out_bias.reshape(1, -1))
+        compiler_params=pltpu.CompilerParams(vmem_limit_bytes=12 * 2**20),
+    )(parts, *[outside(x) for x in others])
 
 
 def body(
@@ -366,17 +487,22 @@
     out_bias,
 ):
     rows, cols = lax.axis_size("row"), lax.axis_size("col")
-    turned = key_single.T
-    keys = lax.all_to_all(
-        jnp.broadcast_to(turned[None], (rows, *turned.shape)), "row", 0, 0, tiled=True
-    ).reshape(-1, turned.shape[1])
-    queries = lax.all_to_all(
-        jnp.broadcast_to(query_single[None], (cols, *query_single.shape)), "col", 0, 0, tiled=True
-    ).reshape(-1, query_single.shape[1])
-    sums = attend(
-        keys, w_key, key_frames, key_chain, key_mask, queries, w_query, query_frames, query_chain,
-        pair_weight, point_raw, chain_bias, pair,
+    query_parts, key_parts = spread_out(query_single, key_single, rows, cols)
+    queries = lax.all_to_all(query_parts, "col", 0, 0, tiled=True).reshape(
+        -1, query_single.shape[1]
     )
+    keys = lax.all_to_all(key_parts, "row", 0, 0, tiled=True).reshape(-1, key_single.shape[0])
+    heads = (lane_heads()[1][None, :] == np.arange(HP)[:, None]).astype(np.float32)
+    feats, mask, wk, bias = shadow(
+        queries,
+        [
+            w_query.T, query_frames, query_chain.reshape(1, -1), point_raw.reshape(1, -1),
+            chain_bias.reshape(1, -1), jnp.asarray(np.concatenate([depth_mask(), heads], 1)),
+            key_frames, key_chain.reshape(1, -1), key_mask.reshape(1, -1), pair_weight.T, w_key.T,
+        ],
+        pair,
+    )
+    sums = attend(keys, wk, feats, mask, bias, pair)
     parts = lax.all_to_all(sums.reshape(cols, -1, CZ), "col", 0, 0, tiled=True)
     return finish(parts, query_frames, out_weight, out_bias)
 

time: 84.9 us -> 71 us (0.84)
  local copies, waits for them, and re-layouts: 15.4 us -> 0.62 us
  Pallas kernels: 13 us -> 17.3 us
  waiting for transfers between devices: 23.2 us -> 20.2 us
    unnamed x31 -> x2, local copies, waits for them, and re-layouts: 13.1 us -> 0.01 us
    pallas_call x1 -> x3, Pallas kernels: 10.9 us -> 14.2 us  [the longest x1 6.93 us: attend(): pl.pallas_call(attend_kernel, out_shape=jax.ShapeDtypeStruct((queries * H...]
    all_to_all x1, waiting for transfers between devices: 6.39 us -> 3.96 us  [body(): lax.all_to_all(key_parts, 'row', 0, 0, tiled=True)]
    broadcast_in_dim x2 -> x0, local copies, waits for them, and re-layouts: 2.26 us -> none  [the longest x1 1.42 us: body(): jnp.broadcast_to(turned[None], (rows, *turned.shape))]
    pallas_call x1, Pallas kernels: 2.06 us -> 3.11 us  [finish(): pl.pallas_call(finish_kernel, out_shape=jax.ShapeDtypeStruct((share, out_...]
  transfers between devices with their start and end apart: 2 -> 2, of which waited for: 2 -> 2; matrix products, arithmetic and copies ran while one was open for 4% -> 1% of each run, Pallas kernels for 0% -> 8%
where the time goes in v2:
time: 71 us; the launch traced here: 70.7 us
  waiting for transfers between devices  20.2 us (28%)
  blocking collectives  18.2 us (26%)
  Pallas kernels  17.3 us (24%)
  starting transfers between devices  14.3 us (20%)
    all_to_all x1, blocking collectives, body(): lax.all_to_all(query_parts, 'col', 0, 0, tiled=True)  18.2 us
    all_to_all x1, waiting for transfers between devices, body(): parts = lax.all_to_all(sums.reshape(cols, -1, CZ), 'col', 0, 0, tiled=True)  16.2 us
    all_to_all x1, starting transfers between devices, body(): lax.all_to_all(key_parts, 'row', 0, 0, tiled=True)  7.95 us
    pallas_call x1, Pallas kernels, attend(): pl.pallas_call(attend_kernel, out_shape=jax.ShapeDtypeStruct((queries * H...  6.93 us
    all_to_all x1, starting transfers between devices, body(): parts = lax.all_to_all(sums.reshape(cols, -1, CZ), 'col', 0, 0, tiled=True)  6.32 us
    pallas_call x1, Pallas kernels, shadow(): pl.pallas_call(shadow_kernel, out_shape=(pltpu.VMEM((queries, KD), F32),...  5.82 us
    all_to_all x1, waiting for transfers between devices, body(): lax.all_to_all(key_parts, 'row', 0, 0, tiled=True)  3.96 us
    pallas_call x1, Pallas kernels, finish(): pl.pallas_call(finish_kernel, out_shape=jax.ShapeDtypeStruct((share, out_...  3.11 us
  transfers between devices with their start and end apart: 2, of which 2 were waited for; matrix products, arithmetic and copies ran while one was open for 1% of the time, Pallas kernels for 8%

profile of v2, /device:TPU:1, one launch (start us, length us, event | category | flops | bytes accessed | tf_op | source)
XLA Modules:
  0.0 70.7 jit_solution(1788600743480982485)
XLA Ops:
  0.0 1.4 %shard_map.163 = (bf16[32,4,384]{2,1,0:T(4,128)(2,1)S(1)}, bf16[8,48,256]{2,1,0:T(8,128)(2,1)}) custom-call(bf16[4,384]{1,0:T(4,128)(2,1)} %q_ref.1, bf16[48,256]{1,0:T(8,128)(2,1)} %bitcast.14), custom_call_target="tpu_custom_call" | custom-call | tf_op jit(solution)/shard_map/pallas_call | solution.py:284
  1.4 18.2 %all_to_all.15 = bf16[32,4,384]{2,1,0:T(4,128)(2,1)S(1)} all-to-all(bf16[32,4,384]{2,1,0:T(4,128)(2,1)S(1)} %get-tuple-element.12), channel_id=1, replica_groups=mesh['row'=8,'col'=32] {'col'}, dimensions={0} | all-to-all | bytes 196608 | tf_op jit(solution)/shard_map/all_to_all | solution.py:491
  19.7 7.9 %all-to-all-start = ((bf16[8,48,256]{2,1,0:T(8,128)(2,1)}), bf16[8,48,256]{2,1,0:T(8,128)(2,1)S(1)}, u32[]{:S(2)}, u32[]{:S(2)}) async-start(bf16[8,48,256]{2,1,0:T(8,128)(2,1)} %get-tuple-element.11), calls=%async_computation | async-start | bytes 393216 | tf_op jit(solution)/shard_map/all_to_all | solution.py:494
  27.7 5.8 %shard_map.164 = (f32[128,768]{1,0:T(8,128)S(1)}, f32[16,1664]{1,0:T(8,128)S(1)}, bf16[816,384]{1,0:T(8,128)(2,1)S(1)}, f32[2048,256]{1,0:T(8,128)S(1)}) custom-call(bf16[128,384]{1,0:T(8,128)(2,1)S(1)} %reshape.28.qs_ref, bf16[336,384]{1,0:T(8,128)(2,1)} %bitcast.13, f32[12,128]{1,0:T(8,128)} %qf_hbm.3, s32[1,128]{1,0:T(1,128)} %bitcast.18, ...), custom_call_target="tpu_custom_call" | custom-call | flops 134217728 | bytes 8388608 | tf_op jit(solution)/shard_map/pallas_call | solution.py:301
  33.5 4.0 %all-to-all-done = bf16[8,48,256]{2,1,0:T(8,128)(2,1)S(1)} async-done(((bf16[8,48,256]{2,1,0:T(8,128)(2,1)}), bf16[8,48,256]{2,1,0:T(8,128)(2,1)S(1)}, u32[]{:S(2)}, u32[]{:S(2)}) %all-to-all-start) | async-done | bytes 196640 | tf_op jit(solution)/shard_map/all_to_all | solution.py:494
  37.5 0.0 copy-start
  37.5 6.9 %shard_map.165 = bf16[2048,128]{1,0:T(8,128)(2,1)} custom-call(bf16[384,256]{1,0:T(8,128)(2,1)S(1)} %bitcast.11, bf16[816,384]{1,0:T(8,128)(2,1)S(1)} %get-tuple-element.13.wk_ref, f32[128,768]{1,0:T(8,128)S(1)} %get-tuple-element.14.feat_ref, f32[16,1664]{1,0:T(8,128)S(1)} %get-tuple-element.15.mask_ref, f32[2048,256]{1,0:T(8,128)S(1)} %get-tuple-element.16.bias_ref, ...), custom_call_target="tpu_custom_call" | custom-call | flops 1476395008 | bytes 8388608 | tf_op jit(solution)/shard_map/pallas_call | solution.py:330
  44.4 6.3 %all-to-all-start.2 = ((bf16[32,64,128]{2,1,0:T(8,128)(2,1)}), bf16[32,64,128]{2,1,0:T(8,128)(2,1)S(1)}, u32[]{:S(2)}, u32[]{:S(2)}) async-start(bf16[32,64,128]{2,1,0:T(8,128)(2,1)} %bitcast.10), calls=%async_computation.2 | async-start | bytes 1048576 | tf_op jit(solution)/shard_map/all_to_all | solution.py:506
  50.7 0.0 copy-done
  50.7 0.6 reshape.35.ob_hbm
  51.3 16.2 %all-to-all-done.2.x_ref = bf16[32,64,128]{2,1,0:T(8,128)(2,1)S(1)} async-done(((bf16[32,64,128]{2,1,0:T(8,128)(2,1)}), bf16[32,64,128]{2,1,0:T(8,128)(2,1)S(1)}, u32[]{:S(2)}, u32[]{:S(2)}) %all-to-all-start.2) | async-done | bytes 524320 | tf_op jit(solution)/shard_map/all_to_all | solution.py:506
  67.5 3.1 %shard_map.166 = bf16[4,384]{1,0:T(4,128)(2,1)} custom-call(bf16[32,64,128]{2,1,0:T(8,128)(2,1)S(1)} %all-to-all-done.2.x_ref, f32[12,128]{1,0:T(8,128)} %qf_hbm.3, bf16[128,512]{1,0:T(8,128)(2,1)} %constant.5.clone.em_hbm, f32[1,384]{1,0:T(1,128)} %reshape.35.ob_hbm, bf16[2112,384]{1,0:T(8,128)(2,1)} %ow_hbm.1), custom_call_target="tpu_custom_call" | custom-call | tf_op jit(solution)/shard_map/pallas_call | solution.py:454
  (1 shorter events, 0.0 us)
Async XLA Ops:
  19.7 17.8 %all-to-all-start = ((bf16[8,48,256]{2,1,0:T(8,128)(2,1)}), bf16[8,48,256]{2,1,0:T(8,128)(2,1)S(1)}, u32[]{:S(2)}, u32[]{:S(2)}) async-start(bf16[8,48,256]{2,1,0:T(8,128)(2,1)} %get-tuple-element.11), calls=%async_computation | async-start | bytes 393216 | tf_op jit(solution)/shard_map/all_to_all | solution.py:494
  37.5 13.3 %copy-start = (f32[384]{0:T(512)S(1)}, f32[384]{0:T(512)}, u32[]{:S(2)}) copy-start(f32[384]{0:T(512)} %param.31) | copy-start | bytes 4612
  44.4 23.1 %all-to-all-start.2 = ((bf16[32,64,128]{2,1,0:T(8,128)(2,1)}), bf16[32,64,128]{2,1,0:T(8,128)(2,1)S(1)}, u32[]{:S(2)}, u32[]{:S(2)}) async-start(bf16[32,64,128]{2,1,0:T(8,128)(2,1)} %bitcast.10), calls=%async_computation.2 | async-start | bytes 1048576 | tf_op jit(solution)/shard_map/all_to_all | solution.py:506

commit v3 on v2

--- a/solution.py
+++ b/solution.py
@@ -17,7 +17,9 @@
 HP = 16
 KD = 768
 GL = 512
-QB = 16
+QB = 32
+SB = 16
+SHARE = 4
 FAR = -1e30
 F32 = jnp.float32
 BF16 = jnp.bfloat16
@@ -103,7 +105,7 @@
     qs_ref, wq_hbm, qf_hbm, qc_hbm, raw_hbm, cb_hbm, dm_hbm, kf_hbm, kc_hbm, km_hbm, pw_hbm, wk_hbm,
     pair_ref, feat_ref, mask_ref, wk_ref, bias_ref,
     wq_v, qf_v, qc_v, raw_v, cb_v, dm_v, kf_v, kc_v, km_v, pw_v,
-    qpt_s, nq_s, qft_s, pw_s, pair_v, sem, pair_sem,
+    qpt_s, nq_s, qft_s, pw_s, feat_s, pair_v, sem, pair_sem,
 ):
     moves = [
         (pw_hbm, pw_v), (wq_hbm, wq_v), (qf_hbm, qf_v), (qc_hbm, qc_v), (raw_hbm, raw_v),
@@ -111,11 +113,17 @@
         (wk_hbm, wk_ref),
     ]
     small = [pltpu.make_async_copy(*move, sem.at[i]) for i, move in enumerate(moves)]
+    core = lax.rem(lax.axis_index("col"), 2)
+    groups = SB // SHARE
+    steps = pair_ref.shape[0] // groups
     copies = [
         pltpu.make_async_copy(
-            pair_ref.at[pl.ds(QB * i, QB)], pair_v.at[pl.ds(QB * i, QB)], pair_sem.at[i]
+            pair_ref.at[pl.ds(groups * step, groups), 1 - core if half == 0 else core],
+            pair_v.at[half * steps + step],
+            pair_sem.at[half * steps + step],
         )
-        for i in range(pair_ref.shape[0] // QB)
+        for half in range(2)
+        for step in range(steps)
     ]
     for copy in small[:1] + copies[:4] + small[1:] + copies[4:]:
         copy.start()
@@ -124,19 +132,29 @@
     pw_s[0:H] = pw_v[...].astype(F32)
     weight = pw_s[...].astype(BF16)
     for i, copy in enumerate(copies):
-        if i == 4:
+        if i == len(copies) // 2:
             for other in small[1:]:
                 other.wait()
             prepare_queries(
-                qs_ref, wq_v, qf_v, qc_v, raw_v, cb_v, dm_v, feat_ref, mask_ref, qpt_s, nq_s, qft_s
+                qs_ref, wq_v, qf_v, qc_v, raw_v, cb_v, dm_v, feat_s, mask_ref, qpt_s, nq_s, qft_s
             )
+            count = feat_ref.shape[0] // 2
+            for group in range(2 * count):
+                half = core if group % 2 == 0 else 1 - core
+                feat_ref[(1 - half) * count + group // 2] = feat_s[
+                    SHARE * group : SHARE * group + SHARE, :
+                ]
             mask_ref[0:H, KD + GL : KD + GL + 256] = kf_v[...]
             mask_ref[H : H + 1, KD + GL : KD + GL + 256] = kc_v[...].astype(F32)
             mask_ref[H + 1 : H + 2, KD + GL : KD + GL + 256] = km_v[...].astype(F32)
         copy.wait()
-        for q in range(QB * i, QB * i + QB):
-            bias_ref[HP * q : HP * q + HP] = lax.dot_general(
-                weight, pair_v[q], NT, preferred_element_type=F32
+        for q in range(SB):
+            row = (SB * i + q) * HP
+            bias_ref[row : row + HP] = lax.dot_general(
+                weight,
+                pair_v[i, q // SHARE, q % SHARE],
+                NT,
+                preferred_element_type=F32,
             )
 
 
@@ -206,17 +224,20 @@
 
 def attend_kernel(
     ks_ref, wk_ref, feat_ref, mask_ref, bias_ref, pair_ref,
-    out_ref, kpt_s, nk_s, kt_s, vt_s, v_s, w_s, z_s, o_s, pair_v, pair_sem,
+    send_ref, own_ref, kpt_s, nk_s, kt_s, vt_s, v_s, w_s, z_s, o_s, pair_v, pair_sem,
 ):
-    queries = pair_ref.shape[0]
-    copies = [
-        pltpu.make_async_copy(
-            pair_ref.at[pl.ds(QB * i, QB)], pair_v.at[pl.ds(QB * i, QB)], pair_sem.at[i]
+    core = lax.rem(lax.axis_index("col"), 2)
+    groups = QB // SHARE
+    steps = pair_ref.shape[0] // groups
+    copies = {}
+    for index in range(2 * steps):
+        half, step = divmod(index, steps)
+        copies[index] = pltpu.make_async_copy(
+            pair_ref.at[pl.ds(groups * step, groups), 1 - core if half == 0 else core],
+            pair_v.at[index],
+            pair_sem.at[index],
         )
-        for i in range(queries // QB)
-    ]
-    for copy in copies:
-        copy.start()
+        copies[index].start()
     put(kpt_s, 0, jnp.dot(wk_ref[...], ks_ref[...], preferred_element_type=F32))
     info = mask_ref[:, KD + GL : KD + GL + 256]
     gamma16 = mask_ref[:, KD + GL + 256 : KD + GL + 257]
@@ -229,43 +250,112 @@
         == lax.broadcasted_iota(jnp.int32, (QB, rows), 0)
     ).astype(BF16)
 
-    for step in range(queries // QB):
-        first, start = step * QB, step * rows
-        mine = feat_ref[first : first + QB, :]
-        spread = (mine[:, None, :] * mask_ref[:, 0:KD][None]).reshape(rows, KD).astype(BF16)
-        logits = jnp.dot(spread, kt_s[...], preferred_element_type=F32)
-        logits = math.sqrt(1.0 / 3.0) * (logits + bias_ref[start : start + rows, :])
-        peak = jnp.maximum(jnp.max(logits, 1, keepdims=True), 0.1 * FAR)
-        expd = jnp.exp(logits - peak)
-        total = jnp.maximum(jnp.sum(expd, 1, keepdims=True), 1e-30)
-        weights = (expd * (1.0 / total)).astype(BF16)
-        hi, lo = split(peak + jnp.log(total))
-        w_s[start : start + rows, :] = weights
-        spots = jnp.dot(weights, v_s[...], preferred_element_type=F32)
-        tail = jnp.where(lane < 96, spots[:, 384:512], jnp.where(lane < 108, hi, lo))
-        own = [
-            (part.reshape(QB, HP, 128) * mask_ref[:, KD + 128 * row : KD + 128 * row + 128][None])
-            .reshape(rows, 128)
-            .astype(BF16)
-            for row, part in enumerate([spots[:, 128 * r : 128 * r + 128] for r in range(3)] + [tail])
-        ]
-        z_s[first : first + QB, :] = jnp.dot(
-            gather, jnp.concatenate(own, 1), preferred_element_type=F32
+    for half in range(2):
+        for step in range(steps):
+            start = (half * steps + step) * rows
+            group = start // (SHARE * HP)
+            mine = feat_ref[group : group + groups].reshape(QB, 1, KD)
+            spread = (mine * mask_ref[:, 0:KD][None]).reshape(rows, KD).astype(BF16)
+            logits = jnp.dot(spread, kt_s[...], preferred_element_type=F32)
+            bias = bias_ref[start : start + rows, :]
+            logits = math.sqrt(1.0 / 3.0) * (logits + bias)
+            peak = jnp.maximum(jnp.max(logits, 1, keepdims=True), 0.1 * FAR)
+            expd = jnp.exp(logits - peak)
+            total = jnp.maximum(jnp.sum(expd, 1, keepdims=True), 1e-30)
+            weights = (expd * (1.0 / total)).astype(BF16)
+            hi, lo = split(peak + jnp.log(total))
+            w_s[start : start + rows, :] = weights
+            spots = jnp.dot(weights, v_s[...], preferred_element_type=F32)
+            tail = jnp.where(lane < 96, spots[:, 384:512], jnp.where(lane < 108, hi, lo))
+            own = [
+                (
+                    tile.reshape(QB, HP, 128)
+                    * mask_ref[:, KD + 128 * row : KD + 128 * row + 128][None]
+                )
+                .reshape(rows, 128)
+                .astype(BF16)
+                for row, tile in enumerate(
+                    [spots[:, 128 * r : 128 * r + 128] for r in range(3)] + [tail]
+                )
+            ]
+            z_s[start // HP : start // HP + QB, :] = jnp.dot(
+                gather, jnp.concatenate(own, 1), preferred_element_type=F32
+            )
+
+    for half in range(2):
+        out_ref = (send_ref, own_ref)[half]
+        for step in range(steps):
+            index = half * steps + step
+            start = index * rows
+            copies[index].wait()
+            block = pair_v.at[index]
+            for i in range(QB):
+                row = start + HP * i
+                o_s[row : row + HP] = jnp.dot(
+                    w_s[row : row + HP, :],
+                    block[i // SHARE, i % SHARE],
+                    preferred_element_type=F32,
+                )
+            for r in range(4):
+                o_s[pl.ds(start + H + r, QB, stride=HP), :] = z_s[
+                    start // HP : start // HP + QB, 128 * r : 128 * r + 128
+                ]
+            out_ref[step * rows : step * rows + rows, :] = o_s[start : start + rows, :].astype(BF16)
+
+
+def lane_columns(row):
+    head = lax.broadcasted_iota(jnp.int32, (128, 128), 0) - 96
+    lane = lax.broadcasted_iota(jnp.int32, (128, 128), 1)
+    value = lax.shift_right_logical(lane + (96 if row == 3 else 0), 4)
+    if row < 3:
+        value = jnp.where(
+            lane < 96,
+            lax.shift_right_logical(lane, 3),
+            lax.shift_right_logical(jnp.maximum(lane - 96, 0) + 32 * row, 4),
         )
-
-    for step, copy in enumerate(copies):
-        first, start = step * QB, step * rows
-        copy.wait()
-        for i in range(QB):
-            row = start + HP * i
-            o_s[row : row + HP] = jnp.dot(
-                w_s[row : row + HP, :], pair_v[first + i], preferred_element_type=F32
-            )
-        for r in range(4):
-            o_s[pl.ds(start + H + r, QB, stride=HP), :] = z_s[
-                first : first + QB, 128 * r : 128 * r + 128
-            ]
-        out_ref[start : start + rows, :] = o_s[start : start + rows, :].astype(BF16)
+        return (head == value).astype(BF16)
+    return ((head == value) & (lane < 96)).astype(BF16)
+
+
+def pair_kernel(own_ref, come_ref, out_ref, a_s, b_s):
+    rows = own_ref.shape[0]
+    queries = rows // HP
+    a_s[...] = own_ref[...].astype(F32)
+    b_s[...] = come_ref[...].astype(F32)
+    lane = lax.broadcasted_iota(jnp.int32, (queries, 128), 1)
+    stat = (lane >= 96) & (lane < 108)
+
+    def level(ref):
+        last = ref[pl.ds(HP - 1, queries, stride=HP), :]
+        return jnp.where(stat, last + pltpu.roll(last, 128 - H, 1), 0.0)
+
+    first, second = level(a_s), level(b_s)
+    top = jnp.maximum(first, second)
+    near, far = jnp.exp(first - top), jnp.exp(second - top)
+    both = near + far
+    share = jnp.where(stat, far / both, 0.0)
+    hi, lo = split(top + jnp.log(both))
+    pieces = [piece.astype(BF16) for piece in split(share)]
+    mixed = []
+    for r in range(4):
+        columns = lane_columns(r)
+        weight = sum(jnp.dot(piece, columns, preferred_element_type=F32) for piece in pieces)
+        one = a_s[pl.ds(H + r, queries, stride=HP), :]
+        two = b_s[pl.ds(H + r, queries, stride=HP), :]
+        mixed.append(one + weight * (two - one))
+    mixed[3] = jnp.where(
+        stat, hi, jnp.where((lane >= 108) & (lane < 120), pltpu.roll(lo, H, 1), mixed[3])
+    )
+    own = (
+        lax.broadcasted_iota(jnp.int32, (HP, 128), 0) + 96
+        == lax.broadcasted_iota(jnp.int32, (HP, 128), 1)
+    ).astype(F32)
+    column = jnp.sum((share[:, None, :] * own[None]).reshape(rows, 128), 1, keepdims=True)
+    one = a_s[...]
+    a_s[...] = one + column * (b_s[...] - one)
+    for r in range(4):
+        a_s[pl.ds(H + r, queries, stride=HP), :] = mixed[r]
+    out_ref[...] = a_s[...].astype(BF16)
 
 
 def inside(x):
@@ -298,10 +388,11 @@
 
 def shadow(qs, others, pair):
     queries, keys = pair.shape[:2]
+    pair = pair.reshape(queries // SHARE // 2, 2, SHARE, keys, CZ)
     return pl.pallas_call(
         shadow_kernel,
         out_shape=(
-            pltpu.VMEM((queries, KD), F32),
+            pltpu.VMEM((queries // SHARE, SHARE, KD), F32),
             pltpu.VMEM((HP, KD + GL + keys + 128), F32),
             pltpu.VMEM(others[10].shape, BF16),
             pltpu.VMEM((queries * HP, keys), F32),
@@ -314,9 +405,10 @@
             pltpu.VMEM((HP, queries), F32),
             pltpu.VMEM((KD, queries), F32),
             pltpu.VMEM((HP, CZ), F32),
-            pltpu.VMEM(pair.shape, BF16),
+            pltpu.VMEM((queries, KD), F32),
+            pltpu.VMEM((queries // SB, SB // SHARE, SHARE, keys, CZ), BF16),
             pltpu.SemaphoreType.DMA((11,)),
-            pltpu.SemaphoreType.DMA((queries // QB,)),
+            pltpu.SemaphoreType.DMA((queries // SB,)),
         ],
         cost_estimate=pl.CostEstimate(
             flops=2 * queries * keys * CZ * HP, bytes_accessed=pair.size * 2, transcendentals=0
@@ -325,13 +417,14 @@
     )(qs, *[outside(x) for x in (*others, pair)])
 
 
-def attend(ks, wk, feats, mask, bias, pair):
+def attend(ks, held, pair):
     queries, keys = pair.shape[:2]
+    pair = pair.reshape(queries // SHARE // 2, 2, SHARE, keys, CZ)
     return pl.pallas_call(
         attend_kernel,
-        out_shape=jax.ShapeDtypeStruct((queries * HP, CZ), BF16),
-        in_specs=[VMEM] * 5 + [HBM],
-        out_specs=VMEM,
+        out_shape=(jax.ShapeDtypeStruct((queries * HP // 2, CZ), BF16),) * 2,
+        in_specs=[VMEM] * (len(held) + 1) + [HBM],
+        out_specs=(VMEM,) * 2,
         scratch_shapes=[
             pltpu.VMEM((keys // 128, 896, 128), F32),
             pltpu.VMEM((HP, keys), F32),
@@ -341,7 +434,7 @@
             pltpu.VMEM((queries * HP, keys), BF16),
             pltpu.VMEM((queries, GL), F32),
             pltpu.VMEM((queries * HP, CZ), F32),
-            pltpu.VMEM(pair.shape, BF16),
+            pltpu.VMEM((queries // QB, QB // SHARE, SHARE, keys, CZ), BF16),
             pltpu.SemaphoreType.DMA((queries // QB,)),
         ],
         cost_estimate=pl.CostEstimate(
@@ -349,21 +442,43 @@
             bytes_accessed=queries * keys * CZ * 2,
             transcendentals=queries * HP * keys,
         ),
-        compiler_params=pltpu.CompilerParams(vmem_limit_bytes=24 * 2**20),
-    )(ks, *[inside(x) for x in (wk, feats, mask, bias)], outside(pair))
-
-
-def finish_kernel(
-    x_ref, qf_hbm, em_hbm, ob_hbm, ow_hbm, out_ref,
-    qf_ref, em_ref, ob_ref, ow_ref, x_s, p_s, g_s, w_s, f_s, sem,
-):
-    moves = [(em_hbm, em_ref), (qf_hbm, qf_ref), (ob_hbm, ob_ref), (ow_hbm, ow_ref)]
+        compiler_params=pltpu.CompilerParams(vmem_limit_bytes=20 * 2**20),
+    )(ks, *[inside(x) for x in held], outside(pair))
+
+
+def join(own, come):
+    return pl.pallas_call(
+        pair_kernel,
+        out_shape=jax.ShapeDtypeStruct(own.shape, BF16),
+        in_specs=[VMEM, VMEM],
+        out_specs=VMEM,
+        scratch_shapes=[pltpu.VMEM(own.shape, F32)] * 2,
+        compiler_params=pltpu.CompilerParams(vmem_limit_bytes=8 * 2**20),
+    )(own, come)
+
+
+def fetch_kernel(after, qf_hbm, em_hbm, ob_hbm, ow_hbm, fr_ref, em_ref, ob_ref, ow_ref, qf_v, sem):
+    moves = [(qf_hbm, qf_v), (em_hbm, em_ref), (ob_hbm, ob_ref), (ow_hbm, ow_ref)]
     copies = [pltpu.make_async_copy(*move, sem.at[i]) for i, move in enumerate(moves)]
     for copy in copies:
         copy.start()
+    copies[0].wait()
+    first = lax.axis_index("col") * SHARE
+    shape = (fr_ref.shape[0], 128)
+    lane = lax.broadcasted_iota(jnp.int32, shape, 1)
+    slot = lane == first + lax.broadcasted_iota(jnp.int32, shape, 0)
+    frame = jnp.zeros(shape, F32)
+    for j in range(12):
+        value = jnp.sum(jnp.where(slot, qf_v[j : j + 1, :], 0.0), 1, keepdims=True)
+        frame = jnp.where(lane == j, value, frame)
+    fr_ref[...] = frame
+    for copy in copies[1:]:
+        copy.wait()
+
+
+def finish_kernel(x_ref, fr_ref, em_ref, ob_ref, ow_ref, out_ref, x_s, p_s, g_s, w_s, f_s):
     share = out_ref.shape[0]
     sources = x_ref.shape[0]
-    first = lax.axis_index("col") * share
     lane = lax.broadcasted_iota(jnp.int32, (sources, 128), 1)
     stat = (lane >= 96) & (lane < 108)
     for q in range(share):
@@ -374,8 +489,6 @@
         part = jnp.exp(level - jnp.max(level, 0, keepdims=True))
         part = jnp.where(stat, part / jnp.sum(part, 0, keepdims=True), 0.0)
         hi, lo = split(part)
-        if q == 0:
-            copies[0].wait()
         spread = jnp.dot(hi.astype(BF16), em_ref[...], preferred_element_type=F32) + jnp.dot(
             lo.astype(BF16), em_ref[...], preferred_element_type=F32
         )
@@ -399,14 +512,7 @@
             paired += jnp.dot(wide, block, preferred_element_type=F32)
         p_s[HP * q : HP * q + HP] = paired
 
-    for copy in copies[1:]:
-        copy.wait()
-    slot = lax.broadcasted_iota(jnp.int32, (share, 128), 1) == first + lax.broadcasted_iota(
-        jnp.int32, (share, 128), 0
-    )
-    frame = [
-        jnp.sum(jnp.where(slot, qf_ref[j : j + 1, :], 0.0), 1, keepdims=True) for j in range(12)
-    ]
+    frame = [fr_ref[0:share, j : j + 1] for j in range(12)]
     g = [g_s[8 * r : 8 * r + share, :] for r in range(4)]
     moved = [g[x] - frame[9 + x] for x in range(3)]
     local = [
@@ -443,30 +549,43 @@
     out_ref[...] = total.astype(BF16)
 
 
-def finish(parts, qf, out_weight, out_bias):
-    share = parts.shape[1] // HP
+def fetch(after, qf, out_weight, out_bias):
     expand = np.zeros((128, GL), np.float32)
     for index, head in enumerate(lane_heads()[0]):
         if head >= 0:
             expand[96 + head, index] = 1.0
-    sources = parts.shape[0]
     others = [qf, jnp.asarray(expand, BF16), out_bias.reshape(1, -1), out_weight]
     return pl.pallas_call(
+        fetch_kernel,
+        out_shape=(
+            pltpu.VMEM((8, 128), F32),
+            *[pltpu.VMEM(x.shape, x.dtype) for x in others[1:]],
+        ),
+        in_specs=[pl.BlockSpec(memory_space=pl.ANY)] + [HBM] * 4,
+        out_specs=(VMEM,) * 4,
+        scratch_shapes=[pltpu.VMEM(qf.shape, F32), pltpu.SemaphoreType.DMA((4,))],
+        cost_estimate=pl.CostEstimate(flops=0, bytes_accessed=4 * 2**20, transcendentals=0),
+        compiler_params=pltpu.CompilerParams(vmem_limit_bytes=4 * 2**20),
+    )(after, *[outside(x) for x in others])
+
+
+def finish(parts, others, columns):
+    share = parts.shape[1] // HP
+    sources = parts.shape[0]
+    return pl.pallas_call(
         finish_kernel,
-        out_shape=jax.ShapeDtypeStruct((share, out_bias.shape[0]), BF16),
-        in_specs=[VMEM] + [HBM] * 4,
+        out_shape=jax.ShapeDtypeStruct((share, columns), BF16),
+        in_specs=[VMEM] * 5,
         out_specs=VMEM,
-        scratch_shapes=[pltpu.VMEM(x.shape, x.dtype) for x in others]
-        + [
+        scratch_shapes=[
             pltpu.VMEM((sources * HP, 128), F32),
             pltpu.VMEM((share * HP, 128), F32),
             pltpu.VMEM((32, 128), F32),
             pltpu.VMEM((128, 128), F32),
             pltpu.VMEM((share, 896), F32),
-            pltpu.SemaphoreType.DMA((4,)),
         ],
-        compiler_params=pltpu.CompilerParams(vmem_limit_bytes=12 * 2**20),
-    )(parts, *[outside(x) for x in others])
+        compiler_params=pltpu.CompilerParams(vmem_limit_bytes=4 * 2**20),
+    )(parts, *[inside(x) for x in others])
 
 
 def body(
@@ -493,7 +612,7 @@
     )
     keys = lax.all_to_all(key_parts, "row", 0, 0, tiled=True).reshape(-1, key_single.shape[0])
     heads = (lane_heads()[1][None, :] == np.arange(HP)[:, None]).astype(np.float32)
-    feats, mask, wk, bias = shadow(
+    feats, mask, wk, *held = shadow(
         queries,
         [
             w_query.T, query_frames, query_chain.reshape(1, -1), point_raw.reshape(1, -1),
@@ -502,9 +621,13 @@
         ],
         pair,
     )
-    sums = attend(keys, wk, feats, mask, bias, pair)
-    parts = lax.all_to_all(sums.reshape(cols, -1, CZ), "col", 0, 0, tiled=True)
-    return finish(parts, query_frames, out_weight, out_bias)
+    send, own = attend(keys, [wk, feats, mask, *held], pair)
+    come = lax.ppermute(send, "col", [(i, i ^ 1) for i in range(cols)])
+    sums = join(own, come).reshape(cols // 2, -1, CZ)
+    groups = [list(range(core, cols, 2)) for core in range(2)]
+    parts = lax.all_to_all(sums, "col", 0, 0, axis_index_groups=groups, tiled=True)
+    others = fetch(sums, query_frames, out_weight, out_bias)
+    return finish(parts, others, out_weight.shape[1])
 
 
 def solution(mesh):

time: 71 us -> 65.4 us (0.921)
  the two profiles are of different devices: /device:TPU:1 before, /device:TPU:2 now
where the time goes in v3:
time: 65.4 us; the launch traced here: 64.2 us
  Pallas kernels  19.3 us (30%)
  blocking collectives  17.1 us (26%)
  waiting for transfers between devices  13.8 us (21%)
  starting transfers between devices  13.3 us (20%)
    all_to_all x1, blocking collectives, body(): lax.all_to_all(query_parts, 'col', 0, 0, tiled=True)  17.1 us
    all_to_all x1, waiting for transfers between devices, body(): lax.all_to_all(sums, 'col', 0, 0, axis_index_groups=groups, tiled=True)  9.03 us
    all_to_all x1, starting transfers between devices, body(): lax.all_to_all(key_parts, 'row', 0, 0, tiled=True)  8.76 us
    pallas_call x1, Pallas kernels, attend(): pl.pallas_call(attend_kernel, out_shape=(jax.ShapeDtypeStruct((queries *...  7.32 us
    pallas_call x1, Pallas kernels, shadow(): pl.pallas_call(shadow_kernel, out_shape=(pltpu.VMEM((queries // SHARE, SH...  5.88 us
    all_to_all x1, starting transfers between devices, body(): lax.all_to_all(sums, 'col', 0, 0, axis_index_groups=groups, tiled=True)  4.4 us
    all_to_all x1, waiting for transfers between devices, body(): lax.all_to_all(key_parts, 'row', 0, 0, tiled=True)  3.25 us
    pallas_call x1, Pallas kernels, finish(): pl.pallas_call(finish_kernel, out_shape=jax.ShapeDtypeStruct((share, colu...  1.93 us
  transfers between devices with their start and end apart: 3, of which 3 were waited for; matrix products, arithmetic and copies ran while one was open for 1% of the time, Pallas kernels for 12%

profile of v3, /device:TPU:2, one launch (start us, length us, event | category | flops | bytes accessed | tf_op | source)
XLA Modules:
  0.0 64.2 jit_solution(5340232042979313061)
XLA Ops:
  0.0 1.4 %shard_map.163 = (bf16[32,4,384]{2,1,0:T(4,128)(2,1)S(1)}, bf16[8,48,256]{2,1,0:T(8,128)(2,1)}) custom-call(bf16[4,384]{1,0:T(4,128)(2,1)} %q_ref.1, bf16[48,256]{1,0:T(8,128)(2,1)} %bitcast.17), custom_call_target="tpu_custom_call" | custom-call | tf_op jit(solution)/shard_map/pallas_call | solution.py:374
  1.4 17.1 %all_to_all.15 = bf16[32,4,384]{2,1,0:T(4,128)(2,1)S(1)} all-to-all(bf16[32,4,384]{2,1,0:T(4,128)(2,1)S(1)} %get-tuple-element.18), channel_id=1, replica_groups=mesh['row'=8,'col'=32] {'col'}, dimensions={0} | all-to-all | bytes 196608 | tf_op jit(solution)/shard_map/all_to_all | solution.py:610
  18.6 8.8 %all-to-all-start = ((bf16[8,48,256]{2,1,0:T(8,128)(2,1)}), bf16[8,48,256]{2,1,0:T(8,128)(2,1)S(1)}, u32[]{:S(2)}, u32[]{:S(2)}) async-start(bf16[8,48,256]{2,1,0:T(8,128)(2,1)} %get-tuple-element.17), calls=%async_computation | async-start | bytes 393216 | tf_op jit(solution)/shard_map/all_to_all | solution.py:613
  27.4 5.9 %shard_map.164 = (f32[32,4,768]{2,1,0:T(4,128)S(1)}, f32[16,1664]{1,0:T(8,128)S(1)}, bf16[816,384]{1,0:T(8,128)(2,1)S(1)}, f32[2048,256]{1,0:T(8,128)S(1)}) custom-call(bf16[128,384]{1,0:T(8,128)(2,1)S(1)} %reshape.32.qs_ref, bf16[336,384]{1,0:T(8,128)(2,1)} %bitcast.16, f32[12,128]{1,0:T(8,128)} %qf_hbm.3, s32[1,128]{1,0:T(1,128)} %bitcast.21, ...), custom_call_target="tpu_custom_call" | custom-call | flops 134217728 | bytes 8388608 | tf_op jit(solution)/shard_map/pallas_call | solution.py:392
  33.3 3.2 %all-to-all-done = bf16[8,48,256]{2,1,0:T(8,128)(2,1)S(1)} async-done(((bf16[8,48,256]{2,1,0:T(8,128)(2,1)}), bf16[8,48,256]{2,1,0:T(8,128)(2,1)S(1)}, u32[]{:S(2)}, u32[]{:S(2)}) %all-to-all-start) | async-done | bytes 196640 | tf_op jit(solution)/shard_map/all_to_all | solution.py:613
  36.5 0.0 copy-start
  36.5 7.3 %shard_map.165 = (bf16[1024,128]{1,0:T(8,128)(2,1)S(1)}, bf16[1024,128]{1,0:T(8,128)(2,1)S(1)}) custom-call(bf16[384,256]{1,0:T(8,128)(2,1)S(1)} %bitcast.12, bf16[816,384]{1,0:T(8,128)(2,1)S(1)} %get-tuple-element.19.wk_ref, f32[32,4,768]{2,1,0:T(4,128)S(1)} %get-tuple-element.20.feat_ref, f32[16,1664]{1,0:T(8,128)S(1)} %get-tuple-element.21.mask_ref, ...), custom_call_target="tpu_custom_call" | custom-call | flops 1476395008 | bytes 8388608 | tf_op jit(solution)/shard_map/pallas_call | solution.py:423
  43.8 0.1 collective-permute-start
  43.9 1.5 %collective-permute-done.come_ref = bf16[1024,128]{1,0:T(8,128)(2,1)S(1)} collective-permute-done((bf16[1024,128]{1,0:T(8,128)(2,1)S(1)}, bf16[1024,128]{1,0:T(8,128)(2,1)S(1)}, u32[]{:S(2)}, u32[]{:S(2)}) %collective-permute-start) | collective-permute-done | bytes 262176 | tf_op jit(solution)/shard_map/ppermute | solution.py:625
  45.5 1.2 %shard_map.166 = bf16[1024,128]{1,0:T(8,128)(2,1)} custom-call(bf16[1024,128]{1,0:T(8,128)(2,1)S(1)} %get-tuple-element.23.own_ref, bf16[1024,128]{1,0:T(8,128)(2,1)S(1)} %collective-permute-done.come_ref), custom_call_target="tpu_custom_call" | custom-call | tf_op jit(solution)/shard_map/pallas_call | solution.py:450
  46.6 4.4 %all-to-all-start.2 = ((bf16[16,64,128]{2,1,0:T(8,128)(2,1)}), bf16[16,64,128]{2,1,0:T(8,128)(2,1)S(1)}, u32[]{:S(2)}, u32[]{:S(2)}) async-start(bf16[16,64,128]{2,1,0:T(8,128)(2,1)} %bitcast.11.after), calls=%async_computation.2 | async-start | bytes 524288 | tf_op jit(solution)/shard_map/all_to_all | solution.py:628
  51.0 0.0 copy-done
  51.1 0.6 reshape.40.ob_hbm
  51.6 1.6 %shard_map.167 = (f32[8,128]{1,0:T(8,128)S(1)}, bf16[128,512]{1,0:T(8,128)(2,1)S(1)}, f32[1,384]{1,0:T(1,128)S(1)}, bf16[2112,384]{1,0:T(8,128)(2,1)S(1)}) custom-call(bf16[16,64,128]{2,1,0:T(8,128)(2,1)} %bitcast.11.after, f32[12,128]{1,0:T(8,128)} %qf_hbm.3, bf16[128,512]{1,0:T(8,128)(2,1)} %constant.5.clone.em_hbm, f32[1,384]{1,0:T(1,128)} %reshape.40.ob_hbm, ...), custom_call_target="tpu_custom_call" | custom-call | bytes 4194304 | tf_op jit(solution)/shard_map/pallas_call | solution.py:558
  53.2 9.0 %all-to-all-done.2.x_ref = bf16[16,64,128]{2,1,0:T(8,128)(2,1)S(1)} async-done(((bf16[16,64,128]{2,1,0:T(8,128)(2,1)}), bf16[16,64,128]{2,1,0:T(8,128)(2,1)S(1)}, u32[]{:S(2)}, u32[]{:S(2)}) %all-to-all-start.2) | async-done | bytes 262176 | tf_op jit(solution)/shard_map/all_to_all | solution.py:628
  62.2 1.9 %shard_map.168 = bf16[4,384]{1,0:T(4,128)(2,1)} custom-call(bf16[16,64,128]{2,1,0:T(8,128)(2,1)S(1)} %all-to-all-done.2.x_ref, f32[8,128]{1,0:T(8,128)S(1)} %get-tuple-element.25.fr_ref, bf16[128,512]{1,0:T(8,128)(2,1)S(1)} %get-tuple-element.26.em_ref, f32[1,384]{1,0:T(1,128)S(1)} %get-tuple-element.27.ob_ref, bf16[2112,384]{1,0:T(8,128)(2,1)S(1)} %get-tuple-element.28.ow_ref), custom_call_target="tpu_custom_call" | custom-call | tf_op jit(solution)/shard_map/pallas_call | solution.py:575
  (1 shorter events, 0.0 us)
Async XLA Ops:
  18.6 17.9 %all-to-all-start = ((bf16[8,48,256]{2,1,0:T(8,128)(2,1)}), bf16[8,48,256]{2,1,0:T(8,128)(2,1)S(1)}, u32[]{:S(2)}, u32[]{:S(2)}) async-start(bf16[8,48,256]{2,1,0:T(8,128)(2,1)} %get-tuple-element.17), calls=%async_computation | async-start | bytes 393216 | tf_op jit(solution)/shard_map/all_to_all | solution.py:613
  36.5 14.5 %copy-start = (f32[384]{0:T(512)S(1)}, f32[384]{0:T(512)}, u32[]{:S(2)}) copy-start(f32[384]{0:T(512)} %param.31) | copy-start | bytes 4612
  43.8 1.6 %collective-permute-start = (bf16[1024,128]{1,0:T(8,128)(2,1)S(1)}, bf16[1024,128]{1,0:T(8,128)(2,1)S(1)}, u32[]{:S(2)}, u32[]{:S(2)}) collective-permute-start(bf16[1024,128]{1,0:T(8,128)(2,1)S(1)} %get-tuple-element.24), channel_id=1, source_target_pairs={{0,1},{1,0},{2,3},{3,2},{4,5},{5,4},{6,7},{7,6},{8,9},{9,8},{10,11... | collective-permute-start | bytes 786440 | tf_op jit(solution)/shard_map/ppermute | solution.py:625
  46.6 15.6 %all-to-all-start.2 = ((bf16[16,64,128]{2,1,0:T(8,128)(2,1)}), bf16[16,64,128]{2,1,0:T(8,128)(2,1)S(1)}, u32[]{:S(2)}, u32[]{:S(2)}) async-start(bf16[16,64,128]{2,1,0:T(8,128)(2,1)} %bitcast.11.after), calls=%async_computation.2 | async-start | bytes 524288 | tf_op jit(solution)/shard_map/all_to_all | solution.py:628

commit v4 on v3

--- a/solution.py
+++ b/solution.py
@@ -94,11 +94,6 @@
 def gamma_of(raw):
     soft = jnp.maximum(raw, 0.0) + jnp.log1p(jnp.exp(-jnp.abs(raw)))
     return (0.5 * math.sqrt(2.0 / (9.0 * PQ))) * soft
-
-
-def spread_kernel(q_ref, k_ref, q_out, k_out):
-    q_out[...] = jnp.broadcast_to(q_ref[...][None], q_out.shape)
-    k_out[...] = jnp.broadcast_to(k_ref[...][None], k_out.shape)
 
 
 def shadow_kernel(
@@ -223,8 +218,8 @@
 
 
 def attend_kernel(
-    ks_ref, wk_ref, feat_ref, mask_ref, bias_ref, pair_ref,
-    send_ref, own_ref, kpt_s, nk_s, kt_s, vt_s, v_s, w_s, z_s, o_s, pair_v, pair_sem,
+    near_ref, far_ref, wk_ref, feat_ref, mask_ref, bias_ref, pair_ref,
+    send_ref, own_ref, kpt_s, nk_s, kt_s, vt_s, v_s, w_s, z_s, o_s, ks_s, pair_v, pair_sem,
 ):
     core = lax.rem(lax.axis_index("col"), 2)
     groups = QB // SHARE
@@ -238,7 +233,13 @@
             pair_sem.at[index],
         )
         copies[index].start()
-    put(kpt_s, 0, jnp.dot(wk_ref[...], ks_ref[...], preferred_element_type=F32))
+    row = lax.axis_index("row")
+    count, part = near_ref.shape[:2]
+    for k in range(count):
+        x = lax.rem(lax.div(row, 2) + k, count)
+        for ref, z in ((near_ref, lax.rem(row, 2)), (far_ref, 1 - lax.rem(row, 2))):
+            ks_s[pl.ds(pl.multiple_of((2 * x + z) * part, part), part), :] = ref[k]
+    put(kpt_s, 0, jnp.dot(wk_ref[...], ks_s[...], preferred_element_type=F32))
     info = mask_ref[:, KD + GL : KD + GL + 256]
     gamma16 = mask_ref[:, KD + GL + 256 : KD + GL + 257]
     prepare_keys(info, gamma16, kt_s, vt_s, kpt_s, nk_s)
@@ -369,20 +370,6 @@
 VMEM = pl.BlockSpec(memory_space=pltpu.VMEM)
 
 
-def spread_out(query_single, key_single, rows, cols):
-    turned = key_single.T
-    return pl.pallas_call(
-        spread_kernel,
-        out_shape=(
-            pltpu.VMEM((cols, *query_single.shape), BF16),
-            pltpu.VMEM((rows, *turned.shape), BF16),
-        ),
-        in_specs=[VMEM, VMEM],
-        out_specs=(VMEM, VMEM),
-        compiler_params=pltpu.CompilerParams(vmem_limit_bytes=4 * 2**20),
-    )(outside(query_single), outside(turned))
-
-
 HBM = pl.BlockSpec(memory_space=pltpu.HBM)
 
 
@@ -417,13 +404,13 @@
     )(qs, *[outside(x) for x in (*others, pair)])
 
 
-def attend(ks, held, pair):
+def attend(near, far, held, pair):
     queries, keys = pair.shape[:2]
     pair = pair.reshape(queries // SHARE // 2, 2, SHARE, keys, CZ)
     return pl.pallas_call(
         attend_kernel,
         out_shape=(jax.ShapeDtypeStruct((queries * HP // 2, CZ), BF16),) * 2,
-        in_specs=[VMEM] * (len(held) + 1) + [HBM],
+        in_specs=[VMEM] * (len(held) + 2) + [HBM],
         out_specs=(VMEM,) * 2,
         scratch_shapes=[
             pltpu.VMEM((keys // 128, 896, 128), F32),
@@ -434,6 +421,7 @@
             pltpu.VMEM((queries * HP, keys), BF16),
             pltpu.VMEM((queries, GL), F32),
             pltpu.VMEM((queries * HP, CZ), F32),
+            pltpu.VMEM((384, keys), BF16),
             pltpu.VMEM((queries // QB, QB // SHARE, SHARE, keys, CZ), BF16),
             pltpu.SemaphoreType.DMA((queries // QB,)),
         ],
@@ -443,7 +431,7 @@
             transcendentals=queries * HP * keys,
         ),
         compiler_params=pltpu.CompilerParams(vmem_limit_bytes=20 * 2**20),
-    )(ks, *[inside(x) for x in held], outside(pair))
+    )(near, far, *[inside(x) for x in held], outside(pair))
 
 
 def join(own, come):
@@ -606,11 +594,21 @@
     out_bias,
 ):
     rows, cols = lax.axis_size("row"), lax.axis_size("col")
-    query_parts, key_parts = spread_out(query_single, key_single, rows, cols)
-    queries = lax.all_to_all(query_parts, "col", 0, 0, tiled=True).reshape(
-        -1, query_single.shape[1]
+    turned = key_single.T
+    chips = rows // 2
+    near = jnp.stack(
+        [turned]
+        + [
+            lax.ppermute(
+                turned, "row", [((i + 2 * k) % rows, i) for i in range(rows)]
+            )
+            for k in range(1, chips)
+        ]
     )
-    keys = lax.all_to_all(key_parts, "row", 0, 0, tiled=True).reshape(-1, key_single.shape[0])
+    far = lax.ppermute(near, "row", [(i, i ^ 1) for i in range(rows)])
+    queries = lax.all_to_all(
+        jnp.broadcast_to(query_single[None], (cols, *query_single.shape)), "col", 0, 0, tiled=True
+    ).reshape(-1, query_single.shape[1])
     heads = (lane_heads()[1][None, :] == np.arange(HP)[:, None]).astype(np.float32)
     feats, mask, wk, *held = shadow(
         queries,
@@ -621,7 +619,7 @@
         ],
         pair,
     )
-    send, own = attend(keys, [wk, feats, mask, *held], pair)
+    send, own = attend(near, far, [wk, feats, mask, *held], pair)
     come = lax.ppermute(send, "col", [(i, i ^ 1) for i in range(cols)])
     sums = join(own, come).reshape(cols // 2, -1, CZ)
     groups = [list(range(core, cols, 2)) for core in range(2)]

time: 65.4 us -> 57.5 us (0.88); the launches traced: 64.2 us -> 57.1 us
  blocking collectives: 17.1 us -> 0 us
  starting transfers between devices: 13.3 us -> 22.8 us
  Pallas kernels: 19.3 us -> 17.9 us
  local copies, waits for them, and re-layouts: 0.6 us -> 1.94 us
  other arithmetic: 0 us -> 0.76 us
    all_to_all x1 -> x0, blocking collectives: 17.1 us -> none  [body(): lax.all_to_all(query_parts, 'col', 0, 0, tiled=True)]
    ppermute x0 -> x4, starting transfers between devices: none -> 9.33 us  [the longest x3 4.76 us: body(): lax.ppermute(turned, 'row', [((i + 2 * k) % rows, i) for i in range(rows)])]
    pallas_call x1 -> x0, Pallas kernels: 1.45 us -> none  [spread_out(): pl.pallas_call(spread_kernel, out_shape=(pltpu.VMEM((cols, *query_single....]
    broadcast_in_dim x0 -> x1, local copies, waits for them, and re-layouts: none -> 1.34 us  [body(): jnp.broadcast_to(query_single[None], (cols, *query_single.shape))]
    another operation x0 -> x1, other arithmetic: none -> 0.76 us  [body(): jnp.stack([turned] + [lax.ppermute(turned, 'row', [((i + 2 * k) % rows, i...]
  transfers between devices with their start and end apart: 3 -> 7, of which waited for: 3 -> 3; matrix products, arithmetic and copies ran while one was open for 1% -> 5% of each run, Pallas kernels for 12% -> 13%
where the time goes in v4:
time: 57.5 us; the launch traced here: 57.1 us
  starting transfers between devices  22.8 us (40%)
  Pallas kernels  17.9 us (31%)
  waiting for transfers between devices  13.5 us (23%)
  local copies, waits for them, and re-layouts  1.94 us (3%)
  other arithmetic  0.76 us (1%)
    all_to_all x1, waiting for transfers between devices, body(): lax.all_to_all(sums, 'col', 0, 0, axis_index_groups=groups, tiled=True)  9.03 us
    all_to_all x1, starting transfers between devices, body(): lax.all_to_all(jnp.broadcast_to(query_single[None], (cols, *query_single....  8.92 us
    pallas_call x1, Pallas kernels, attend(): pl.pallas_call(attend_kernel, out_shape=(jax.ShapeDtypeStruct((queries *...  7.36 us
    pallas_call x1, Pallas kernels, shadow(): pl.pallas_call(shadow_kernel, out_shape=(pltpu.VMEM((queries // SHARE, SH...  5.88 us
    ppermute x3, starting transfers between devices, body(): lax.ppermute(turned, 'row', [((i + 2 * k) % rows, i) for i in range(rows)])  4.76 us
    ppermute x1, starting transfers between devices, body(): far = lax.ppermute(near, 'row', [(i, i ^ 1) for i in range(rows)])  4.58 us
    all_to_all x1, starting transfers between devices, body(): lax.all_to_all(sums, 'col', 0, 0, axis_index_groups=groups, tiled=True)  4.34 us
    all_to_all x1, waiting for transfers between devices, body(): lax.all_to_all(jnp.broadcast_to(query_single[None], (cols, *query_single....  3.07 us
  transfers between devices with their start and end apart: 7, of which 3 were waited for; matrix products, arithmetic and copies ran while one was open for 5% of the time, Pallas kernels for 13%

profile of v4, /device:TPU:2, one launch (start us, length us, event | category | flops | bytes accessed | tf_op | source)
XLA Modules:
  0.0 57.1 jit_solution(5251142860348179184)
XLA Ops:
  0.0 2.3 %collective-permute-start = (bf16[48,256]{1,0:T(8,128)(2,1)}, bf16[48,256]{1,0:T(8,128)(2,1)S(1)}, u32[]{:S(2)}, u32[]{:S(2)}) collective-permute-start(bf16[48,256]{1,0:T(8,128)(2,1)} %bitcast.20), channel_id=1, source_target_pairs={{64,0},{96,32},{128,64},{160,96},{192,128},{224,160},{0,192},{32,2... | collective-permute-start | bytes 73736 | tf_op jit(solution)/shard_map/ppermute | solution.py:602
  2.3 0.7 %collective-permute-start.1 = (bf16[48,256]{1,0:T(8,128)(2,1)}, bf16[48,256]{1,0:T(8,128)(2,1)S(1)}, u32[]{:S(2)}, u32[]{:S(2)}) collective-permute-start(bf16[48,256]{1,0:T(8,128)(2,1)} %bitcast.21), channel_id=1, source_target_pairs={{128,0},{160,32},{192,64},{224,96},{0,128},{32,160},{64,192},{96,2... | collective-permute-start | bytes 73736 | tf_op jit(solution)/shard_map/ppermute | solution.py:602
  3.0 1.8 %collective-permute-start.2 = (bf16[48,256]{1,0:T(8,128)(2,1)}, bf16[48,256]{1,0:T(8,128)(2,1)S(1)}, u32[]{:S(2)}, u32[]{:S(2)}) collective-permute-start(bf16[48,256]{1,0:T(8,128)(2,1)} %bitcast.22), channel_id=1, source_target_pairs={{192,0},{224,32},{0,64},{32,96},{64,128},{96,160},{128,192},{160,2... | collective-permute-start | bytes 73736 | tf_op jit(solution)/shard_map/ppermute | solution.py:602
  4.8 1.3 %broadcast_in_dim.2 = bf16[32,4,384]{2,1,0:T(4,128)(2,1)} broadcast(bf16[4,384]{1,0:T(4,128)(2,1)} %param.17), dimensions={1,2} | broadcast | bytes 101376 | tf_op jit(solution)/shard_map/broadcast_in_dim | solution.py:610
  6.1 8.9 %all-to-all-start = ((bf16[32,4,384]{2,1,0:T(4,128)(2,1)}), bf16[32,4,384]{2,1,0:T(4,128)(2,1)S(1)}, u32[]{:S(2)}, u32[]{:S(2)}) async-start(bf16[32,4,384]{2,1,0:T(4,128)(2,1)} %broadcast_in_dim.2), calls=%async_computation | async-start | bytes 196608 | tf_op jit(solution)/shard_map/all_to_all | solution.py:609
  15.0 0.0 collective-permute-done
  15.0 0.0 collective-permute-done.1
  15.0 0.0 collective-permute-done.2
  15.1 0.8 %pad_maximum_fusion.near_ref = bf16[4,48,256]{2,1,0:T(8,128)(2,1)S(1)} fusion(bf16[1,48,256]{2,1,0:T(8,128)(2,1)S(1)} %bitcast.26, bf16[1,48,256]{2,1,0:T(8,128)(2,1)S(1)} %bitcast.25, bf16[1,48,256]{2,1,0:T(8,128)(2,1)S(1)} %bitcast.24, bf16[1,48,256]{2,1,0:T(8,128)(2,1)} %bitcast.23), kind=kLoop, calls=%fused_computation | loop fusion | flops 147456 | bytes 196608 | tf_op jit(solution)/shard_map/stack | solution.py:599
  15.8 4.6 %collective-permute-start.3 = (bf16[4,48,256]{2,1,0:T(8,128)(2,1)S(1)}, bf16[4,48,256]{2,1,0:T(8,128)(2,1)S(1)}, u32[]{:S(2)}, u32[]{:S(2)}) collective-permute-start(bf16[4,48,256]{2,1,0:T(8,128)(2,1)S(1)} %pad_maximum_fusion.near_ref), channel_id=1, source_target_pairs={{0,32},{32,0},{64,96},{96,64},{128,160},{160,128},{192,224},{224,1... | collective-permute-start | bytes 294920 | tf_op jit(solution)/shard_map/ppermute | solution.py:608
  20.4 3.1 %all-to-all-done = bf16[32,4,384]{2,1,0:T(4,128)(2,1)S(1)} async-done(((bf16[32,4,384]{2,1,0:T(4,128)(2,1)}), bf16[32,4,384]{2,1,0:T(4,128)(2,1)S(1)}, u32[]{:S(2)}, u32[]{:S(2)}) %all-to-all-start) | async-done | bytes 98336 | tf_op jit(solution)/shard_map/all_to_all | solution.py:609
  23.5 5.9 %shard_map.163 = (f32[32,4,768]{2,1,0:T(4,128)S(1)}, f32[16,1664]{1,0:T(8,128)S(1)}, bf16[816,384]{1,0:T(8,128)(2,1)S(1)}, f32[2048,256]{1,0:T(8,128)S(1)}) custom-call(bf16[128,384]{1,0:T(8,128)(2,1)S(1)} %reshape.29.qs_ref, bf16[336,384]{1,0:T(8,128)(2,1)} %bitcast.19, f32[12,128]{1,0:T(8,128)} %qf_hbm.3, s32[1,128]{1,0:T(1,128)} %bitcast.30, ...), custom_call_target="tpu_custom_call" | custom-call | flops 134217728 | bytes 8388608 | tf_op jit(solution)/shard_map/pallas_call | solution.py:379
  29.4 0.0 collective-permute-done.3.far_ref
  29.4 0.0 copy-start
  29.4 7.4 %shard_map.164 = (bf16[1024,128]{1,0:T(8,128)(2,1)S(1)}, bf16[1024,128]{1,0:T(8,128)(2,1)S(1)}) custom-call(bf16[4,48,256]{2,1,0:T(8,128)(2,1)S(1)} %pad_maximum_fusion.near_ref, bf16[4,48,256]{2,1,0:T(8,128)(2,1)S(1)} %collective-permute-done.3.far_ref, bf16[816,384]{1,0:T(8,128)(2,1)S(1)} %get-tuple-element.15.wk_ref, ...), custom_call_target="tpu_custom_call" | custom-call | flops 1476395008 | bytes 8388608 | tf_op jit(solution)/shard_map/pallas_call | solution.py:410
  36.8 0.2 collective-permute-start.4
  37.0 1.4 %collective-permute-done.4.come_ref = bf16[1024,128]{1,0:T(8,128)(2,1)S(1)} collective-permute-done((bf16[1024,128]{1,0:T(8,128)(2,1)S(1)}, bf16[1024,128]{1,0:T(8,128)(2,1)S(1)}, u32[]{:S(2)}, u32[]{:S(2)}) %collective-permute-start.4) | collective-permute-done | bytes 262176 | tf_op jit(solution)/shard_map/ppermute | solution.py:623
  38.4 1.2 %shard_map.165 = bf16[1024,128]{1,0:T(8,128)(2,1)} custom-call(bf16[1024,128]{1,0:T(8,128)(2,1)S(1)} %get-tuple-element.19.own_ref, bf16[1024,128]{1,0:T(8,128)(2,1)S(1)} %collective-permute-done.4.come_ref), custom_call_target="tpu_custom_call" | custom-call | tf_op jit(solution)/shard_map/pallas_call | solution.py:438
  39.6 4.3 %all-to-all-start.1 = ((bf16[16,64,128]{2,1,0:T(8,128)(2,1)}), bf16[16,64,128]{2,1,0:T(8,128)(2,1)S(1)}, u32[]{:S(2)}, u32[]{:S(2)}) async-start(bf16[16,64,128]{2,1,0:T(8,128)(2,1)} %bitcast.14.after), calls=%async_computation.1 | async-start | bytes 524288 | tf_op jit(solution)/shard_map/all_to_all | solution.py:626
  43.9 0.0 copy-done
  43.9 0.6 reshape.37.ob_hbm
  44.5 1.6 %shard_map.166 = (f32[8,128]{1,0:T(8,128)S(1)}, bf16[128,512]{1,0:T(8,128)(2,1)S(1)}, f32[1,384]{1,0:T(1,128)S(1)}, bf16[2112,384]{1,0:T(8,128)(2,1)S(1)}) custom-call(bf16[16,64,128]{2,1,0:T(8,128)(2,1)} %bitcast.14.after, f32[12,128]{1,0:T(8,128)} %qf_hbm.3, bf16[128,512]{1,0:T(8,128)(2,1)} %constant.5.clone.em_hbm, f32[1,384]{1,0:T(1,128)} %reshape.37.ob_hbm, ...), custom_call_target="tpu_custom_call" | custom-call | bytes 4194304 | tf_op jit(solution)/shard_map/pallas_call | solution.py:546
  46.1 9.0 %all-to-all-done.1.x_ref = bf16[16,64,128]{2,1,0:T(8,128)(2,1)S(1)} async-done(((bf16[16,64,128]{2,1,0:T(8,128)(2,1)}), bf16[16,64,128]{2,1,0:T(8,128)(2,1)S(1)}, u32[]{:S(2)}, u32[]{:S(2)}) %all-to-all-start.1) | async-done | bytes 262176 | tf_op jit(solution)/shard_map/all_to_all | solution.py:626
  55.1 1.9 %shard_map.167 = bf16[4,384]{1,0:T(4,128)(2,1)} custom-call(bf16[16,64,128]{2,1,0:T(8,128)(2,1)S(1)} %all-to-all-done.1.x_ref, f32[8,128]{1,0:T(8,128)S(1)} %get-tuple-element.21.fr_ref, bf16[128,512]{1,0:T(8,128)(2,1)S(1)} %get-tuple-element.22.em_ref, f32[1,384]{1,0:T(1,128)S(1)} %get-tuple-element.23.ob_ref, bf16[2112,384]{1,0:T(8,128)(2,1)S(1)} %get-tuple-element.24.ow_ref), custom_call_target="tpu_custom_call" | custom-call | tf_op jit(solution)/shard_map/pallas_call | solution.py:563
  (1 shorter events, 0.0 us)
Async XLA Ops:
  0.0 15.0 %collective-permute-start = (bf16[48,256]{1,0:T(8,128)(2,1)}, bf16[48,256]{1,0:T(8,128)(2,1)S(1)}, u32[]{:S(2)}, u32[]{:S(2)}) collective-permute-start(bf16[48,256]{1,0:T(8,128)(2,1)} %bitcast.20), channel_id=1, source_target_pairs={{64,0},{96,32},{128,64},{160,96},{192,128},{224,160},{0,192},{32,2... | collective-permute-start | bytes 73736 | tf_op jit(solution)/shard_map/ppermute | solution.py:602
  2.3 12.8 %collective-permute-start.1 = (bf16[48,256]{1,0:T(8,128)(2,1)}, bf16[48,256]{1,0:T(8,128)(2,1)S(1)}, u32[]{:S(2)}, u32[]{:S(2)}) collective-permute-start(bf16[48,256]{1,0:T(8,128)(2,1)} %bitcast.21), channel_id=1, source_target_pairs={{128,0},{160,32},{192,64},{224,96},{0,128},{32,160},{64,192},{96,2... | collective-permute-start | bytes 73736 | tf_op jit(solution)/shard_map/ppermute | solution.py:602
  3.0 12.1 %collective-permute-start.2 = (bf16[48,256]{1,0:T(8,128)(2,1)}, bf16[48,256]{1,0:T(8,128)(2,1)S(1)}, u32[]{:S(2)}, u32[]{:S(2)}) collective-permute-start(bf16[48,256]{1,0:T(8,128)(2,1)} %bitcast.22), channel_id=1, source_target_pairs={{192,0},{224,32},{0,64},{32,96},{64,128},{96,160},{128,192},{160,2... | collective-permute-start | bytes 73736 | tf_op jit(solution)/shard_map/ppermute | solution.py:602
  6.1 17.4 %all-to-all-start = ((bf16[32,4,384]{2,1,0:T(4,128)(2,1)}), bf16[32,4,384]{2,1,0:T(4,128)(2,1)S(1)}, u32[]{:S(2)}, u32[]{:S(2)}) async-start(bf16[32,4,384]{2,1,0:T(4,128)(2,1)} %broadcast_in_dim.2), calls=%async_computation | async-start | bytes 196608 | tf_op jit(solution)/shard_map/all_to_all | solution.py:609
  15.8 13.6 %collective-permute-start.3 = (bf16[4,48,256]{2,1,0:T(8,128)(2,1)S(1)}, bf16[4,48,256]{2,1,0:T(8,128)(2,1)S(1)}, u32[]{:S(2)}, u32[]{:S(2)}) collective-permute-start(bf16[4,48,256]{2,1,0:T(8,128)(2,1)S(1)} %pad_maximum_fusion.near_ref), channel_id=1, source_target_pairs={{0,32},{32,0},{64,96},{96,64},{128,160},{160,128},{192,224},{224,1... | collective-permute-start | bytes 294920 | tf_op jit(solution)/shard_map/ppermute | solution.py:608
  29.4 14.5 %copy-start = (f32[384]{0:T(512)S(1)}, f32[384]{0:T(512)}, u32[]{:S(2)}) copy-start(f32[384]{0:T(512)} %param.31) | copy-start | bytes 4612
  36.8 1.6 %collective-permute-start.4 = (bf16[1024,128]{1,0:T(8,128)(2,1)S(1)}, bf16[1024,128]{1,0:T(8,128)(2,1)S(1)}, u32[]{:S(2)}, u32[]{:S(2)}) collective-permute-start(bf16[1024,128]{1,0:T(8,128)(2,1)S(1)} %get-tuple-element.20), channel_id=1, source_target_pairs={{0,1},{1,0},{2,3},{3,2},{4,5},{5,4},{6,7},{7,6},{8,9},{9,8},{10,11... | collective-permute-start | bytes 786440 | tf_op jit(solution)/shard_map/ppermute | solution.py:623
  39.6 15.5 %all-to-all-start.1 = ((bf16[16,64,128]{2,1,0:T(8,128)(2,1)}), bf16[16,64,128]{2,1,0:T(8,128)(2,1)S(1)}, u32[]{:S(2)}, u32[]{:S(2)}) async-start(bf16[16,64,128]{2,1,0:T(8,128)(2,1)} %bitcast.14.after), calls=%async_computation.1 | async-start | bytes 524288 | tf_op jit(solution)/shard_map/all_to_all | solution.py:626

commit v5 on v4

--- a/solution.py
+++ b/solution.py
@@ -97,15 +97,14 @@
 
 
 def shadow_kernel(
-    qs_ref, wq_hbm, qf_hbm, qc_hbm, raw_hbm, cb_hbm, dm_hbm, kf_hbm, kc_hbm, km_hbm, pw_hbm, wk_hbm,
-    pair_ref, feat_ref, mask_ref, wk_ref, bias_ref,
-    wq_v, qf_v, qc_v, raw_v, cb_v, dm_v, kf_v, kc_v, km_v, pw_v,
-    qpt_s, nq_s, qft_s, pw_s, feat_s, pair_v, sem, pair_sem,
+    raw_hbm, cb_hbm, dm_hbm, kf_hbm, kc_hbm, km_hbm, qf_hbm, qc_hbm, pw_hbm, wk_hbm, wq_hbm,
+    pair_ref, mask_ref, wk_ref, wq_ref, bias_ref,
+    raw_v, cb_v, dm_v, kf_v, kc_v, km_v, qf_v, qc_v, pw_v, pw_s, pair_v, sem, pair_sem,
 ):
     moves = [
-        (pw_hbm, pw_v), (wq_hbm, wq_v), (qf_hbm, qf_v), (qc_hbm, qc_v), (raw_hbm, raw_v),
-        (cb_hbm, cb_v), (dm_hbm, dm_v), (kf_hbm, kf_v), (kc_hbm, kc_v), (km_hbm, km_v),
-        (wk_hbm, wk_ref),
+        (pw_hbm, pw_v), (raw_hbm, raw_v), (cb_hbm, cb_v), (dm_hbm, dm_v), (kf_hbm, kf_v),
+        (kc_hbm, kc_v), (km_hbm, km_v), (qf_hbm, qf_v), (qc_hbm, qc_v), (wk_hbm, wk_ref),
+        (wq_hbm, wq_ref),
     ]
     small = [pltpu.make_async_copy(*move, sem.at[i]) for i, move in enumerate(moves)]
     core = lax.rem(lax.axis_index("col"), 2)
@@ -130,18 +129,7 @@
         if i == len(copies) // 2:
             for other in small[1:]:
                 other.wait()
-            prepare_queries(
-                qs_ref, wq_v, qf_v, qc_v, raw_v, cb_v, dm_v, feat_s, mask_ref, qpt_s, nq_s, qft_s
-            )
-            count = feat_ref.shape[0] // 2
-            for group in range(2 * count):
-                half = core if group % 2 == 0 else 1 - core
-                feat_ref[(1 - half) * count + group // 2] = feat_s[
-                    SHARE * group : SHARE * group + SHARE, :
-                ]
-            mask_ref[0:H, KD + GL : KD + GL + 256] = kf_v[...]
-            mask_ref[H : H + 1, KD + GL : KD + GL + 256] = kc_v[...].astype(F32)
-            mask_ref[H + 1 : H + 2, KD + GL : KD + GL + 256] = km_v[...].astype(F32)
+            prepare_masks(raw_v, cb_v, dm_v, kf_v, kc_v, km_v, qf_v, qc_v, mask_ref)
         copy.wait()
         for q in range(SB):
             row = (SB * i + q) * HP
@@ -151,6 +139,24 @@
                 NT,
                 preferred_element_type=F32,
             )
+
+
+def prepare_masks(raw_v, cb_v, dm_v, kf_v, kc_v, km_v, qf_v, qc_v, mask_ref):
+    mask_ref[:, 0 : KD + GL] = dm_v[...]
+    lane = lax.broadcasted_iota(jnp.int32, (HP, 128), 1)
+    tail = dm_v[:, 640:768]
+    for t, part in enumerate(split3(column_of(cb_v[...], HP, 1))):
+        tail = jnp.where((lane >= 80 + 8 * t) & (lane < 88 + 8 * t), part, tail)
+    mask_ref[:, 640:768] = tail
+    at = KD + GL
+    mask_ref[0:H, at : at + 256] = kf_v[...]
+    mask_ref[H : H + 1, at : at + 256] = kc_v[...].astype(F32)
+    mask_ref[H + 1 : H + 2, at : at + 256] = km_v[...].astype(F32)
+    gamma = column_of(gamma_of(raw_v[...]), HP, 1)
+    mask_ref[:, at + 256 : at + 384] = jnp.broadcast_to(gamma, (HP, 128))
+    mask_ref[0:H, at + 384 : at + 512] = qf_v[...]
+    mask_ref[H : H + 1, at + 384 : at + 512] = qc_v[...].astype(F32)
+    mask_ref[H + 1 : H + 2, at + 384 : at + 384 + H] = raw_v[...]
 
 
 def prepare_keys(info, gamma16, kt_ref, vt_ref, kpt_s, nk_s):
@@ -181,14 +187,10 @@
     vt_ref[480:512] = jnp.zeros((32, vt_ref.shape[1]), BF16)
 
 
-def prepare_queries(
-    qs_ref, wq_ref, qf_ref, qc_ref, raw_ref, cb_ref, dm_ref, qf_s, m_s, qpt_s, nq_s, qft_s
-):
-    gamma = gamma_of(raw_ref[...])
-    gamma16 = column_of(gamma, HP, 1)
-    gamma48 = column_of(gamma, H * PQ, PQ)
+def prepare_queries(qs_ref, wq_ref, info, gamma16, qpt_s, nq_s, qft_s, qf_s):
+    gamma48 = column_of(gamma_of(info[H + 1 : H + 2, 0:H]), H * PQ, PQ)
     put(qpt_s, 0, lax.dot_general(wq_ref[...], qs_ref[...], NT, preferred_element_type=F32))
-    frames = qf_ref[...]
+    frames = info[0:H]
     qft_s[0:192] = take(qpt_s, 0, 192, 1).astype(BF16).astype(F32) * (1.0 / math.sqrt(C))
     points = rotate([take(qpt_s, 192 + x, 48, 3) for x in range(3)], frames)
     for x in range(3):
@@ -204,22 +206,15 @@
         qft_s[672 + HP * t : 688 + HP * t] = part
     shape = (48, qft_s.shape[1])
     index = lax.broadcasted_iota(jnp.int32, shape, 0)
-    same = (jnp.bitwise_and(index, 7) == qc_ref[...]) & (index < 24)
+    same = (jnp.bitwise_and(index, 7).astype(F32) == info[H : H + 1]) & (index < 24)
     qft_s[720:768] = (same | (index == 24)).astype(F32)
     qf_s[...] = qft_s[...].T
 
-    m_s[:, 0 : KD + GL] = dm_ref[...]
-    m_s[:, KD + GL + 256 :] = jnp.broadcast_to(gamma16, (HP, 128))
-    lane = lax.broadcasted_iota(jnp.int32, (HP, 128), 1)
-    tail = dm_ref[:, 640:768]
-    for t, part in enumerate(split3(column_of(cb_ref[...], HP, 1))):
-        tail = jnp.where((lane >= 80 + 8 * t) & (lane < 88 + 8 * t), part, tail)
-    m_s[:, 640:768] = tail
-
 
 def attend_kernel(
-    near_ref, far_ref, wk_ref, feat_ref, mask_ref, bias_ref, pair_ref,
-    send_ref, own_ref, kpt_s, nk_s, kt_s, vt_s, v_s, w_s, z_s, o_s, ks_s, pair_v, pair_sem,
+    near_ref, far_ref, qs_ref, wk_ref, mask_ref, wq_ref, bias_ref, pair_ref,
+    send_ref, own_ref, kpt_s, nk_s, kt_s, vt_s, v_s, w_s, z_s, o_s, ks_s,
+    qpt_s, nq_s, qft_s, qf_s, feat_s, pair_v, pair_sem,
 ):
     core = lax.rem(lax.axis_index("col"), 2)
     groups = QB // SHARE
@@ -243,6 +238,12 @@
     info = mask_ref[:, KD + GL : KD + GL + 256]
     gamma16 = mask_ref[:, KD + GL + 256 : KD + GL + 257]
     prepare_keys(info, gamma16, kt_s, vt_s, kpt_s, nk_s)
+    info = mask_ref[:, KD + GL + 384 : KD + GL + 512]
+    prepare_queries(qs_ref, wq_ref, info, gamma16, qpt_s, nq_s, qft_s, qf_s)
+    half_groups = feat_s.shape[0] // 2
+    for group in range(2 * half_groups):
+        half = core if group % 2 == 0 else 1 - core
+        feat_s[(1 - half) * half_groups + group // 2] = qf_s[SHARE * group : SHARE * group + SHARE]
     v_s[...] = vt_s[...].T
     rows = QB * HP
     lane = lax.broadcasted_iota(jnp.int32, (rows, 128), 1)
@@ -255,7 +256,7 @@
         for step in range(steps):
             start = (half * steps + step) * rows
             group = start // (SHARE * HP)
-            mine = feat_ref[group : group + groups].reshape(QB, 1, KD)
+            mine = feat_s[group : group + groups].reshape(QB, 1, KD)
             spread = (mine * mask_ref[:, 0:KD][None]).reshape(rows, KD).astype(BF16)
             logits = jnp.dot(spread, kt_s[...], preferred_element_type=F32)
             bias = bias_ref[start : start + rows, :]
@@ -318,11 +319,11 @@
     return ((head == value) & (lane < 96)).astype(BF16)
 
 
-def pair_kernel(own_ref, come_ref, out_ref, a_s, b_s):
-    rows = own_ref.shape[0]
+def merge(sources, held):
+    rows = sources[0].shape[0]
     queries = rows // HP
-    a_s[...] = own_ref[...].astype(F32)
-    b_s[...] = come_ref[...].astype(F32)
+    for source, ref in zip(sources, held, strict=True):
+        ref[...] = source[...].astype(F32)
     lane = lax.broadcasted_iota(jnp.int32, (queries, 128), 1)
     stat = (lane >= 96) & (lane < 108)
 
@@ -330,33 +331,46 @@
         last = ref[pl.ds(HP - 1, queries, stride=HP), :]
         return jnp.where(stat, last + pltpu.roll(last, 128 - H, 1), 0.0)
 
-    first, second = level(a_s), level(b_s)
-    top = jnp.maximum(first, second)
-    near, far = jnp.exp(first - top), jnp.exp(second - top)
-    both = near + far
-    share = jnp.where(stat, far / both, 0.0)
-    hi, lo = split(top + jnp.log(both))
-    pieces = [piece.astype(BF16) for piece in split(share)]
-    mixed = []
-    for r in range(4):
-        columns = lane_columns(r)
-        weight = sum(jnp.dot(piece, columns, preferred_element_type=F32) for piece in pieces)
-        one = a_s[pl.ds(H + r, queries, stride=HP), :]
-        two = b_s[pl.ds(H + r, queries, stride=HP), :]
-        mixed.append(one + weight * (two - one))
-    mixed[3] = jnp.where(
-        stat, hi, jnp.where((lane >= 108) & (lane < 120), pltpu.roll(lo, H, 1), mixed[3])
-    )
+    levels = [level(ref) for ref in held]
+    top = functools.reduce(jnp.maximum, levels)
+    shares = [jnp.exp(one - top) for one in levels]
+    total = sum(shares)
+    hi, lo = split(top + jnp.log(total))
+    shares = [jnp.where(stat, one / total, 0.0) for one in shares]
     own = (
         lax.broadcasted_iota(jnp.int32, (HP, 128), 0) + 96
         == lax.broadcasted_iota(jnp.int32, (HP, 128), 1)
     ).astype(F32)
-    column = jnp.sum((share[:, None, :] * own[None]).reshape(rows, 128), 1, keepdims=True)
-    one = a_s[...]
-    a_s[...] = one + column * (b_s[...] - one)
+    mixed = [held[0][pl.ds(H + r, queries, stride=HP), :] for r in range(4)]
+    base = held[0][...]
+    result = base
+    for share, ref in zip(shares[1:], held[1:], strict=True):
+        pieces = [piece.astype(BF16) for piece in split(share)]
+        for r in range(4):
+            columns = lane_columns(r)
+            weight = sum(jnp.dot(piece, columns, preferred_element_type=F32) for piece in pieces)
+            near = held[0][pl.ds(H + r, queries, stride=HP), :]
+            far = ref[pl.ds(H + r, queries, stride=HP), :]
+            mixed[r] = mixed[r] + weight * (far - near)
+        column = jnp.sum((share[:, None, :] * own[None]).reshape(rows, 128), 1, keepdims=True)
+        result = result + column * (ref[...] - base)
+    mixed[3] = jnp.where(
+        stat, hi, jnp.where((lane >= 108) & (lane < 120), pltpu.roll(lo, H, 1), mixed[3])
+    )
+    held[0][...] = result
     for r in range(4):
-        a_s[pl.ds(H + r, queries, stride=HP), :] = mixed[r]
-    out_ref[...] = a_s[...].astype(BF16)
+        held[0][pl.ds(H + r, queries, stride=HP), :] = mixed[r]
+
+
+def join_kernel(count, first, *refs):
+    sources, parts, held = refs[:count], refs[count:-count], refs[-count:]
+    rows = sources[0].shape[0]
+    merge(sources, held)
+    place = first(lax.axis_index("col"))
+    size = rows // len(parts)
+    for k, part in enumerate(parts):
+        start = pl.multiple_of(lax.rem(place + k, len(parts)) * size, size)
+        part[...] = held[0][pl.ds(start, size), :].astype(BF16)
 
 
 def inside(x):
@@ -373,26 +387,22 @@
 HBM = pl.BlockSpec(memory_space=pltpu.HBM)
 
 
-def shadow(qs, others, pair):
+def shadow(others, pair):
     queries, keys = pair.shape[:2]
     pair = pair.reshape(queries // SHARE // 2, 2, SHARE, keys, CZ)
     return pl.pallas_call(
         shadow_kernel,
         out_shape=(
-            pltpu.VMEM((queries // SHARE, SHARE, KD), F32),
-            pltpu.VMEM((HP, KD + GL + keys + 128), F32),
+            pltpu.VMEM((HP, KD + GL + keys + 256), F32),
+            pltpu.VMEM(others[9].shape, BF16),
             pltpu.VMEM(others[10].shape, BF16),
             pltpu.VMEM((queries * HP, keys), F32),
         ),
-        in_specs=[VMEM] + [HBM] * 12,
+        in_specs=[HBM] * 12,
         out_specs=(VMEM,) * 4,
-        scratch_shapes=[pltpu.VMEM(x.shape, x.dtype) for x in others[:10]]
+        scratch_shapes=[pltpu.VMEM(x.shape, x.dtype) for x in others[:9]]
         + [
-            pltpu.VMEM((queries // 128, 384, 128), F32),
-            pltpu.VMEM((HP, queries), F32),
-            pltpu.VMEM((KD, queries), F32),
             pltpu.VMEM((HP, CZ), F32),
-            pltpu.VMEM((queries, KD), F32),
             pltpu.VMEM((queries // SB, SB // SHARE, SHARE, keys, CZ), BF16),
             pltpu.SemaphoreType.DMA((11,)),
             pltpu.SemaphoreType.DMA((queries // SB,)),
@@ -401,16 +411,16 @@
             flops=2 * queries * keys * CZ * HP, bytes_accessed=pair.size * 2, transcendentals=0
         ),
         compiler_params=pltpu.CompilerParams(vmem_limit_bytes=16 * 2**20),
-    )(qs, *[outside(x) for x in (*others, pair)])
-
-
-def attend(near, far, held, pair):
+    )(*[outside(x) for x in (*others, pair)])
+
+
+def attend(came, held, pair):
     queries, keys = pair.shape[:2]
     pair = pair.reshape(queries // SHARE // 2, 2, SHARE, keys, CZ)
     return pl.pallas_call(
         attend_kernel,
         out_shape=(jax.ShapeDtypeStruct((queries * HP // 2, CZ), BF16),) * 2,
-        in_specs=[VMEM] * (len(held) + 2) + [HBM],
+        in_specs=[VMEM] * (len(held) + 3) + [HBM],
         out_specs=(VMEM,) * 2,
         scratch_shapes=[
             pltpu.VMEM((keys // 128, 896, 128), F32),
@@ -422,6 +432,11 @@
             pltpu.VMEM((queries, GL), F32),
             pltpu.VMEM((queries * HP, CZ), F32),
             pltpu.VMEM((384, keys), BF16),
+            pltpu.VMEM((queries // 128, 384, 128), F32),
+            pltpu.VMEM((HP, queries), F32),
+            pltpu.VMEM((KD, queries), F32),
+            pltpu.VMEM((queries, KD), F32),
+            pltpu.VMEM((queries // SHARE, SHARE, KD), F32),
             pltpu.VMEM((queries // QB, QB // SHARE, SHARE, keys, CZ), BF16),
             pltpu.SemaphoreType.DMA((queries // QB,)),
         ],
@@ -431,22 +446,34 @@
             transcendentals=queries * HP * keys,
         ),
         compiler_params=pltpu.CompilerParams(vmem_limit_bytes=20 * 2**20),
-    )(near, far, *[inside(x) for x in held], outside(pair))
-
-
-def join(own, come):
+    )(*came, *[inside(x) for x in held], outside(pair))
+
+
+def join(sources, first, parts):
+    rows, columns = sources[0].shape
     return pl.pallas_call(
-        pair_kernel,
-        out_shape=jax.ShapeDtypeStruct(own.shape, BF16),
-        in_specs=[VMEM, VMEM],
-        out_specs=VMEM,
-        scratch_shapes=[pltpu.VMEM(own.shape, F32)] * 2,
+        functools.partial(join_kernel, len(sources), first),
+        out_shape=(jax.ShapeDtypeStruct((rows // parts, columns), BF16),) * parts,
+        in_specs=[VMEM] * len(sources),
+        out_specs=(VMEM,) * parts,
+        scratch_shapes=[pltpu.VMEM((rows, columns), F32)] * len(sources),
         compiler_params=pltpu.CompilerParams(vmem_limit_bytes=8 * 2**20),
-    )(own, come)
-
-
-def fetch_kernel(after, qf_hbm, em_hbm, ob_hbm, ow_hbm, fr_ref, em_ref, ob_ref, ow_ref, qf_v, sem):
-    moves = [(qf_hbm, qf_v), (em_hbm, em_ref), (ob_hbm, ob_ref), (ow_hbm, ow_ref)]
+    )(*sources)
+
+
+def exchange(parts, width, apart, count):
+    def to(i, k):
+        place = (i // apart) % width
+        return i + ((place + k) % width - place) * apart
+
+    return [parts[0]] + [
+        lax.ppermute(parts[k], "col", [(i, to(i, k)) for i in range(count)])
+        for k in range(1, width)
+    ]
+
+
+def fetch_kernel(after, qf_hbm, ob_hbm, ow_hbm, fr_ref, ob_ref, ow_ref, qf_v, sem):
+    moves = [(qf_hbm, qf_v), (ob_hbm, ob_ref), (ow_hbm, ow_ref)]
     copies = [pltpu.make_async_copy(*move, sem.at[i]) for i, move in enumerate(moves)]
     for copy in copies:
         copy.start()
@@ -464,44 +491,14 @@
         copy.wait()
 
 
-def finish_kernel(x_ref, fr_ref, em_ref, ob_ref, ow_ref, out_ref, x_s, p_s, g_s, w_s, f_s):
+def finish_kernel(sources, *refs):
+    parts, refs = refs[:sources], refs[sources:]
+    fr_ref, ob_ref, ow_ref, out_ref, f_s, *held = refs
     share = out_ref.shape[0]
-    sources = x_ref.shape[0]
-    lane = lax.broadcasted_iota(jnp.int32, (sources, 128), 1)
-    stat = (lane >= 96) & (lane < 108)
-    for q in range(share):
-        block = x_ref[:, HP * q : HP * q + HP, :].reshape(sources * HP, 128)
-        x_s[...] = block.astype(F32)
-        rows = [x_s[pl.ds(H + r, sources, stride=HP), :] for r in range(4)]
-        level = jnp.where(stat, rows[3] + pltpu.roll(rows[3], 128 - H, 1), 0.0)
-        part = jnp.exp(level - jnp.max(level, 0, keepdims=True))
-        part = jnp.where(stat, part / jnp.sum(part, 0, keepdims=True), 0.0)
-        hi, lo = split(part)
-        spread = jnp.dot(hi.astype(BF16), em_ref[...], preferred_element_type=F32) + jnp.dot(
-            lo.astype(BF16), em_ref[...], preferred_element_type=F32
-        )
-        for r in range(4):
-            g_s[pl.ds(8 * r + q, 1), :] = jnp.sum(
-                spread[:, 128 * r : 128 * r + 128] * rows[r], 0, keepdims=True
-            )
-        w_s[...] = jnp.zeros_like(w_s)
-        w_s[0:sources] = part
-        turned = w_s[...].T[96:112]
-        source = lax.broadcasted_iota(jnp.int32, (128, sources * HP), 0)
-        column = lax.broadcasted_iota(jnp.int32, (128, sources * HP), 1)
-        repeat = (lax.shift_right_logical(column, 4) == source).astype(BF16)
-        own = lax.broadcasted_iota(jnp.int32, (HP, sources * HP), 0) == jnp.bitwise_and(
-            lax.broadcasted_iota(jnp.int32, (HP, sources * HP), 1), HP - 1
-        )
-        paired = jnp.zeros((HP, 128), F32)
-        for piece in split(turned):
-            wide = jnp.dot(piece.astype(BF16), repeat, preferred_element_type=F32)
-            wide = jnp.where(own, wide, 0.0).astype(BF16)
-            paired += jnp.dot(wide, block, preferred_element_type=F32)
-        p_s[HP * q : HP * q + HP] = paired
-
+    merge(parts, held)
+    sums = held[0]
     frame = [fr_ref[0:share, j : j + 1] for j in range(12)]
-    g = [g_s[8 * r : 8 * r + share, :] for r in range(4)]
+    g = [sums[pl.ds(H + r, share, stride=HP), :] for r in range(4)]
     moved = [g[x] - frame[9 + x] for x in range(3)]
     local = [
         frame[x] * moved[0] + frame[3 + x] * moved[1] + frame[6 + x] * moved[2] for x in range(3)
@@ -532,48 +529,41 @@
         total += add(f_s[:, 512 + 128 * r : 544 + 128 * r], 32 * r, 32 * r + 32)
     total += add(g[3][:, 0:96], 96, 192)
     for h in range(H):
-        value = p_s[pl.ds(h, share, stride=HP), :]
+        value = sums[pl.ds(h, share, stride=HP), :]
         total += add(value, 576 + CZ * h, 576 + CZ * h + CZ)
     out_ref[...] = total.astype(BF16)
 
 
 def fetch(after, qf, out_weight, out_bias):
-    expand = np.zeros((128, GL), np.float32)
-    for index, head in enumerate(lane_heads()[0]):
-        if head >= 0:
-            expand[96 + head, index] = 1.0
-    others = [qf, jnp.asarray(expand, BF16), out_bias.reshape(1, -1), out_weight]
+    others = [qf, out_bias.reshape(1, -1), out_weight]
     return pl.pallas_call(
         fetch_kernel,
         out_shape=(
             pltpu.VMEM((8, 128), F32),
             *[pltpu.VMEM(x.shape, x.dtype) for x in others[1:]],
         ),
-        in_specs=[pl.BlockSpec(memory_space=pl.ANY)] + [HBM] * 4,
-        out_specs=(VMEM,) * 4,
-        scratch_shapes=[pltpu.VMEM(qf.shape, F32), pltpu.SemaphoreType.DMA((4,))],
+        in_specs=[pl.BlockSpec(memory_space=pl.ANY)] + [HBM] * 3,
+        out_specs=(VMEM,) * 3,
+        scratch_shapes=[pltpu.VMEM(qf.shape, F32), pltpu.SemaphoreType.DMA((3,))],
         cost_estimate=pl.CostEstimate(flops=0, bytes_accessed=4 * 2**20, transcendentals=0),
         compiler_params=pltpu.CompilerParams(vmem_limit_bytes=4 * 2**20),
     )(after, *[outside(x) for x in others])
 
 
 def finish(parts, others, columns):
-    share = parts.shape[1] // HP
-    sources = parts.shape[0]
+    share = parts[0].shape[0] // HP
+    sources = len(parts)
     return pl.pallas_call(
-        finish_kernel,
+        functools.partial(finish_kernel, sources),
         out_shape=jax.ShapeDtypeStruct((share, columns), BF16),
-        in_specs=[VMEM] * 5,
+        in_specs=[VMEM] * (sources + 3),
         out_specs=VMEM,
         scratch_shapes=[
-            pltpu.VMEM((sources * HP, 128), F32),
-            pltpu.VMEM((share * HP, 128), F32),
-            pltpu.VMEM((32, 128), F32),
-            pltpu.VMEM((128, 128), F32),
             pltpu.VMEM((share, 896), F32),
+            *[pltpu.VMEM(parts[0].shape, F32)] * sources,
         ],
         compiler_params=pltpu.CompilerParams(vmem_limit_bytes=4 * 2**20),
-    )(parts, *[inside(x) for x in others])
+    )(*parts, *[inside(x) for x in others])
 
 
 def body(
@@ -610,21 +600,22 @@
         jnp.broadcast_to(query_single[None], (cols, *query_single.shape)), "col", 0, 0, tiled=True
     ).reshape(-1, query_single.shape[1])
     heads = (lane_heads()[1][None, :] == np.arange(HP)[:, None]).astype(np.float32)
-    feats, mask, wk, *held = shadow(
-        queries,
+    mask, wk, wq, bias = shadow(
         [
-            w_query.T, query_frames, query_chain.reshape(1, -1), point_raw.reshape(1, -1),
-            chain_bias.reshape(1, -1), jnp.asarray(np.concatenate([depth_mask(), heads], 1)),
-            key_frames, key_chain.reshape(1, -1), key_mask.reshape(1, -1), pair_weight.T, w_key.T,
+            point_raw.reshape(1, -1), chain_bias.reshape(1, -1),
+            jnp.asarray(np.concatenate([depth_mask(), heads], 1)),
+            key_frames, key_chain.reshape(1, -1), key_mask.reshape(1, -1), query_frames,
+            query_chain.reshape(1, -1), pair_weight.T, w_key.T, w_query.T,
         ],
         pair,
     )
-    send, own = attend(near, far, [wk, feats, mask, *held], pair)
+    send, own = attend([near, far, queries], [wk, mask, wq, bias], pair)
     come = lax.ppermute(send, "col", [(i, i ^ 1) for i in range(cols)])
-    sums = join(own, come).reshape(cols // 2, -1, CZ)
-    groups = [list(range(core, cols, 2)) for core in range(2)]
-    parts = lax.all_to_all(sums, "col", 0, 0, axis_index_groups=groups, tiled=True)
-    others = fetch(sums, query_frames, out_weight, out_bias)
+    sums = join([own, come], lambda col: lax.div(col, 8), 4)
+    sums = exchange(sums, 4, 8, cols)
+    others = fetch(sums[0], query_frames, out_weight, out_bias)
+    sums = join(sums, lambda col: lax.rem(lax.div(col, 2), 4), 4)
+    parts = exchange(sums, 4, 2, cols)
     return finish(parts, others, out_weight.shape[1])
 
 

time: 57.5 us -> 55.3 us (0.962)
  waiting for transfers between devices: 13.5 us -> 5.64 us
  starting transfers between devices: 22.8 us -> 29.9 us
  Pallas kernels: 17.9 us -> 16.6 us
    ppermute x0 -> x6, starting transfers between devices: none -> 11.6 us  [exchange(): lax.ppermute(parts[k], 'col', [(i, to(i, k)) for i in range(count)])]
    all_to_all x1 -> x0, waiting for transfers between devices: 9.03 us -> none  [body(): lax.all_to_all(sums, 'col', 0, 0, axis_index_groups=groups, tiled=True)]
    all_to_all x1 -> x0, starting transfers between devices: 4.34 us -> none  [body(): lax.all_to_all(sums, 'col', 0, 0, axis_index_groups=groups, tiled=True)]
    ppermute x0 -> x6, waiting for transfers between devices: none -> 4.11 us  [exchange(): lax.ppermute(parts[k], 'col', [(i, to(i, k)) for i in range(count)])]
    all_to_all x1, waiting for transfers between devices: 3.07 us -> 0.01 us  [body(): lax.all_to_all(jnp.broadcast_to(query_single[None], (cols, *query_single....]
    pallas_call x3 -> x4, Pallas kernels: 9 us -> 7.67 us  [the longest x1 5.24 us: shadow(): pl.pallas_call(shadow_kernel, out_shape=(pltpu.VMEM((HP, KD + GL + keys +...]
  transfers between devices with their start and end apart: 7 -> 12, of which waited for: 3 -> 4; matrix products, arithmetic and copies ran while one was open for 5% -> 5% of each run, Pallas kernels for 13% -> 12%
where the time goes in v5:
time: 55.3 us; the launch traced here: 55.1 us
  starting transfers between devices  29.9 us (54%)
  Pallas kernels  16.6 us (30%)
  waiting for transfers between devices  5.64 us (10%)
  local copies, waits for them, and re-layouts  1.96 us (4%)
  other arithmetic  0.76 us (1%)
    ppermute x6, starting transfers between devices, exchange(): lax.ppermute(parts[k], 'col', [(i, to(i, k)) for i in range(count)])  11.6 us
    all_to_all x1, starting transfers between devices, body(): lax.all_to_all(jnp.broadcast_to(query_single[None], (cols, *query_single....  8.92 us
    pallas_call x1, Pallas kernels, attend(): pl.pallas_call(attend_kernel, out_shape=(jax.ShapeDtypeStruct((queries *...  7.5 us
    pallas_call x1, Pallas kernels, shadow(): pl.pallas_call(shadow_kernel, out_shape=(pltpu.VMEM((HP, KD + GL + keys +...  5.24 us
    ppermute x3, starting transfers between devices, body(): lax.ppermute(turned, 'row', [((i + 2 * k) % rows, i) for i in range(rows)])  4.76 us
    ppermute x1, starting transfers between devices, body(): far = lax.ppermute(near, 'row', [(i, i ^ 1) for i in range(rows)])  4.58 us
    ppermute x6, waiting for transfers between devices, exchange(): lax.ppermute(parts[k], 'col', [(i, to(i, k)) for i in range(count)])  4.11 us
    pallas_call x1, Pallas kernels, finish(): pl.pallas_call(functools.partial(finish_kernel, sources), out_shape=jax.S...  1.54 us
  transfers between devices with their start and end apart: 12, of which 4 were waited for; matrix products, arithmetic and copies ran while one was open for 5% of the time, Pallas kernels for 12%

profile of v5, /device:TPU:2, one launch (start us, length us, event | category | flops | bytes accessed | tf_op | source)
XLA Modules:
  0.0 55.1 jit_solution(16414048574431117190)
XLA Ops:
  0.0 2.3 %collective-permute-start = (bf16[48,256]{1,0:T(8,128)(2,1)}, bf16[48,256]{1,0:T(8,128)(2,1)S(1)}, u32[]{:S(2)}, u32[]{:S(2)}) collective-permute-start(bf16[48,256]{1,0:T(8,128)(2,1)} %bitcast.19), channel_id=1, source_target_pairs={{64,0},{96,32},{128,64},{160,96},{192,128},{224,160},{0,192},{32,2... | collective-permute-start | bytes 73736 | tf_op jit(solution)/shard_map/ppermute | solution.py:592
  2.3 0.7 %collective-permute-start.1 = (bf16[48,256]{1,0:T(8,128)(2,1)}, bf16[48,256]{1,0:T(8,128)(2,1)S(1)}, u32[]{:S(2)}, u32[]{:S(2)}) collective-permute-start(bf16[48,256]{1,0:T(8,128)(2,1)} %bitcast.20), channel_id=1, source_target_pairs={{128,0},{160,32},{192,64},{224,96},{0,128},{32,160},{64,192},{96,2... | collective-permute-start | bytes 73736 | tf_op jit(solution)/shard_map/ppermute | solution.py:592
  3.0 1.8 %collective-permute-start.2 = (bf16[48,256]{1,0:T(8,128)(2,1)}, bf16[48,256]{1,0:T(8,128)(2,1)S(1)}, u32[]{:S(2)}, u32[]{:S(2)}) collective-permute-start(bf16[48,256]{1,0:T(8,128)(2,1)} %bitcast.21), channel_id=1, source_target_pairs={{192,0},{224,32},{0,64},{32,96},{64,128},{96,160},{128,192},{160,2... | collective-permute-start | bytes 73736 | tf_op jit(solution)/shard_map/ppermute | solution.py:592
  4.8 1.4 %broadcast_in_dim.2 = bf16[32,4,384]{2,1,0:T(4,128)(2,1)} broadcast(bf16[4,384]{1,0:T(4,128)(2,1)} %param.16), dimensions={1,2} | broadcast | bytes 101376 | tf_op jit(solution)/shard_map/broadcast_in_dim | solution.py:600
  6.1 8.9 %all-to-all-start = ((bf16[32,4,384]{2,1,0:T(4,128)(2,1)}), bf16[32,4,384]{2,1,0:T(4,128)(2,1)S(1)}, u32[]{:S(2)}, u32[]{:S(2)}) async-start(bf16[32,4,384]{2,1,0:T(4,128)(2,1)} %broadcast_in_dim.2), calls=%async_computation | async-start | bytes 196608 | tf_op jit(solution)/shard_map/all_to_all | solution.py:599
  15.0 0.0 collective-permute-done
  15.1 0.0 collective-permute-done.1
  15.1 0.0 collective-permute-done.2
  15.1 0.8 %pad_maximum_fusion.near_ref = bf16[4,48,256]{2,1,0:T(8,128)(2,1)S(1)} fusion(bf16[1,48,256]{2,1,0:T(8,128)(2,1)S(1)} %bitcast.25, bf16[1,48,256]{2,1,0:T(8,128)(2,1)S(1)} %bitcast.24, bf16[1,48,256]{2,1,0:T(8,128)(2,1)S(1)} %bitcast.23, bf16[1,48,256]{2,1,0:T(8,128)(2,1)} %bitcast.22), kind=kLoop, calls=%fused_computation | loop fusion | flops 147456 | bytes 196608 | tf_op jit(solution)/shard_map/stack | solution.py:589
  15.8 4.6 %collective-permute-start.3 = (bf16[4,48,256]{2,1,0:T(8,128)(2,1)S(1)}, bf16[4,48,256]{2,1,0:T(8,128)(2,1)S(1)}, u32[]{:S(2)}, u32[]{:S(2)}) collective-permute-start(bf16[4,48,256]{2,1,0:T(8,128)(2,1)S(1)} %pad_maximum_fusion.near_ref), channel_id=1, source_target_pairs={{0,32},{32,0},{64,96},{96,64},{128,160},{160,128},{192,224},{224,1... | collective-permute-start | bytes 294920 | tf_op jit(solution)/shard_map/ppermute | solution.py:598
  20.4 5.2 %shard_map.154 = (f32[16,1792]{1,0:T(8,128)S(1)}, bf16[816,384]{1,0:T(8,128)(2,1)S(1)}, bf16[336,384]{1,0:T(8,128)(2,1)S(1)}, f32[2048,256]{1,0:T(8,128)S(1)}) custom-call(f32[1,12]{1,0:T(1,128)} %bitcast.29, f32[1,12]{1,0:T(1,128)} %bitcast.30, f32[16,1280]{1,0:T(8,128)} %constant.2.clone.dm_hbm, f32[12,256]{1,0:T(8,128)} %kf_hbm.1, s32[1,256]{1,0:T(1,128)} %bitcast.27, ...), custom_call_target="tpu_custom_call" | custom-call | flops 134217728 | bytes 8388608 | tf_op jit(solution)/shard_map/pallas_call | solution.py:393
  25.7 0.0 all-to-all-done
  25.7 0.0 collective-permute-done.3.far_ref
  25.7 0.0 copy-start
  25.7 7.5 %shard_map.155 = (bf16[1024,128]{1,0:T(8,128)(2,1)S(1)}, bf16[1024,128]{1,0:T(8,128)(2,1)S(1)}) custom-call(bf16[4,48,256]{2,1,0:T(8,128)(2,1)S(1)} %pad_maximum_fusion.near_ref, bf16[4,48,256]{2,1,0:T(8,128)(2,1)S(1)} %collective-permute-done.3.far_ref, bf16[128,384]{1,0:T(8,128)(2,1)S(1)} %reshape.26.qs_ref, ...), custom_call_target="tpu_custom_call" | custom-call | flops 1476395008 | bytes 8388608 | tf_op jit(solution)/shard_map/pallas_call | solution.py:420
  33.2 0.1 collective-permute-start.4
  33.3 1.5 %collective-permute-done.4.refs_1_ = bf16[1024,128]{1,0:T(8,128)(2,1)S(1)} collective-permute-done((bf16[1024,128]{1,0:T(8,128)(2,1)S(1)}, bf16[1024,128]{1,0:T(8,128)(2,1)S(1)}, u32[]{:S(2)}, u32[]{:S(2)}) %collective-permute-start.4) | collective-permute-done | bytes 262176 | tf_op jit(solution)/shard_map/ppermute | solution.py:613
  34.9 0.4 shard_map.156
  35.3 1.9 %collective-permute-start.5 = (bf16[256,128]{1,0:T(8,128)(2,1)S(1)}, bf16[256,128]{1,0:T(8,128)(2,1)S(1)}, u32[]{:S(2)}, u32[]{:S(2)}) collective-permute-start(bf16[256,128]{1,0:T(8,128)(2,1)S(1)} %get-tuple-element.29), channel_id=1, source_target_pairs={{0,8},{1,9},{2,10},{3,11},{4,12},{5,13},{6,14},{7,15},{8,16},{9,17... | collective-permute-start | bytes 196616 | tf_op jit(solution)/shard_map/ppermute | solution.py:470
  37.2 2.7 %collective-permute-start.6 = (bf16[256,128]{1,0:T(8,128)(2,1)S(1)}, bf16[256,128]{1,0:T(8,128)(2,1)S(1)}, u32[]{:S(2)}, u32[]{:S(2)}) collective-permute-start(bf16[256,128]{1,0:T(8,128)(2,1)S(1)} %get-tuple-element.30), channel_id=1, source_target_pairs={{0,16},{1,17},{2,18},{3,19},{4,20},{5,21},{6,22},{7,23},{8,24},{9,... | collective-permute-start | bytes 196616 | tf_op jit(solution)/shard_map/ppermute | solution.py:470
  39.9 1.4 %collective-permute-start.7 = (bf16[256,128]{1,0:T(8,128)(2,1)S(1)}, bf16[256,128]{1,0:T(8,128)(2,1)S(1)}, u32[]{:S(2)}, u32[]{:S(2)}) collective-permute-start(bf16[256,128]{1,0:T(8,128)(2,1)S(1)} %get-tuple-element.31), channel_id=1, source_target_pairs={{0,24},{1,25},{2,26},{3,27},{4,28},{5,29},{6,30},{7,31},{8,0},{9,1... | collective-permute-start | bytes 196616 | tf_op jit(solution)/shard_map/ppermute | solution.py:470
  41.3 0.0 collective-permute-done.5.refs_1_
  41.3 2.1 %collective-permute-done.6.refs_2_ = bf16[256,128]{1,0:T(8,128)(2,1)S(1)} collective-permute-done((bf16[256,128]{1,0:T(8,128)(2,1)S(1)}, bf16[256,128]{1,0:T(8,128)(2,1)S(1)}, u32[]{:S(2)}, u32[]{:S(2)}) %collective-permute-start.6) | collective-permute-done | bytes 65568 | tf_op jit(solution)/shard_map/ppermute | solution.py:470
  43.4 0.8 %collective-permute-done.7.refs_3_ = bf16[256,128]{1,0:T(8,128)(2,1)S(1)} collective-permute-done((bf16[256,128]{1,0:T(8,128)(2,1)S(1)}, bf16[256,128]{1,0:T(8,128)(2,1)S(1)}, u32[]{:S(2)}, u32[]{:S(2)}) %collective-permute-start.7) | collective-permute-done | bytes 65568 | tf_op jit(solution)/shard_map/ppermute | solution.py:470
  44.2 0.4 shard_map.157
  44.6 3.4 %collective-permute-start.10 = (bf16[64,128]{1,0:T(8,128)(2,1)S(1)}, bf16[64,128]{1,0:T(8,128)(2,1)S(1)}, u32[]{:S(2)}, u32[]{:S(2)}) collective-permute-start(bf16[64,128]{1,0:T(8,128)(2,1)S(1)} %get-tuple-element.35), channel_id=1, source_target_pairs={{0,6},{1,7},{2,0},{3,1},{4,2},{5,3},{6,4},{7,5},{8,14},{9,15},{10,... | collective-permute-start | bytes 49160 | tf_op jit(solution)/shard_map/ppermute | solution.py:470
  48.0 0.0 collective-permute-start.8
  48.0 2.2 %collective-permute-start.9 = (bf16[64,128]{1,0:T(8,128)(2,1)S(1)}, bf16[64,128]{1,0:T(8,128)(2,1)S(1)}, u32[]{:S(2)}, u32[]{:S(2)}) collective-permute-start(bf16[64,128]{1,0:T(8,128)(2,1)S(1)} %get-tuple-element.34), channel_id=1, source_target_pairs={{0,4},{1,5},{2,6},{3,7},{4,0},{5,1},{6,2},{7,3},{8,12},{9,13},{10,... | collective-permute-start | bytes 49160 | tf_op jit(solution)/shard_map/ppermute | solution.py:470
  50.2 0.0 copy-done
  50.2 0.6 %reshape.33.ob_hbm = f32[1,384]{1,0:T(1,128)} reshape(f32[384]{0:T(512)S(1)} %copy-done) | data formatting | bytes 3072 | tf_op jit(solution)/shard_map/reshape | solution.py:538
  50.8 1.5 %shard_map.158 = (f32[8,128]{1,0:T(8,128)S(1)}, f32[1,384]{1,0:T(1,128)S(1)}, bf16[2112,384]{1,0:T(8,128)(2,1)S(1)}) custom-call(bf16[256,128]{1,0:T(8,128)(2,1)S(1)} %get-tuple-element.28.refs_0_.after, f32[12,128]{1,0:T(8,128)} %qf_hbm.3, f32[1,384]{1,0:T(1,128)} %reshape.33.ob_hbm, bf16[2112,384]{1,0:T(8,128)(2,1)} %ow_hbm.1), custom_call_target="tpu_custom_call" | custom-call | bytes 4194304 | tf_op jit(solution)/shard_map/pallas_call | solution.py:539
  52.3 0.0 collective-permute-done.10.refs_3_
  52.3 1.3 %collective-permute-done.8.refs_1_ = bf16[64,128]{1,0:T(8,128)(2,1)S(1)} collective-permute-done((bf16[64,128]{1,0:T(8,128)(2,1)S(1)}, bf16[64,128]{1,0:T(8,128)(2,1)S(1)}, u32[]{:S(2)}, u32[]{:S(2)}) %collective-permute-start.8) | collective-permute-done | bytes 16416 | tf_op jit(solution)/shard_map/ppermute | solution.py:470
  53.5 0.0 collective-permute-done.9.refs_2_
  53.5 1.5 %shard_map.159 = bf16[4,384]{1,0:T(4,128)(2,1)} custom-call(bf16[64,128]{1,0:T(8,128)(2,1)S(1)} %get-tuple-element.32.refs_0_, bf16[64,128]{1,0:T(8,128)(2,1)S(1)} %collective-permute-done.8.refs_1_, bf16[64,128]{1,0:T(8,128)(2,1)S(1)} %collective-permute-done.9.refs_2_, bf16[64,128]{1,0:T(8,128)(2,1)S(1)} %collective-permute-done.10.refs_3_, ...), custom_call_target="tpu_custom_call" | custom-call | tf_op jit(solution)/shard_map/pallas_call | solution.py:556
  (1 shorter events, 0.0 us)
Async XLA Ops:
  0.0 15.0 %collective-permute-start = (bf16[48,256]{1,0:T(8,128)(2,1)}, bf16[48,256]{1,0:T(8,128)(2,1)S(1)}, u32[]{:S(2)}, u32[]{:S(2)}) collective-permute-start(bf16[48,256]{1,0:T(8,128)(2,1)} %bitcast.19), channel_id=1, source_target_pairs={{64,0},{96,32},{128,64},{160,96},{192,128},{224,160},{0,192},{32,2... | collective-permute-start | bytes 73736 | tf_op jit(solution)/shard_map/ppermute | solution.py:592
  2.3 12.8 %collective-permute-start.1 = (bf16[48,256]{1,0:T(8,128)(2,1)}, bf16[48,256]{1,0:T(8,128)(2,1)S(1)}, u32[]{:S(2)}, u32[]{:S(2)}) collective-permute-start(bf16[48,256]{1,0:T(8,128)(2,1)} %bitcast.20), channel_id=1, source_target_pairs={{128,0},{160,32},{192,64},{224,96},{0,128},{32,160},{64,192},{96,2... | collective-permute-start | bytes 73736 | tf_op jit(solution)/shard_map/ppermute | solution.py:592
  3.0 12.1 %collective-permute-start.2 = (bf16[48,256]{1,0:T(8,128)(2,1)}, bf16[48,256]{1,0:T(8,128)(2,1)S(1)}, u32[]{:S(2)}, u32[]{:S(2)}) collective-permute-start(bf16[48,256]{1,0:T(8,128)(2,1)} %bitcast.21), channel_id=1, source_target_pairs={{192,0},{224,32},{0,64},{32,96},{64,128},{96,160},{128,192},{160,2... | collective-permute-start | bytes 73736 | tf_op jit(solution)/shard_map/ppermute | solution.py:592
  6.1 19.6 %all-to-all-start = ((bf16[32,4,384]{2,1,0:T(4,128)(2,1)}), bf16[32,4,384]{2,1,0:T(4,128)(2,1)S(1)}, u32[]{:S(2)}, u32[]{:S(2)}) async-start(bf16[32,4,384]{2,1,0:T(4,128)(2,1)} %broadcast_in_dim.2), calls=%async_computation | async-start | bytes 196608 | tf_op jit(solution)/shard_map/all_to_all | solution.py:599
  15.8 9.9 %collective-permute-start.3 = (bf16[4,48,256]{2,1,0:T(8,128)(2,1)S(1)}, bf16[4,48,256]{2,1,0:T(8,128)(2,1)S(1)}, u32[]{:S(2)}, u32[]{:S(2)}) collective-permute-start(bf16[4,48,256]{2,1,0:T(8,128)(2,1)S(1)} %pad_maximum_fusion.near_ref), channel_id=1, source_target_pairs={{0,32},{32,0},{64,96},{96,64},{128,160},{160,128},{192,224},{224,1... | collective-permute-start | bytes 294920 | tf_op jit(solution)/shard_map/ppermute | solution.py:598
  25.7 24.5 %copy-start = (f32[384]{0:T(512)S(1)}, f32[384]{0:T(512)}, u32[]{:S(2)}) copy-start(f32[384]{0:T(512)} %param.30) | copy-start | bytes 4612
  33.2 1.6 %collective-permute-start.4 = (bf16[1024,128]{1,0:T(8,128)(2,1)S(1)}, bf16[1024,128]{1,0:T(8,128)(2,1)S(1)}, u32[]{:S(2)}, u32[]{:S(2)}) collective-permute-start(bf16[1024,128]{1,0:T(8,128)(2,1)S(1)} %get-tuple-element.27), channel_id=1, source_target_pairs={{0,1},{1,0},{2,3},{3,2},{4,5},{5,4},{6,7},{7,6},{8,9},{9,8},{10,11... | collective-permute-start | bytes 786440 | tf_op jit(solution)/shard_map/ppermute | solution.py:613
  35.3 6.0 %collective-permute-start.5 = (bf16[256,128]{1,0:T(8,128)(2,1)S(1)}, bf16[256,128]{1,0:T(8,128)(2,1)S(1)}, u32[]{:S(2)}, u32[]{:S(2)}) collective-permute-start(bf16[256,128]{1,0:T(8,128)(2,1)S(1)} %get-tuple-element.29), channel_id=1, source_target_pairs={{0,8},{1,9},{2,10},{3,11},{4,12},{5,13},{6,14},{7,15},{8,16},{9,17... | collective-permute-start | bytes 196616 | tf_op jit(solution)/shard_map/ppermute | solution.py:470
  37.2 6.2 %collective-permute-start.6 = (bf16[256,128]{1,0:T(8,128)(2,1)S(1)}, bf16[256,128]{1,0:T(8,128)(2,1)S(1)}, u32[]{:S(2)}, u32[]{:S(2)}) collective-permute-start(bf16[256,128]{1,0:T(8,128)(2,1)S(1)} %get-tuple-element.30), channel_id=1, source_target_pairs={{0,16},{1,17},{2,18},{3,19},{4,20},{5,21},{6,22},{7,23},{8,24},{9,... | collective-permute-start | bytes 196616 | tf_op jit(solution)/shard_map/ppermute | solution.py:470
  39.9 4.3 %collective-permute-start.7 = (bf16[256,128]{1,0:T(8,128)(2,1)S(1)}, bf16[256,128]{1,0:T(8,128)(2,1)S(1)}, u32[]{:S(2)}, u32[]{:S(2)}) collective-permute-start(bf16[256,128]{1,0:T(8,128)(2,1)S(1)} %get-tuple-element.31), channel_id=1, source_target_pairs={{0,24},{1,25},{2,26},{3,27},{4,28},{5,29},{6,30},{7,31},{8,0},{9,1... | collective-permute-start | bytes 196616 | tf_op jit(solution)/shard_map/ppermute | solution.py:470
  44.6 7.6 %collective-permute-start.10 = (bf16[64,128]{1,0:T(8,128)(2,1)S(1)}, bf16[64,128]{1,0:T(8,128)(2,1)S(1)}, u32[]{:S(2)}, u32[]{:S(2)}) collective-permute-start(bf16[64,128]{1,0:T(8,128)(2,1)S(1)} %get-tuple-element.35), channel_id=1, source_target_pairs={{0,6},{1,7},{2,0},{3,1},{4,2},{5,3},{6,4},{7,5},{8,14},{9,15},{10,... | collective-permute-start | bytes 49160 | tf_op jit(solution)/shard_map/ppermute | solution.py:470
  48.0 5.5 %collective-permute-start.8 = (bf16[64,128]{1,0:T(8,128)(2,1)S(1)}, bf16[64,128]{1,0:T(8,128)(2,1)S(1)}, u32[]{:S(2)}, u32[]{:S(2)}) collective-permute-start(bf16[64,128]{1,0:T(8,128)(2,1)S(1)} %get-tuple-element.33), channel_id=1, source_target_pairs={{0,2},{1,3},{2,4},{3,5},{4,6},{5,7},{6,0},{7,1},{8,10},{9,11},{10,... | collective-permute-start | bytes 49160 | tf_op jit(solution)/shard_map/ppermute | solution.py:470
  48.0 5.5 %collective-permute-start.9 = (bf16[64,128]{1,0:T(8,128)(2,1)S(1)}, bf16[64,128]{1,0:T(8,128)(2,1)S(1)}, u32[]{:S(2)}, u32[]{:S(2)}) collective-permute-start(bf16[64,128]{1,0:T(8,128)(2,1)S(1)} %get-tuple-element.34), channel_id=1, source_target_pairs={{0,4},{1,5},{2,6},{3,7},{4,0},{5,1},{6,2},{7,3},{8,12},{9,13},{10,... | collective-permute-start | bytes 49160 | tf_op jit(solution)/shard_map/ppermute | solution.py:470

commit v6 on v5

--- a/solution.py
+++ b/solution.py
@@ -112,14 +112,11 @@
     steps = pair_ref.shape[0] // groups
     copies = [
         pltpu.make_async_copy(
-            pair_ref.at[pl.ds(groups * step, groups), 1 - core if half == 0 else core],
-            pair_v.at[half * steps + step],
-            pair_sem.at[half * steps + step],
+            pair_ref.at[pl.ds(groups * step, groups), 1 - core], pair_v.at[step], pair_sem.at[step]
         )
-        for half in range(2)
         for step in range(steps)
     ]
-    for copy in small[:1] + copies[:4] + small[1:] + copies[4:]:
+    for copy in small[:1] + copies[:2] + small[1:] + copies[2:]:
         copy.start()
     small[0].wait()
     pw_s[...] = jnp.zeros_like(pw_s)
@@ -129,7 +126,7 @@
         if i == len(copies) // 2:
             for other in small[1:]:
                 other.wait()
-            prepare_masks(raw_v, cb_v, dm_v, kf_v, kc_v, km_v, qf_v, qc_v, mask_ref)
+            prepare_masks(raw_v, cb_v, dm_v, kf_v, kc_v, km_v, qf_v, qc_v, pw_s[...], mask_ref)
         copy.wait()
         for q in range(SB):
             row = (SB * i + q) * HP
@@ -141,7 +138,7 @@
             )
 
 
-def prepare_masks(raw_v, cb_v, dm_v, kf_v, kc_v, km_v, qf_v, qc_v, mask_ref):
+def prepare_masks(raw_v, cb_v, dm_v, kf_v, kc_v, km_v, qf_v, qc_v, pw, mask_ref):
     mask_ref[:, 0 : KD + GL] = dm_v[...]
     lane = lax.broadcasted_iota(jnp.int32, (HP, 128), 1)
     tail = dm_v[:, 640:768]
@@ -157,6 +154,7 @@
     mask_ref[0:H, at + 384 : at + 512] = qf_v[...]
     mask_ref[H : H + 1, at + 384 : at + 512] = qc_v[...].astype(F32)
     mask_ref[H + 1 : H + 2, at + 384 : at + 384 + H] = raw_v[...]
+    mask_ref[:, at + 512 :] = pw
 
 
 def prepare_keys(info, gamma16, kt_ref, vt_ref, kpt_s, nk_s):
@@ -212,7 +210,7 @@
 
 
 def attend_kernel(
-    near_ref, far_ref, qs_ref, wk_ref, mask_ref, wq_ref, bias_ref, pair_ref,
+    both_ref, next_ref, over_ref, last_ref, qs_ref, wk_ref, mask_ref, wq_ref, bias_ref, pair_ref,
     send_ref, own_ref, kpt_s, nk_s, kt_s, vt_s, v_s, w_s, z_s, o_s, ks_s,
     qpt_s, nq_s, qft_s, qf_s, feat_s, pair_v, pair_sem,
 ):
@@ -220,7 +218,8 @@
     groups = QB // SHARE
     steps = pair_ref.shape[0] // groups
     copies = {}
-    for index in range(2 * steps):
+    order = [*range(steps, 2 * steps), *range(steps)]
+    for index in order:
         half, step = divmod(index, steps)
         copies[index] = pltpu.make_async_copy(
             pair_ref.at[pl.ds(groups * step, groups), 1 - core if half == 0 else core],
@@ -229,11 +228,13 @@
         )
         copies[index].start()
     row = lax.axis_index("row")
-    count, part = near_ref.shape[:2]
-    for k in range(count):
-        x = lax.rem(lax.div(row, 2) + k, count)
-        for ref, z in ((near_ref, lax.rem(row, 2)), (far_ref, 1 - lax.rem(row, 2))):
-            ks_s[pl.ds(pl.multiple_of((2 * x + z) * part, part), part), :] = ref[k]
+    pieces = (both_ref, next_ref, over_ref, last_ref)
+    part = both_ref.shape[1]
+    for k, ref in enumerate(pieces):
+        x = lax.rem(lax.div(row, 2) + k, len(pieces))
+        for z in range(2):
+            own = jnp.bitwise_xor(lax.rem(row, 2), z)
+            ks_s[pl.ds(pl.multiple_of((2 * x + own) * part, part), part), :] = ref[z]
     put(kpt_s, 0, jnp.dot(wk_ref[...], ks_s[...], preferred_element_type=F32))
     info = mask_ref[:, KD + GL : KD + GL + 256]
     gamma16 = mask_ref[:, KD + GL + 256 : KD + GL + 257]
@@ -252,6 +253,7 @@
         == lax.broadcasted_iota(jnp.int32, (QB, rows), 0)
     ).astype(BF16)
 
+    weight = mask_ref[:, KD + GL + 512 :].astype(BF16)
     for half in range(2):
         for step in range(steps):
             start = (half * steps + step) * rows
@@ -259,7 +261,23 @@
             mine = feat_s[group : group + groups].reshape(QB, 1, KD)
             spread = (mine * mask_ref[:, 0:KD][None]).reshape(rows, KD).astype(BF16)
             logits = jnp.dot(spread, kt_s[...], preferred_element_type=F32)
-            bias = bias_ref[start : start + rows, :]
+            if half == 0:
+                bias = bias_ref[start : start + rows, :]
+            else:
+                index = steps + step
+                copies[index].wait()
+                bias = jnp.concatenate(
+                    [
+                        lax.dot_general(
+                            weight,
+                            pair_v[index, q // SHARE, q % SHARE],
+                            NT,
+                            preferred_element_type=F32,
+                        )
+                        for q in range(QB)
+                    ],
+                    0,
+                )
             logits = math.sqrt(1.0 / 3.0) * (logits + bias)
             peak = jnp.maximum(jnp.max(logits, 1, keepdims=True), 0.1 * FAR)
             expd = jnp.exp(logits - peak)
@@ -284,12 +302,13 @@
                 gather, jnp.concatenate(own, 1), preferred_element_type=F32
             )
 
-    for half in range(2):
+    for half in (1, 0):
         out_ref = (send_ref, own_ref)[half]
         for step in range(steps):
             index = half * steps + step
             start = index * rows
-            copies[index].wait()
+            if half == 0:
+                copies[index].wait()
             block = pair_v.at[index]
             for i in range(QB):
                 row = start + HP * i
@@ -362,8 +381,8 @@
         held[0][pl.ds(H + r, queries, stride=HP), :] = mixed[r]
 
 
-def join_kernel(count, first, *refs):
-    sources, parts, held = refs[:count], refs[count:-count], refs[-count:]
+def join_kernel(count, first, skip, *refs):
+    sources, parts, held = refs[:count], refs[count + skip : -count], refs[-count:]
     rows = sources[0].shape[0]
     merge(sources, held)
     place = first(lax.axis_index("col"))
@@ -393,22 +412,22 @@
     return pl.pallas_call(
         shadow_kernel,
         out_shape=(
-            pltpu.VMEM((HP, KD + GL + keys + 256), F32),
+            pltpu.VMEM((HP, KD + GL + keys + 384), F32),
             pltpu.VMEM(others[9].shape, BF16),
             pltpu.VMEM(others[10].shape, BF16),
-            pltpu.VMEM((queries * HP, keys), F32),
+            pltpu.VMEM((queries * HP // 2, keys), F32),
         ),
         in_specs=[HBM] * 12,
         out_specs=(VMEM,) * 4,
         scratch_shapes=[pltpu.VMEM(x.shape, x.dtype) for x in others[:9]]
         + [
             pltpu.VMEM((HP, CZ), F32),
-            pltpu.VMEM((queries // SB, SB // SHARE, SHARE, keys, CZ), BF16),
+            pltpu.VMEM((queries // SB // 2, SB // SHARE, SHARE, keys, CZ), BF16),
             pltpu.SemaphoreType.DMA((11,)),
-            pltpu.SemaphoreType.DMA((queries // SB,)),
+            pltpu.SemaphoreType.DMA((queries // SB // 2,)),
         ],
         cost_estimate=pl.CostEstimate(
-            flops=2 * queries * keys * CZ * HP, bytes_accessed=pair.size * 2, transcendentals=0
+            flops=queries * keys * CZ * HP, bytes_accessed=pair.size, transcendentals=0
         ),
         compiler_params=pltpu.CompilerParams(vmem_limit_bytes=16 * 2**20),
     )(*[outside(x) for x in (*others, pair)])
@@ -420,7 +439,7 @@
     return pl.pallas_call(
         attend_kernel,
         out_shape=(jax.ShapeDtypeStruct((queries * HP // 2, CZ), BF16),) * 2,
-        in_specs=[VMEM] * (len(held) + 3) + [HBM],
+        in_specs=[VMEM] * (len(held) + 5) + [HBM],
         out_specs=(VMEM,) * 2,
         scratch_shapes=[
             pltpu.VMEM((keys // 128, 896, 128), F32),
@@ -432,7 +451,7 @@
             pltpu.VMEM((queries, GL), F32),
             pltpu.VMEM((queries * HP, CZ), F32),
             pltpu.VMEM((384, keys), BF16),
-            pltpu.VMEM((queries // 128, 384, 128), F32),
+            pltpu.VMEM((queries // 128, 448, 128), F32),
             pltpu.VMEM((HP, queries), F32),
             pltpu.VMEM((KD, queries), F32),
             pltpu.VMEM((queries, KD), F32),
@@ -449,16 +468,16 @@
     )(*came, *[inside(x) for x in held], outside(pair))
 
 
-def join(sources, first, parts):
+def join(sources, first, parts, after=()):
     rows, columns = sources[0].shape
     return pl.pallas_call(
-        functools.partial(join_kernel, len(sources), first),
+        functools.partial(join_kernel, len(sources), first, len(after)),
         out_shape=(jax.ShapeDtypeStruct((rows // parts, columns), BF16),) * parts,
-        in_specs=[VMEM] * len(sources),
+        in_specs=[VMEM] * (len(sources) + len(after)),
         out_specs=(VMEM,) * parts,
         scratch_shapes=[pltpu.VMEM((rows, columns), F32)] * len(sources),
         compiler_params=pltpu.CompilerParams(vmem_limit_bytes=8 * 2**20),
-    )(*sources)
+    )(*sources, *[inside(x) for x in after])
 
 
 def exchange(parts, width, apart, count):
@@ -495,6 +514,7 @@
     parts, refs = refs[:sources], refs[sources:]
     fr_ref, ob_ref, ow_ref, out_ref, f_s, *held = refs
     share = out_ref.shape[0]
+    held = [ref.at[pl.ds(0, share * HP)] for ref in held]
     merge(parts, held)
     sums = held[0]
     frame = [fr_ref[0:share, j : j + 1] for j in range(12)]
@@ -560,7 +580,7 @@
         out_specs=VMEM,
         scratch_shapes=[
             pltpu.VMEM((share, 896), F32),
-            *[pltpu.VMEM(parts[0].shape, F32)] * sources,
+            *[pltpu.VMEM((8 * HP + HP, CZ), F32)] * sources,
         ],
         compiler_params=pltpu.CompilerParams(vmem_limit_bytes=4 * 2**20),
     )(*parts, *[inside(x) for x in others])
@@ -586,19 +606,24 @@
     rows, cols = lax.axis_size("row"), lax.axis_size("col")
     turned = key_single.T
     chips = rows // 2
-    near = jnp.stack(
-        [turned]
-        + [
-            lax.ppermute(
-                turned, "row", [((i + 2 * k) % rows, i) for i in range(rows)]
-            )
-            for k in range(1, chips)
-        ]
+    both = jnp.stack([turned, lax.ppermute(turned, "row", [(i, i ^ 1) for i in range(rows)])])
+    rest = [
+        lax.ppermute(both, "row", [((i + 2 * k) % rows, i) for i in range(rows)])
+        for k in range(1, chips)
+    ]
+    other = lax.ppermute(query_single, "col", [(i, i ^ 1) for i in range(cols)])
+    even = lax.rem(lax.axis_index("col"), 2) == 0
+    chip = jnp.concatenate(
+        [jnp.where(even, query_single, other), jnp.where(even, other, query_single)], 0
     )
-    far = lax.ppermute(near, "row", [(i, i ^ 1) for i in range(rows)])
     queries = lax.all_to_all(
-        jnp.broadcast_to(query_single[None], (cols, *query_single.shape)), "col", 0, 0, tiled=True
-    ).reshape(-1, query_single.shape[1])
+        jnp.broadcast_to(chip[None], (cols // 2, *chip.shape)),
+        "col",
+        0,
+        0,
+        axis_index_groups=[list(range(core, cols, 2)) for core in range(2)],
+        tiled=True,
+    ).reshape(-1, chip.shape[1])
     heads = (lane_heads()[1][None, :] == np.arange(HP)[:, None]).astype(np.float32)
     mask, wk, wq, bias = shadow(
         [
@@ -609,13 +634,16 @@
         ],
         pair,
     )
-    send, own = attend([near, far, queries], [wk, mask, wq, bias], pair)
+    send, own = attend([both, *rest, queries], [wk, mask, wq, bias], pair)
     come = lax.ppermute(send, "col", [(i, i ^ 1) for i in range(cols)])
     sums = join([own, come], lambda col: lax.div(col, 8), 4)
     sums = exchange(sums, 4, 8, cols)
     others = fetch(sums[0], query_frames, out_weight, out_bias)
-    sums = join(sums, lambda col: lax.rem(lax.div(col, 2), 4), 4)
-    parts = exchange(sums, 4, 2, cols)
+    keep, send = join(sums, lambda col: lax.rem(lax.div(col, 4), 2), 2, others[:1])
+    come = lax.ppermute(send, "col", [(i, i ^ 4) for i in range(cols)])
+    keep, send = join([keep, come], lambda col: lax.rem(lax.div(col, 2), 2), 2)
+    come = lax.ppermute(send, "col", [(i, i ^ 2) for i in range(cols)])
+    parts = [keep, come]
     return finish(parts, others, out_weight.shape[1])
 
 

time: 55.3 us -> 53.8 us (0.973)
  starting transfers between devices: 29.9 us -> 28.1 us
  Pallas kernels: 16.6 us -> 15.1 us
  waiting for transfers between devices: 5.64 us -> 7 us
  local copies, waits for them, and re-layouts: 1.96 us -> 1.22 us
  other arithmetic: 0.76 us -> 1.45 us
    ppermute x4 -> x7, starting transfers between devices: 9.33 us -> 15.9 us  [the longest x1 7.19 us: body(): lax.ppermute(turned, 'row', [(i, i ^ 1) for i in range(rows)])]
    ppermute x6 -> x3, starting transfers between devices: 11.6 us -> 6.14 us  [exchange(): lax.ppermute(parts[k], 'col', [(i, to(i, k)) for i in range(count)])]
    ppermute x4 -> x7, waiting for transfers between devices: 0.01 us -> 4.75 us  [the longest x1 2.46 us: body(): come = lax.ppermute(send, 'col', [(i, i ^ 4) for i in range(cols)])]
    ppermute x6 -> x3, waiting for transfers between devices: 4.11 us -> 0.73 us  [exchange(): lax.ppermute(parts[k], 'col', [(i, to(i, k)) for i in range(count)])]
    all_to_all x1, starting transfers between devices: 8.92 us -> 5.94 us  [body(): lax.all_to_all(jnp.broadcast_to(chip[None], (cols // 2, *chip.shape)), 'c...]
    pallas_call x1, Pallas kernels: 5.24 us -> 3.25 us  [shadow(): pl.pallas_call(shadow_kernel, out_shape=(pltpu.VMEM((HP, KD + GL + keys +...]
    broadcast_in_dim x1, local copies, waits for them, and re-layouts: 1.36 us -> 0.65 us  [body(): jnp.broadcast_to(chip[None], (cols // 2, *chip.shape))]
    select_n x0 -> x1, other arithmetic: none -> 0.69 us  [body(): jnp.where(even, query_single, other)]
  transfers between devices with their start and end apart: 12 -> 12, of which waited for: 4 -> 4; matrix products, arithmetic and copies ran while one was open for 5% -> 5% of each run, Pallas kernels for 12% -> 9%
where the time goes in v6:
time: 53.8 us; the launch traced here: 53.1 us
  starting transfers between devices  28.1 us (52%)
  Pallas kernels  15.1 us (28%)
  waiting for transfers between devices  7 us (13%)
  other arithmetic  1.45 us (3%)
  local copies, waits for them, and re-layouts  1.22 us (2%)
    pallas_call x1, Pallas kernels, attend(): pl.pallas_call(attend_kernel, out_shape=(jax.ShapeDtypeStruct((queries *...  7.84 us
    ppermute x1, starting transfers between devices, body(): lax.ppermute(turned, 'row', [(i, i ^ 1) for i in range(rows)])  7.19 us
    ppermute x3, starting transfers between devices, exchange(): lax.ppermute(parts[k], 'col', [(i, to(i, k)) for i in range(count)])  6.14 us
    all_to_all x1, starting transfers between devices, body(): lax.all_to_all(jnp.broadcast_to(chip[None], (cols // 2, *chip.shape)), 'c...  5.94 us
    ppermute x3, starting transfers between devices, body(): lax.ppermute(both, 'row', [((i + 2 * k) % rows, i) for i in range(rows)])  4.76 us
    pallas_call x1, Pallas kernels, shadow(): pl.pallas_call(shadow_kernel, out_shape=(pltpu.VMEM((HP, KD + GL + keys +...  3.25 us
    ppermute x1, waiting for transfers between devices, body(): come = lax.ppermute(send, 'col', [(i, i ^ 4) for i in range(cols)])  2.46 us
    ppermute x1, starting transfers between devices, body(): come = lax.ppermute(send, 'col', [(i, i ^ 4) for i in range(cols)])  2.45 us
  transfers between devices with their start and end apart: 12, of which 4 were waited for; matrix products, arithmetic and copies ran while one was open for 5% of the time, Pallas kernels for 9%

profile of v6, /device:TPU:2, one launch (start us, length us, event | category | flops | bytes accessed | tf_op | source)
XLA Modules:
  0.0 53.1 jit_solution(11684736954011499290)
XLA Ops:
  0.0 0.0 collective-permute-start.4
  0.0 7.2 %collective-permute-start = (bf16[48,256]{1,0:T(8,128)(2,1)}, bf16[48,256]{1,0:T(8,128)(2,1)S(1)}, u32[]{:S(2)}, u32[]{:S(2)}) collective-permute-start(bf16[48,256]{1,0:T(8,128)(2,1)} %bitcast.19), channel_id=1, source_target_pairs={{0,32},{32,0},{64,96},{96,64},{128,160},{160,128},{192,224},{224,1... | collective-permute-start | bytes 73736 | tf_op jit(solution)/shard_map/ppermute | solution.py:609
  7.2 0.0 collective-permute-done.4
  7.2 0.7 %broadcast_select_fusion.1 = (bf16[4,384]{1,0:T(4,128)(2,1)S(1)}, bf16[4,384]{1,0:T(4,128)(2,1)S(1)}) fusion(bf16[4,384]{1,0:T(4,128)(2,1)} %param.16, bf16[4,384]{1,0:T(4,128)(2,1)S(1)} %collective-permute-done.4, pred[]{:T(512)S(6)} %eq.3), kind=kLoop, calls=%fused_computation.3 | loop fusion | flops 3072 | bytes 12289 | tf_op jit(solution)/shard_map/jit(_where)/select_n | solution.py:617
  7.9 0.7 %broadcast_in_dim.2 = bf16[16,8,384]{2,1,0:T(8,128)(2,1)} broadcast(bf16[8,384]{1,0:T(8,128)(2,1)S(1)} %pad_maximum_fusion.1), dimensions={1,2} | broadcast | bytes 104448 | tf_op jit(solution)/shard_map/broadcast_in_dim | solution.py:620
  8.6 5.9 %all-to-all-start = ((bf16[16,8,384]{2,1,0:T(8,128)(2,1)}), bf16[16,8,384]{2,1,0:T(8,128)(2,1)S(1)}, u32[]{:S(2)}, u32[]{:S(2)}) async-start(bf16[16,8,384]{2,1,0:T(8,128)(2,1)} %broadcast_in_dim.2), calls=%async_computation | async-start | bytes 196608 | tf_op jit(solution)/shard_map/all_to_all | solution.py:619
  14.5 0.0 collective-permute-done
  14.5 0.7 %pad_maximum_fusion.both_ref = bf16[2,48,256]{2,1,0:T(8,128)(2,1)S(1)} fusion(bf16[1,48,256]{2,1,0:T(8,128)(2,1)S(1)} %bitcast.21, bf16[1,48,256]{2,1,0:T(8,128)(2,1)} %bitcast.20), kind=kLoop, calls=%fused_computation | loop fusion | flops 24576 | bytes 98304 | tf_op jit(solution)/shard_map/stack | solution.py:609
  15.3 0.5 %collective-permute-start.1 = (bf16[2,48,256]{2,1,0:T(8,128)(2,1)S(1)}, bf16[2,48,256]{2,1,0:T(8,128)(2,1)S(1)}, u32[]{:S(2)}, u32[]{:S(2)}) collective-permute-start(bf16[2,48,256]{2,1,0:T(8,128)(2,1)S(1)} %pad_maximum_fusion.both_ref), channel_id=1, source_target_pairs={{64,0},{96,32},{128,64},{160,96},{192,128},{224,160},{0,192},{32,2... | collective-permute-start | bytes 147464 | tf_op jit(solution)/shard_map/ppermute | solution.py:611
  15.8 2.4 %collective-permute-start.2 = (bf16[2,48,256]{2,1,0:T(8,128)(2,1)S(1)}, bf16[2,48,256]{2,1,0:T(8,128)(2,1)S(1)}, u32[]{:S(2)}, u32[]{:S(2)}) collective-permute-start(bf16[2,48,256]{2,1,0:T(8,128)(2,1)S(1)} %pad_maximum_fusion.both_ref), channel_id=1, source_target_pairs={{128,0},{160,32},{192,64},{224,96},{0,128},{32,160},{64,192},{96,2... | collective-permute-start | bytes 147464 | tf_op jit(solution)/shard_map/ppermute | solution.py:611
  18.2 1.8 %collective-permute-start.3 = (bf16[2,48,256]{2,1,0:T(8,128)(2,1)S(1)}, bf16[2,48,256]{2,1,0:T(8,128)(2,1)S(1)}, u32[]{:S(2)}, u32[]{:S(2)}) collective-permute-start(bf16[2,48,256]{2,1,0:T(8,128)(2,1)S(1)} %pad_maximum_fusion.both_ref), channel_id=1, source_target_pairs={{192,0},{224,32},{0,64},{32,96},{64,128},{96,160},{128,192},{160,2... | collective-permute-start | bytes 147464 | tf_op jit(solution)/shard_map/ppermute | solution.py:611
  20.0 3.3 %shard_map.154 = (f32[16,1920]{1,0:T(8,128)S(1)}, bf16[816,384]{1,0:T(8,128)(2,1)S(1)}, bf16[336,384]{1,0:T(8,128)(2,1)S(1)}, f32[1024,256]{1,0:T(8,128)S(1)}) custom-call(f32[1,12]{1,0:T(1,128)} %bitcast.25, f32[1,12]{1,0:T(1,128)} %bitcast.26, f32[16,1280]{1,0:T(8,128)} %constant.12.clone.dm_hbm, f32[12,256]{1,0:T(8,128)} %kf_hbm.1, s32[1,256]{1,0:T(1,128)} %bitcast.23, ...), custom_call_target="tpu_custom_call" | custom-call | flops 67108864 | bytes 4194304 | tf_op jit(solution)/shard_map/pallas_call | solution.py:412
  23.3 0.0 collective-permute-done.1.next_ref
  23.3 0.0 collective-permute-done.2.over_ref
  23.3 0.0 collective-permute-done.3.last_ref
  23.3 0.0 all-to-all-done
  23.3 0.0 copy-start
  23.3 7.8 %shard_map.155 = (bf16[1024,128]{1,0:T(8,128)(2,1)S(1)}, bf16[1024,128]{1,0:T(8,128)(2,1)S(1)}) custom-call(bf16[2,48,256]{2,1,0:T(8,128)(2,1)S(1)} %pad_maximum_fusion.both_ref, bf16[2,48,256]{2,1,0:T(8,128)(2,1)S(1)} %collective-permute-done.1.next_ref, bf16[2,48,256]{2,1,0:T(8,128)(2,1)S(1)} %collective-permute-done.2.over_ref, ...), custom_call_target="tpu_custom_call" | custom-call | flops 1476395008 | bytes 8388608 | tf_op jit(solution)/shard_map/pallas_call | solution.py:439
  31.2 0.1 collective-permute-start.5
  31.3 1.5 %collective-permute-done.5.refs_1_ = bf16[1024,128]{1,0:T(8,128)(2,1)S(1)} collective-permute-done((bf16[1024,128]{1,0:T(8,128)(2,1)S(1)}, bf16[1024,128]{1,0:T(8,128)(2,1)S(1)}, u32[]{:S(2)}, u32[]{:S(2)}) %collective-permute-start.5) | collective-permute-done | bytes 262176 | tf_op jit(solution)/shard_map/ppermute | solution.py:638
  32.8 0.5 shard_map.156
  33.3 2.0 %collective-permute-start.6 = (bf16[256,128]{1,0:T(8,128)(2,1)S(1)}, bf16[256,128]{1,0:T(8,128)(2,1)S(1)}, u32[]{:S(2)}, u32[]{:S(2)}) collective-permute-start(bf16[256,128]{1,0:T(8,128)(2,1)S(1)} %get-tuple-element.29), channel_id=1, source_target_pairs={{0,8},{1,9},{2,10},{3,11},{4,12},{5,13},{6,14},{7,15},{8,16},{9,17... | collective-permute-start | bytes 196616 | tf_op jit(solution)/shard_map/ppermute | solution.py:489
  35.3 2.7 %collective-permute-start.7 = (bf16[256,128]{1,0:T(8,128)(2,1)S(1)}, bf16[256,128]{1,0:T(8,128)(2,1)S(1)}, u32[]{:S(2)}, u32[]{:S(2)}) collective-permute-start(bf16[256,128]{1,0:T(8,128)(2,1)S(1)} %get-tuple-element.30), channel_id=1, source_target_pairs={{0,16},{1,17},{2,18},{3,19},{4,20},{5,21},{6,22},{7,23},{8,24},{9,... | collective-permute-start | bytes 196616 | tf_op jit(solution)/shard_map/ppermute | solution.py:489
  37.9 1.5 %collective-permute-start.8 = (bf16[256,128]{1,0:T(8,128)(2,1)S(1)}, bf16[256,128]{1,0:T(8,128)(2,1)S(1)}, u32[]{:S(2)}, u32[]{:S(2)}) collective-permute-start(bf16[256,128]{1,0:T(8,128)(2,1)S(1)} %get-tuple-element.31), channel_id=1, source_target_pairs={{0,24},{1,25},{2,26},{3,27},{4,28},{5,29},{6,30},{7,31},{8,0},{9,1... | collective-permute-start | bytes 196616 | tf_op jit(solution)/shard_map/ppermute | solution.py:489
  39.4 0.0 copy-done
  39.4 0.6 %reshape.33.ob_hbm = f32[1,384]{1,0:T(1,128)} reshape(f32[384]{0:T(512)S(1)} %copy-done) | data formatting | bytes 3072 | tf_op jit(solution)/shard_map/reshape | solution.py:558
  40.0 1.5 %shard_map.157 = (f32[8,128]{1,0:T(8,128)S(1)}, f32[1,384]{1,0:T(1,128)S(1)}, bf16[2112,384]{1,0:T(8,128)(2,1)S(1)}) custom-call(bf16[256,128]{1,0:T(8,128)(2,1)S(1)} %get-tuple-element.28.after.refs_0_, f32[12,128]{1,0:T(8,128)} %qf_hbm.3, f32[1,384]{1,0:T(1,128)} %reshape.33.ob_hbm, bf16[2112,384]{1,0:T(8,128)(2,1)} %ow_hbm.1), custom_call_target="tpu_custom_call" | custom-call | bytes 4194304 | tf_op jit(solution)/shard_map/pallas_call | solution.py:559
  41.5 0.0 collective-permute-done.6.refs_1_
  41.5 0.0 collective-permute-done.7.refs_2_
  41.5 0.7 %collective-permute-done.8.refs_3_ = bf16[256,128]{1,0:T(8,128)(2,1)S(1)} collective-permute-done((bf16[256,128]{1,0:T(8,128)(2,1)S(1)}, bf16[256,128]{1,0:T(8,128)(2,1)S(1)}, u32[]{:S(2)}, u32[]{:S(2)}) %collective-permute-start.8) | collective-permute-done | bytes 65568 | tf_op jit(solution)/shard_map/ppermute | solution.py:489
  42.2 0.4 shard_map.158
  42.7 2.4 %collective-permute-start.9 = (bf16[128,128]{1,0:T(8,128)(2,1)S(1)}, bf16[128,128]{1,0:T(8,128)(2,1)S(1)}, u32[]{:S(2)}, u32[]{:S(2)}) collective-permute-start(bf16[128,128]{1,0:T(8,128)(2,1)S(1)} %get-tuple-element.34), channel_id=1, source_target_pairs={{0,4},{1,5},{2,6},{3,7},{4,0},{5,1},{6,2},{7,3},{8,12},{9,13},{10,... | collective-permute-start | bytes 98312 | tf_op jit(solution)/shard_map/ppermute | solution.py:643
  45.1 2.5 %collective-permute-done.9.refs_1_ = bf16[128,128]{1,0:T(8,128)(2,1)S(1)} collective-permute-done((bf16[128,128]{1,0:T(8,128)(2,1)S(1)}, bf16[128,128]{1,0:T(8,128)(2,1)S(1)}, u32[]{:S(2)}, u32[]{:S(2)}) %collective-permute-start.9) | collective-permute-done | bytes 32800 | tf_op jit(solution)/shard_map/ppermute | solution.py:643
  47.6 0.3 shard_map.159
  47.8 1.5 %collective-permute-start.10 = (bf16[64,128]{1,0:T(8,128)(2,1)S(1)}, bf16[64,128]{1,0:T(8,128)(2,1)S(1)}, u32[]{:S(2)}, u32[]{:S(2)}) collective-permute-start(bf16[64,128]{1,0:T(8,128)(2,1)S(1)} %get-tuple-element.36), channel_id=1, source_target_pairs={{0,2},{1,3},{2,0},{3,1},{4,6},{5,7},{6,4},{7,5},{8,10},{9,11},{10,... | collective-permute-start | bytes 49160 | tf_op jit(solution)/shard_map/ppermute | solution.py:645
  49.4 2.3 %collective-permute-done.10.refs_1_ = bf16[64,128]{1,0:T(8,128)(2,1)S(1)} collective-permute-done((bf16[64,128]{1,0:T(8,128)(2,1)S(1)}, bf16[64,128]{1,0:T(8,128)(2,1)S(1)}, u32[]{:S(2)}, u32[]{:S(2)}) %collective-permute-start.10) | collective-permute-done | bytes 16416 | tf_op jit(solution)/shard_map/ppermute | solution.py:645
  51.7 1.4 %shard_map.160 = bf16[4,384]{1,0:T(4,128)(2,1)} custom-call(bf16[64,128]{1,0:T(8,128)(2,1)S(1)} %get-tuple-element.35.refs_0_, bf16[64,128]{1,0:T(8,128)(2,1)S(1)} %collective-permute-done.10.refs_1_, f32[8,128]{1,0:T(8,128)S(1)} %get-tuple-element.32.refs_4_.refs_2_, f32[1,384]{1,0:T(1,128)S(1)} %get-tuple-element.37.refs_3_, ...), custom_call_target="tpu_custom_call" | custom-call | tf_op jit(solution)/shard_map/pallas_call | solution.py:576
  (1 shorter events, 0.0 us)
Async XLA Ops:
  0.0 7.2 %collective-permute-start.4 = (bf16[4,384]{1,0:T(4,128)(2,1)}, bf16[4,384]{1,0:T(4,128)(2,1)S(1)}, u32[]{:S(2)}, u32[]{:S(2)}) collective-permute-start(bf16[4,384]{1,0:T(4,128)(2,1)} %param.16), channel_id=1, source_target_pairs={{0,1},{1,0},{2,3},{3,2},{4,5},{5,4},{6,7},{7,6},{8,9},{9,8},{10,11... | collective-permute-start | bytes 9224 | tf_op jit(solution)/shard_map/ppermute | solution.py:614
  0.0 14.5 %collective-permute-start = (bf16[48,256]{1,0:T(8,128)(2,1)}, bf16[48,256]{1,0:T(8,128)(2,1)S(1)}, u32[]{:S(2)}, u32[]{:S(2)}) collective-permute-start(bf16[48,256]{1,0:T(8,128)(2,1)} %bitcast.19), channel_id=1, source_target_pairs={{0,32},{32,0},{64,96},{96,64},{128,160},{160,128},{192,224},{224,1... | collective-permute-start | bytes 73736 | tf_op jit(solution)/shard_map/ppermute | solution.py:609
  8.6 14.8 %all-to-all-start = ((bf16[16,8,384]{2,1,0:T(8,128)(2,1)}), bf16[16,8,384]{2,1,0:T(8,128)(2,1)S(1)}, u32[]{:S(2)}, u32[]{:S(2)}) async-start(bf16[16,8,384]{2,1,0:T(8,128)(2,1)} %broadcast_in_dim.2), calls=%async_computation | async-start | bytes 196608 | tf_op jit(solution)/shard_map/all_to_all | solution.py:619
  15.3 8.0 %collective-permute-start.1 = (bf16[2,48,256]{2,1,0:T(8,128)(2,1)S(1)}, bf16[2,48,256]{2,1,0:T(8,128)(2,1)S(1)}, u32[]{:S(2)}, u32[]{:S(2)}) collective-permute-start(bf16[2,48,256]{2,1,0:T(8,128)(2,1)S(1)} %pad_maximum_fusion.both_ref), channel_id=1, source_target_pairs={{64,0},{96,32},{128,64},{160,96},{192,128},{224,160},{0,192},{32,2... | collective-permute-start | bytes 147464 | tf_op jit(solution)/shard_map/ppermute | solution.py:611
  15.8 7.5 %collective-permute-start.2 = (bf16[2,48,256]{2,1,0:T(8,128)(2,1)S(1)}, bf16[2,48,256]{2,1,0:T(8,128)(2,1)S(1)}, u32[]{:S(2)}, u32[]{:S(2)}) collective-permute-start(bf16[2,48,256]{2,1,0:T(8,128)(2,1)S(1)} %pad_maximum_fusion.both_ref), channel_id=1, source_target_pairs={{128,0},{160,32},{192,64},{224,96},{0,128},{32,160},{64,192},{96,2... | collective-permute-start | bytes 147464 | tf_op jit(solution)/shard_map/ppermute | solution.py:611
  18.2 5.1 %collective-permute-start.3 = (bf16[2,48,256]{2,1,0:T(8,128)(2,1)S(1)}, bf16[2,48,256]{2,1,0:T(8,128)(2,1)S(1)}, u32[]{:S(2)}, u32[]{:S(2)}) collective-permute-start(bf16[2,48,256]{2,1,0:T(8,128)(2,1)S(1)} %pad_maximum_fusion.both_ref), channel_id=1, source_target_pairs={{192,0},{224,32},{0,64},{32,96},{64,128},{96,160},{128,192},{160,2... | collective-permute-start | bytes 147464 | tf_op jit(solution)/shard_map/ppermute | solution.py:611
  23.3 16.1 %copy-start = (f32[384]{0:T(512)S(1)}, f32[384]{0:T(512)}, u32[]{:S(2)}) copy-start(f32[384]{0:T(512)} %param.30) | copy-start | bytes 4612
  31.2 1.6 %collective-permute-start.5 = (bf16[1024,128]{1,0:T(8,128)(2,1)S(1)}, bf16[1024,128]{1,0:T(8,128)(2,1)S(1)}, u32[]{:S(2)}, u32[]{:S(2)}) collective-permute-start(bf16[1024,128]{1,0:T(8,128)(2,1)S(1)} %get-tuple-element.27), channel_id=1, source_target_pairs={{0,1},{1,0},{2,3},{3,2},{4,5},{5,4},{6,7},{7,6},{8,9},{9,8},{10,11... | collective-permute-start | bytes 786440 | tf_op jit(solution)/shard_map/ppermute | solution.py:638
  33.3 8.2 %collective-permute-start.6 = (bf16[256,128]{1,0:T(8,128)(2,1)S(1)}, bf16[256,128]{1,0:T(8,128)(2,1)S(1)}, u32[]{:S(2)}, u32[]{:S(2)}) collective-permute-start(bf16[256,128]{1,0:T(8,128)(2,1)S(1)} %get-tuple-element.29), channel_id=1, source_target_pairs={{0,8},{1,9},{2,10},{3,11},{4,12},{5,13},{6,14},{7,15},{8,16},{9,17... | collective-permute-start | bytes 196616 | tf_op jit(solution)/shard_map/ppermute | solution.py:489
  35.3 6.2 %collective-permute-start.7 = (bf16[256,128]{1,0:T(8,128)(2,1)S(1)}, bf16[256,128]{1,0:T(8,128)(2,1)S(1)}, u32[]{:S(2)}, u32[]{:S(2)}) collective-permute-start(bf16[256,128]{1,0:T(8,128)(2,1)S(1)} %get-tuple-element.30), channel_id=1, source_target_pairs={{0,16},{1,17},{2,18},{3,19},{4,20},{5,21},{6,22},{7,23},{8,24},{9,... | collective-permute-start | bytes 196616 | tf_op jit(solution)/shard_map/ppermute | solution.py:489
  37.9 4.3 %collective-permute-start.8 = (bf16[256,128]{1,0:T(8,128)(2,1)S(1)}, bf16[256,128]{1,0:T(8,128)(2,1)S(1)}, u32[]{:S(2)}, u32[]{:S(2)}) collective-permute-start(bf16[256,128]{1,0:T(8,128)(2,1)S(1)} %get-tuple-element.31), channel_id=1, source_target_pairs={{0,24},{1,25},{2,26},{3,27},{4,28},{5,29},{6,30},{7,31},{8,0},{9,1... | collective-permute-start | bytes 196616 | tf_op jit(solution)/shard_map/ppermute | solution.py:489
  42.7 4.9 %collective-permute-start.9 = (bf16[128,128]{1,0:T(8,128)(2,1)S(1)}, bf16[128,128]{1,0:T(8,128)(2,1)S(1)}, u32[]{:S(2)}, u32[]{:S(2)}) collective-permute-start(bf16[128,128]{1,0:T(8,128)(2,1)S(1)} %get-tuple-element.34), channel_id=1, source_target_pairs={{0,4},{1,5},{2,6},{3,7},{4,0},{5,1},{6,2},{7,3},{8,12},{9,13},{10,... | collective-permute-start | bytes 98312 | tf_op jit(solution)/shard_map/ppermute | solution.py:643
  47.8 3.8 %collective-permute-start.10 = (bf16[64,128]{1,0:T(8,128)(2,1)S(1)}, bf16[64,128]{1,0:T(8,128)(2,1)S(1)}, u32[]{:S(2)}, u32[]{:S(2)}) collective-permute-start(bf16[64,128]{1,0:T(8,128)(2,1)S(1)} %get-tuple-element.36), channel_id=1, source_target_pairs={{0,2},{1,3},{2,0},{3,1},{4,6},{5,7},{6,4},{7,5},{8,10},{9,11},{10,... | collective-permute-start | bytes 49160 | tf_op jit(solution)/shard_map/ppermute | solution.py:645

commit v7 on v6

--- a/solution.py
+++ b/solution.py
@@ -98,7 +98,7 @@
 
 def shadow_kernel(
     raw_hbm, cb_hbm, dm_hbm, kf_hbm, kc_hbm, km_hbm, qf_hbm, qc_hbm, pw_hbm, wk_hbm, wq_hbm,
-    pair_ref, mask_ref, wk_ref, wq_ref, bias_ref,
+    pair_ref, mask_ref, wk_ref, wq_ref, bias_ref, kept_ref,
     raw_v, cb_v, dm_v, kf_v, kc_v, km_v, qf_v, qc_v, pw_v, pw_s, pair_v, sem, pair_sem,
 ):
     moves = [
@@ -110,9 +110,10 @@
     core = lax.rem(lax.axis_index("col"), 2)
     groups = SB // SHARE
     steps = pair_ref.shape[0] // groups
+    blocks = [kept_ref] + [pair_v.at[i] for i in range(steps - 1)]
     copies = [
         pltpu.make_async_copy(
-            pair_ref.at[pl.ds(groups * step, groups), 1 - core], pair_v.at[step], pair_sem.at[step]
+            pair_ref.at[pl.ds(groups * step, groups), 1 - core], blocks[step], pair_sem.at[step]
         )
         for step in range(steps)
     ]
@@ -132,7 +133,7 @@
             row = (SB * i + q) * HP
             bias_ref[row : row + HP] = lax.dot_general(
                 weight,
-                pair_v[i, q // SHARE, q % SHARE],
+                blocks[i][q // SHARE, q % SHARE],
                 NT,
                 preferred_element_type=F32,
             )
@@ -210,7 +211,7 @@
 
 
 def attend_kernel(
-    both_ref, next_ref, over_ref, last_ref, qs_ref, wk_ref, mask_ref, wq_ref, bias_ref, pair_ref,
+    both_ref, next_ref, over_ref, last_ref, qs_ref, wk_ref, mask_ref, wq_ref, bias_ref, kept_ref, pair_ref,
     send_ref, own_ref, kpt_s, nk_s, kt_s, vt_s, v_s, w_s, z_s, o_s, ks_s,
     qpt_s, nq_s, qft_s, qf_s, feat_s, pair_v, pair_sem,
 ):
@@ -221,9 +222,12 @@
     order = [*range(steps, 2 * steps), *range(steps)]
     for index in order:
         half, step = divmod(index, steps)
+        skip = kept_ref.shape[0] if index == 0 else 0
         copies[index] = pltpu.make_async_copy(
-            pair_ref.at[pl.ds(groups * step, groups), 1 - core if half == 0 else core],
-            pair_v.at[index],
+            pair_ref.at[
+                pl.ds(groups * step + skip, groups - skip), 1 - core if half == 0 else core
+            ],
+            pair_v.at[index, pl.ds(skip, groups - skip)],
             pair_sem.at[index],
         )
         copies[index].start()
@@ -314,7 +318,7 @@
                 row = start + HP * i
                 o_s[row : row + HP] = jnp.dot(
                     w_s[row : row + HP, :],
-                    block[i // SHARE, i % SHARE],
+                    (kept_ref if index == 0 and i < SB else block)[i // SHARE, i % SHARE],
                     preferred_element_type=F32,
                 )
             for r in range(4):
@@ -416,13 +420,14 @@
             pltpu.VMEM(others[9].shape, BF16),
             pltpu.VMEM(others[10].shape, BF16),
             pltpu.VMEM((queries * HP // 2, keys), F32),
+            pltpu.VMEM((SB // SHARE, SHARE, keys, CZ), BF16),
         ),
         in_specs=[HBM] * 12,
-        out_specs=(VMEM,) * 4,
+        out_specs=(VMEM,) * 5,
         scratch_shapes=[pltpu.VMEM(x.shape, x.dtype) for x in others[:9]]
         + [
             pltpu.VMEM((HP, CZ), F32),
-            pltpu.VMEM((queries // SB // 2, SB // SHARE, SHARE, keys, CZ), BF16),
+            pltpu.VMEM((queries // SB // 2 - 1, SB // SHARE, SHARE, keys, CZ), BF16),
             pltpu.SemaphoreType.DMA((11,)),
             pltpu.SemaphoreType.DMA((queries // SB // 2,)),
         ],
@@ -625,7 +630,7 @@
         tiled=True,
     ).reshape(-1, chip.shape[1])
     heads = (lane_heads()[1][None, :] == np.arange(HP)[:, None]).astype(np.float32)
-    mask, wk, wq, bias = shadow(
+    mask, wk, wq, *held = shadow(
         [
             point_raw.reshape(1, -1), chain_bias.reshape(1, -1),
             jnp.asarray(np.concatenate([depth_mask(), heads], 1)),
@@ -634,7 +639,7 @@
         ],
         pair,
     )
-    send, own = attend([both, *rest, queries], [wk, mask, wq, bias], pair)
+    send, own = attend([both, *rest, queries], [wk, mask, wq, *held], pair)
     come = lax.ppermute(send, "col", [(i, i ^ 1) for i in range(cols)])
     sums = join([own, come], lambda col: lax.div(col, 8), 4)
     sums = exchange(sums, 4, 8, cols)

time: 53.8 us -> 53.8 us (level)
  no operation moved by 1% of the time
where the time goes in v7:
time: 53.8 us; the launch traced here: 53.1 us
  starting transfers between devices  28.1 us (52%)
  Pallas kernels  15.1 us (28%)
  waiting for transfers between devices  7 us (13%)
  other arithmetic  1.45 us (3%)
  local copies, waits for them, and re-layouts  1.22 us (2%)
    pallas_call x1, Pallas kernels, attend(): pl.pallas_call(attend_kernel, out_shape=(jax.ShapeDtypeStruct((queries *...  7.84 us
    ppermute x1, starting transfers between devices, body(): lax.ppermute(turned, 'row', [(i, i ^ 1) for i in range(rows)])  7.19 us
    ppermute x3, starting transfers between devices, exchange(): lax.ppermute(parts[k], 'col', [(i, to(i, k)) for i in range(count)])  6.14 us
    all_to_all x1, starting transfers between devices, body(): lax.all_to_all(jnp.broadcast_to(chip[None], (cols // 2, *chip.shape)), 'c...  5.94 us
    ppermute x3, starting transfers between devices, body(): lax.ppermute(both, 'row', [((i + 2 * k) % rows, i) for i in range(rows)])  4.76 us
    pallas_call x1, Pallas kernels, shadow(): pl.pallas_call(shadow_kernel, out_shape=(pltpu.VMEM((HP, KD + GL + keys +...  3.25 us
    ppermute x1, waiting for transfers between devices, body(): come = lax.ppermute(send, 'col', [(i, i ^ 4) for i in range(cols)])  2.45 us
    ppermute x1, starting transfers between devices, body(): come = lax.ppermute(send, 'col', [(i, i ^ 4) for i in range(cols)])  2.45 us
  transfers between devices with their start and end apart: 12, of which 4 were waited for; matrix products, arithmetic and copies ran while one was open for 5% of the time, Pallas kernels for 9%

profile of v7, /device:TPU:2, one launch (start us, length us, event | category | flops | bytes accessed | tf_op | source)
XLA Modules:
  0.0 53.1 jit_solution(7619695978422067131)
XLA Ops:
  0.0 0.0 collective-permute-start.4
  0.0 7.2 %collective-permute-start = (bf16[48,256]{1,0:T(8,128)(2,1)}, bf16[48,256]{1,0:T(8,128)(2,1)S(1)}, u32[]{:S(2)}, u32[]{:S(2)}) collective-permute-start(bf16[48,256]{1,0:T(8,128)(2,1)} %bitcast.19), channel_id=1, source_target_pairs={{0,32},{32,0},{64,96},{96,64},{128,160},{160,128},{192,224},{224,1... | collective-permute-start | bytes 73736 | tf_op jit(solution)/shard_map/ppermute | solution.py:614
  7.2 0.0 collective-permute-done.4
  7.2 0.7 %broadcast_select_fusion.1 = (bf16[4,384]{1,0:T(4,128)(2,1)S(1)}, bf16[4,384]{1,0:T(4,128)(2,1)S(1)}) fusion(bf16[4,384]{1,0:T(4,128)(2,1)} %param.16, bf16[4,384]{1,0:T(4,128)(2,1)S(1)} %collective-permute-done.4, pred[]{:T(512)S(6)} %eq.3), kind=kLoop, calls=%fused_computation.3 | loop fusion | flops 3072 | bytes 12289 | tf_op jit(solution)/shard_map/jit(_where)/select_n | solution.py:622
  7.9 0.7 %broadcast_in_dim.2 = bf16[16,8,384]{2,1,0:T(8,128)(2,1)} broadcast(bf16[8,384]{1,0:T(8,128)(2,1)S(1)} %pad_maximum_fusion.1), dimensions={1,2} | broadcast | bytes 104448 | tf_op jit(solution)/shard_map/broadcast_in_dim | solution.py:625
  8.6 5.9 %all-to-all-start = ((bf16[16,8,384]{2,1,0:T(8,128)(2,1)}), bf16[16,8,384]{2,1,0:T(8,128)(2,1)S(1)}, u32[]{:S(2)}, u32[]{:S(2)}) async-start(bf16[16,8,384]{2,1,0:T(8,128)(2,1)} %broadcast_in_dim.2), calls=%async_computation | async-start | bytes 196608 | tf_op jit(solution)/shard_map/all_to_all | solution.py:624
  14.5 0.0 collective-permute-done
  14.5 0.7 %pad_maximum_fusion.both_ref = bf16[2,48,256]{2,1,0:T(8,128)(2,1)S(1)} fusion(bf16[1,48,256]{2,1,0:T(8,128)(2,1)S(1)} %bitcast.21, bf16[1,48,256]{2,1,0:T(8,128)(2,1)} %bitcast.20), kind=kLoop, calls=%fused_computation | loop fusion | flops 24576 | bytes 98304 | tf_op jit(solution)/shard_map/stack | solution.py:614
  15.3 0.5 %collective-permute-start.1 = (bf16[2,48,256]{2,1,0:T(8,128)(2,1)S(1)}, bf16[2,48,256]{2,1,0:T(8,128)(2,1)S(1)}, u32[]{:S(2)}, u32[]{:S(2)}) collective-permute-start(bf16[2,48,256]{2,1,0:T(8,128)(2,1)S(1)} %pad_maximum_fusion.both_ref), channel_id=1, source_target_pairs={{64,0},{96,32},{128,64},{160,96},{192,128},{224,160},{0,192},{32,2... | collective-permute-start | bytes 147464 | tf_op jit(solution)/shard_map/ppermute | solution.py:616
  15.8 2.4 %collective-permute-start.2 = (bf16[2,48,256]{2,1,0:T(8,128)(2,1)S(1)}, bf16[2,48,256]{2,1,0:T(8,128)(2,1)S(1)}, u32[]{:S(2)}, u32[]{:S(2)}) collective-permute-start(bf16[2,48,256]{2,1,0:T(8,128)(2,1)S(1)} %pad_maximum_fusion.both_ref), channel_id=1, source_target_pairs={{128,0},{160,32},{192,64},{224,96},{0,128},{32,160},{64,192},{96,2... | collective-permute-start | bytes 147464 | tf_op jit(solution)/shard_map/ppermute | solution.py:616
  18.2 1.8 %collective-permute-start.3 = (bf16[2,48,256]{2,1,0:T(8,128)(2,1)S(1)}, bf16[2,48,256]{2,1,0:T(8,128)(2,1)S(1)}, u32[]{:S(2)}, u32[]{:S(2)}) collective-permute-start(bf16[2,48,256]{2,1,0:T(8,128)(2,1)S(1)} %pad_maximum_fusion.both_ref), channel_id=1, source_target_pairs={{192,0},{224,32},{0,64},{32,96},{64,128},{96,160},{128,192},{160,2... | collective-permute-start | bytes 147464 | tf_op jit(solution)/shard_map/ppermute | solution.py:616
  20.0 3.3 %shard_map.154 = (f32[16,1920]{1,0:T(8,128)S(1)}, bf16[816,384]{1,0:T(8,128)(2,1)S(1)}, bf16[336,384]{1,0:T(8,128)(2,1)S(1)}, f32[1024,256]{1,0:T(8,128)S(1)}, bf16[4,4,256,128]{3,2,1,0:T(8,128)(2,1)S(1)}) custom-call(f32[1,12]{1,0:T(1,128)} %bitcast.25, f32[1,12]{1,0:T(1,128)} %bitcast.26, f32[16,1280]{1,0:T(8,128)} %constant.12.clone.dm_hbm, ...), custom_call_target="tpu_custom_call" | custom-call | flops 67108864 | bytes 4194304 | tf_op jit(solution)/shard_map/pallas_call | solution.py:416
  23.3 0.0 collective-permute-done.1.next_ref
  23.3 0.0 collective-permute-done.2.over_ref
  23.3 0.0 collective-permute-done.3.last_ref
  23.3 0.0 all-to-all-done
  23.3 0.0 copy-start
  23.3 7.8 %shard_map.155 = (bf16[1024,128]{1,0:T(8,128)(2,1)S(1)}, bf16[1024,128]{1,0:T(8,128)(2,1)S(1)}) custom-call(bf16[2,48,256]{2,1,0:T(8,128)(2,1)S(1)} %pad_maximum_fusion.both_ref, bf16[2,48,256]{2,1,0:T(8,128)(2,1)S(1)} %collective-permute-done.1.next_ref, bf16[2,48,256]{2,1,0:T(8,128)(2,1)S(1)} %collective-permute-done.2.over_ref, ...), custom_call_target="tpu_custom_call" | custom-call | flops 1476395008 | bytes 8388608 | tf_op jit(solution)/shard_map/pallas_call | solution.py:444
  31.2 0.1 collective-permute-start.5
  31.3 1.5 %collective-permute-done.5.refs_1_ = bf16[1024,128]{1,0:T(8,128)(2,1)S(1)} collective-permute-done((bf16[1024,128]{1,0:T(8,128)(2,1)S(1)}, bf16[1024,128]{1,0:T(8,128)(2,1)S(1)}, u32[]{:S(2)}, u32[]{:S(2)}) %collective-permute-start.5) | collective-permute-done | bytes 262176 | tf_op jit(solution)/shard_map/ppermute | solution.py:643
  32.8 0.5 shard_map.156
  33.3 2.0 %collective-permute-start.6 = (bf16[256,128]{1,0:T(8,128)(2,1)S(1)}, bf16[256,128]{1,0:T(8,128)(2,1)S(1)}, u32[]{:S(2)}, u32[]{:S(2)}) collective-permute-start(bf16[256,128]{1,0:T(8,128)(2,1)S(1)} %get-tuple-element.31), channel_id=1, source_target_pairs={{0,8},{1,9},{2,10},{3,11},{4,12},{5,13},{6,14},{7,15},{8,16},{9,17... | collective-permute-start | bytes 196616 | tf_op jit(solution)/shard_map/ppermute | solution.py:494
  35.3 2.7 %collective-permute-start.7 = (bf16[256,128]{1,0:T(8,128)(2,1)S(1)}, bf16[256,128]{1,0:T(8,128)(2,1)S(1)}, u32[]{:S(2)}, u32[]{:S(2)}) collective-permute-start(bf16[256,128]{1,0:T(8,128)(2,1)S(1)} %get-tuple-element.32), channel_id=1, source_target_pairs={{0,16},{1,17},{2,18},{3,19},{4,20},{5,21},{6,22},{7,23},{8,24},{9,... | collective-permute-start | bytes 196616 | tf_op jit(solution)/shard_map/ppermute | solution.py:494
  37.9 1.5 %collective-permute-start.8 = (bf16[256,128]{1,0:T(8,128)(2,1)S(1)}, bf16[256,128]{1,0:T(8,128)(2,1)S(1)}, u32[]{:S(2)}, u32[]{:S(2)}) collective-permute-start(bf16[256,128]{1,0:T(8,128)(2,1)S(1)} %get-tuple-element.33), channel_id=1, source_target_pairs={{0,24},{1,25},{2,26},{3,27},{4,28},{5,29},{6,30},{7,31},{8,0},{9,1... | collective-permute-start | bytes 196616 | tf_op jit(solution)/shard_map/ppermute | solution.py:494
  39.4 0.0 copy-done
  39.4 0.6 %reshape.33.ob_hbm = f32[1,384]{1,0:T(1,128)} reshape(f32[384]{0:T(512)S(1)} %copy-done) | data formatting | bytes 3072 | tf_op jit(solution)/shard_map/reshape | solution.py:563
  40.0 1.5 %shard_map.157 = (f32[8,128]{1,0:T(8,128)S(1)}, f32[1,384]{1,0:T(1,128)S(1)}, bf16[2112,384]{1,0:T(8,128)(2,1)S(1)}) custom-call(bf16[256,128]{1,0:T(8,128)(2,1)S(1)} %get-tuple-element.30.after.refs_0_, f32[12,128]{1,0:T(8,128)} %qf_hbm.3, f32[1,384]{1,0:T(1,128)} %reshape.33.ob_hbm, bf16[2112,384]{1,0:T(8,128)(2,1)} %ow_hbm.1), custom_call_target="tpu_custom_call" | custom-call | bytes 4194304 | tf_op jit(solution)/shard_map/pallas_call | solution.py:564
  41.5 0.0 collective-permute-done.6.refs_1_
  41.5 0.0 collective-permute-done.7.refs_2_
  41.5 0.7 %collective-permute-done.8.refs_3_ = bf16[256,128]{1,0:T(8,128)(2,1)S(1)} collective-permute-done((bf16[256,128]{1,0:T(8,128)(2,1)S(1)}, bf16[256,128]{1,0:T(8,128)(2,1)S(1)}, u32[]{:S(2)}, u32[]{:S(2)}) %collective-permute-start.8) | collective-permute-done | bytes 65568 | tf_op jit(solution)/shard_map/ppermute | solution.py:494
  42.2 0.4 shard_map.158
  42.7 2.4 %collective-permute-start.9 = (bf16[128,128]{1,0:T(8,128)(2,1)S(1)}, bf16[128,128]{1,0:T(8,128)(2,1)S(1)}, u32[]{:S(2)}, u32[]{:S(2)}) collective-permute-start(bf16[128,128]{1,0:T(8,128)(2,1)S(1)} %get-tuple-element.36), channel_id=1, source_target_pairs={{0,4},{1,5},{2,6},{3,7},{4,0},{5,1},{6,2},{7,3},{8,12},{9,13},{10,... | collective-permute-start | bytes 98312 | tf_op jit(solution)/shard_map/ppermute | solution.py:648
  45.1 2.5 %collective-permute-done.9.refs_1_ = bf16[128,128]{1,0:T(8,128)(2,1)S(1)} collective-permute-done((bf16[128,128]{1,0:T(8,128)(2,1)S(1)}, bf16[128,128]{1,0:T(8,128)(2,1)S(1)}, u32[]{:S(2)}, u32[]{:S(2)}) %collective-permute-start.9) | collective-permute-done | bytes 32800 | tf_op jit(solution)/shard_map/ppermute | solution.py:648
  47.6 0.3 shard_map.159
  47.8 1.5 %collective-permute-start.10 = (bf16[64,128]{1,0:T(8,128)(2,1)S(1)}, bf16[64,128]{1,0:T(8,128)(2,1)S(1)}, u32[]{:S(2)}, u32[]{:S(2)}) collective-permute-start(bf16[64,128]{1,0:T(8,128)(2,1)S(1)} %get-tuple-element.38), channel_id=1, source_target_pairs={{0,2},{1,3},{2,0},{3,1},{4,6},{5,7},{6,4},{7,5},{8,10},{9,11},{10,... | collective-permute-start | bytes 49160 | tf_op jit(solution)/shard_map/ppermute | solution.py:650
  49.4 2.3 %collective-permute-done.10.refs_1_ = bf16[64,128]{1,0:T(8,128)(2,1)S(1)} collective-permute-done((bf16[64,128]{1,0:T(8,128)(2,1)S(1)}, bf16[64,128]{1,0:T(8,128)(2,1)S(1)}, u32[]{:S(2)}, u32[]{:S(2)}) %collective-permute-start.10) | collective-permute-done | bytes 16416 | tf_op jit(solution)/shard_map/ppermute | solution.py:650
  51.7 1.4 %shard_map.160 = bf16[4,384]{1,0:T(4,128)(2,1)} custom-call(bf16[64,128]{1,0:T(8,128)(2,1)S(1)} %get-tuple-element.37.refs_0_, bf16[64,128]{1,0:T(8,128)(2,1)S(1)} %collective-permute-done.10.refs_1_, f32[8,128]{1,0:T(8,128)S(1)} %get-tuple-element.34.refs_4_.refs_2_, f32[1,384]{1,0:T(1,128)S(1)} %get-tuple-element.39.refs_3_, ...), custom_call_target="tpu_custom_call" | custom-call | tf_op jit(solution)/shard_map/pallas_call | solution.py:581
  (1 shorter events, 0.0 us)
Async XLA Ops:
  0.0 7.2 %collective-permute-start.4 = (bf16[4,384]{1,0:T(4,128)(2,1)}, bf16[4,384]{1,0:T(4,128)(2,1)S(1)}, u32[]{:S(2)}, u32[]{:S(2)}) collective-permute-start(bf16[4,384]{1,0:T(4,128)(2,1)} %param.16), channel_id=1, source_target_pairs={{0,1},{1,0},{2,3},{3,2},{4,5},{5,4},{6,7},{7,6},{8,9},{9,8},{10,11... | collective-permute-start | bytes 9224 | tf_op jit(solution)/shard_map/ppermute | solution.py:619
  0.0 14.5 %collective-permute-start = (bf16[48,256]{1,0:T(8,128)(2,1)}, bf16[48,256]{1,0:T(8,128)(2,1)S(1)}, u32[]{:S(2)}, u32[]{:S(2)}) collective-permute-start(bf16[48,256]{1,0:T(8,128)(2,1)} %bitcast.19), channel_id=1, source_target_pairs={{0,32},{32,0},{64,96},{96,64},{128,160},{160,128},{192,224},{224,1... | collective-permute-start | bytes 73736 | tf_op jit(solution)/shard_map/ppermute | solution.py:614
  8.6 14.8 %all-to-all-start = ((bf16[16,8,384]{2,1,0:T(8,128)(2,1)}), bf16[16,8,384]{2,1,0:T(8,128)(2,1)S(1)}, u32[]{:S(2)}, u32[]{:S(2)}) async-start(bf16[16,8,384]{2,1,0:T(8,128)(2,1)} %broadcast_in_dim.2), calls=%async_computation | async-start | bytes 196608 | tf_op jit(solution)/shard_map/all_to_all | solution.py:624
  15.3 8.0 %collective-permute-start.1 = (bf16[2,48,256]{2,1,0:T(8,128)(2,1)S(1)}, bf16[2,48,256]{2,1,0:T(8,128)(2,1)S(1)}, u32[]{:S(2)}, u32[]{:S(2)}) collective-permute-start(bf16[2,48,256]{2,1,0:T(8,128)(2,1)S(1)} %pad_maximum_fusion.both_ref), channel_id=1, source_target_pairs={{64,0},{96,32},{128,64},{160,96},{192,128},{224,160},{0,192},{32,2... | collective-permute-start | bytes 147464 | tf_op jit(solution)/shard_map/ppermute | solution.py:616
  15.8 7.5 %collective-permute-start.2 = (bf16[2,48,256]{2,1,0:T(8,128)(2,1)S(1)}, bf16[2,48,256]{2,1,0:T(8,128)(2,1)S(1)}, u32[]{:S(2)}, u32[]{:S(2)}) collective-permute-start(bf16[2,48,256]{2,1,0:T(8,128)(2,1)S(1)} %pad_maximum_fusion.both_ref), channel_id=1, source_target_pairs={{128,0},{160,32},{192,64},{224,96},{0,128},{32,160},{64,192},{96,2... | collective-permute-start | bytes 147464 | tf_op jit(solution)/shard_map/ppermute | solution.py:616
  18.2 5.1 %collective-permute-start.3 = (bf16[2,48,256]{2,1,0:T(8,128)(2,1)S(1)}, bf16[2,48,256]{2,1,0:T(8,128)(2,1)S(1)}, u32[]{:S(2)}, u32[]{:S(2)}) collective-permute-start(bf16[2,48,256]{2,1,0:T(8,128)(2,1)S(1)} %pad_maximum_fusion.both_ref), channel_id=1, source_target_pairs={{192,0},{224,32},{0,64},{32,96},{64,128},{96,160},{128,192},{160,2... | collective-permute-start | bytes 147464 | tf_op jit(solution)/shard_map/ppermute | solution.py:616
  23.3 16.1 %copy-start = (f32[384]{0:T(512)S(1)}, f32[384]{0:T(512)}, u32[]{:S(2)}) copy-start(f32[384]{0:T(512)} %param.30) | copy-start | bytes 4612
  31.2 1.6 %collective-permute-start.5 = (bf16[1024,128]{1,0:T(8,128)(2,1)S(1)}, bf16[1024,128]{1,0:T(8,128)(2,1)S(1)}, u32[]{:S(2)}, u32[]{:S(2)}) collective-permute-start(bf16[1024,128]{1,0:T(8,128)(2,1)S(1)} %get-tuple-element.29), channel_id=1, source_target_pairs={{0,1},{1,0},{2,3},{3,2},{4,5},{5,4},{6,7},{7,6},{8,9},{9,8},{10,11... | collective-permute-start | bytes 786440 | tf_op jit(solution)/shard_map/ppermute | solution.py:643
  33.3 8.2 %collective-permute-start.6 = (bf16[256,128]{1,0:T(8,128)(2,1)S(1)}, bf16[256,128]{1,0:T(8,128)(2,1)S(1)}, u32[]{:S(2)}, u32[]{:S(2)}) collective-permute-start(bf16[256,128]{1,0:T(8,128)(2,1)S(1)} %get-tuple-element.31), channel_id=1, source_target_pairs={{0,8},{1,9},{2,10},{3,11},{4,12},{5,13},{6,14},{7,15},{8,16},{9,17... | collective-permute-start | bytes 196616 | tf_op jit(solution)/shard_map/ppermute | solution.py:494
  35.3 6.2 %collective-permute-start.7 = (bf16[256,128]{1,0:T(8,128)(2,1)S(1)}, bf16[256,128]{1,0:T(8,128)(2,1)S(1)}, u32[]{:S(2)}, u32[]{:S(2)}) collective-permute-start(bf16[256,128]{1,0:T(8,128)(2,1)S(1)} %get-tuple-element.32), channel_id=1, source_target_pairs={{0,16},{1,17},{2,18},{3,19},{4,20},{5,21},{6,22},{7,23},{8,24},{9,... | collective-permute-start | bytes 196616 | tf_op jit(solution)/shard_map/ppermute | solution.py:494
  37.9 4.3 %collective-permute-start.8 = (bf16[256,128]{1,0:T(8,128)(2,1)S(1)}, bf16[256,128]{1,0:T(8,128)(2,1)S(1)}, u32[]{:S(2)}, u32[]{:S(2)}) collective-permute-start(bf16[256,128]{1,0:T(8,128)(2,1)S(1)} %get-tuple-element.33), channel_id=1, source_target_pairs={{0,24},{1,25},{2,26},{3,27},{4,28},{5,29},{6,30},{7,31},{8,0},{9,1... | collective-permute-start | bytes 196616 | tf_op jit(solution)/shard_map/ppermute | solution.py:494
  42.7 4.9 %collective-permute-start.9 = (bf16[128,128]{1,0:T(8,128)(2,1)S(1)}, bf16[128,128]{1,0:T(8,128)(2,1)S(1)}, u32[]{:S(2)}, u32[]{:S(2)}) collective-permute-start(bf16[128,128]{1,0:T(8,128)(2,1)S(1)} %get-tuple-element.36), channel_id=1, source_target_pairs={{0,4},{1,5},{2,6},{3,7},{4,0},{5,1},{6,2},{7,3},{8,12},{9,13},{10,... | collective-permute-start | bytes 98312 | tf_op jit(solution)/shard_map/ppermute | solution.py:648
  47.8 3.8 %collective-permute-start.10 = (bf16[64,128]{1,0:T(8,128)(2,1)S(1)}, bf16[64,128]{1,0:T(8,128)(2,1)S(1)}, u32[]{:S(2)}, u32[]{:S(2)}) collective-permute-start(bf16[64,128]{1,0:T(8,128)(2,1)S(1)} %get-tuple-element.38), channel_id=1, source_target_pairs={{0,2},{1,3},{2,0},{3,1},{4,6},{5,7},{6,4},{7,5},{8,10},{9,11},{10,... | collective-permute-start | bytes 49160 | tf_op jit(solution)/shard_map/ppermute | solution.py:650
